TPU v7x, 32 devices: a whole 2x2x4 slice. The times are simulated.
32 devices in a mesh: section: 2 (over x), tensor: 2 (over y), wide: 8 (over z, core).
Axes of the slice: x: 2, y: 2, z: 4, core: 2. Of those that a mesh axis runs over, the one named last changes fastest.
Arguments:
- block_input: bfloat16 [4, 2048, 1024], P(None, ('wide', 'tensor')), may hold values from -6 to 6
- doc_lengths: int32 [4, 8], replicated, may hold values from 1 to 1536, 2048 in all within a row
- norm_gain: float32 [2, 2, 1024], P('section'), may hold values from 0.5 to 1.5
- norm_bias: float32 [2, 2, 1024], P('section'), may hold values from -1.8 to 1.8
- qkv_weight: bfloat16 [2, 1024, 3072], P('section', None, 'tensor'), may hold values from -0.1875 to 0.1875
- qkv_bias: float32 [2, 3072], P('section', 'tensor'), may hold values from -1.8 to 1.8
- dense_weight: bfloat16 [2, 1024, 1024], P('section', 'tensor'), may hold values from -0.75 to 0.75
- dense_bias: float32 [2, 1024], P('section'), may hold values from -1.8 to 1.8
- up_weight: bfloat16 [2, 1024, 4096], P('section', None, 'tensor'), may hold values from -0.1875 to 0.1875
- up_bias: float32 [2, 4096], P('section', 'tensor'), may hold values from -3 to 3
- down_weight: bfloat16 [2, 4096, 1024], P('section', 'tensor'), may hold values from -0.09375 to 0.09375
- down_bias: float32 [2, 1024], P('section'), may hold values from -1.8 to 1.8
- cotangent: float32 [4, 2048, 1024], P(None, ('wide', 'tensor')), may hold values from -9 to 9
Outputs:
- layer_out: bfloat16 [2, 4, 2048, 1024], P('section', None, ('wide', 'tensor'))
- input_grad: float32 [2, 4, 2048, 1024], P('section', None, ('wide', 'tensor'))
- norm_gain_grad: float32 [2, 2, 1024], P('section')
- norm_bias_grad: float32 [2, 2, 1024], P('section')
- qkv_weight_grad: float32 [2, 1024, 3072], P('section', None, 'tensor')
- qkv_bias_grad: float32 [2, 3072], P('section', 'tensor')
- dense_weight_grad: float32 [2, 1024, 1024], P('section', 'tensor')
- dense_bias_grad: float32 [2, 1024], P('section')
- up_weight_grad: float32 [2, 1024, 4096], P('section', None, 'tensor')
- up_bias_grad: float32 [2, 4096], P('section', 'tensor')
- down_weight_grad: float32 [2, 4096, 1024], P('section', 'tensor')
- down_bias_grad: float32 [2, 1024], P('section')
Inputs may be any that keep to these rules, and one draw needn't show every extreme that they name: `doc_lengths`: row s holds, in order, the lengths of the 8 documents packed in sequence s; each row sums to 2048, and in each row one document has exactly 1536 tokens.
All inputs are finite; a program needn't handle non-finite values.
Results may differ from a plain program's by a relative error of at most 0.018.
Values may be sent and summed in bfloat16 or wider, within the bound.
A program may use at most 192 MiB of HBM per device.

v0:
```python
import math

import jax
import jax.numpy as jnp
from jax import lax
from jax.sharding import PartitionSpec as P

HEAD_DIM = 64
ROT = 16
SEQ = 2048


EPSILON = 1e-05
ROPE_BASE = 10000.0


def shortened(shard):

    def short(part):
        return part.astype(jnp.bfloat16) if part.dtype == jnp.float32 else part

    return jax.tree.map(short, shard)


def from_behind(block, axis, distance):
    devices = range(lax.axis_size(axis))
    route = [(i - distance, i) for i in devices if i - distance in devices]
    return lax.ppermute(block, axis, route)


def norm_parts(values, gain, shift):
    center = jnp.mean(values, axis=-1, keepdims=True)
    centred = values - center
    spread = jnp.mean(centred * centred, axis=-1, keepdims=True)
    inv_scale = lax.rsqrt(spread + EPSILON)
    normed = centred * inv_scale
    return (normed * gain + shift, normed, inv_scale)


def norm_back(grad, normed, inv_scale, gain):
    scaled = grad * gain
    inner_mean = jnp.mean(scaled, axis=-1, keepdims=True)
    cross_mean = jnp.mean(scaled * normed, axis=-1, keepdims=True)
    return inv_scale * (scaled - inner_mean - normed * cross_mean)


def doc_layout(lengths, tok_index):
    ends = jnp.cumsum(lengths)
    starts = ends - lengths
    doc_ids = jnp.sum((tok_index[:, None] >= ends[None, :]).astype(jnp.int32), axis=1)
    numbers = jnp.arange(lengths.shape[0], dtype=jnp.int32)
    picked = doc_ids[:, None] == numbers[None, :]
    begins = jnp.sum(jnp.where(picked, starts[None, :], 0), axis=1)
    return (doc_ids, tok_index - begins)


def rope_tables(offsets):
    half = ROT // 2
    freqs = ROPE_BASE ** (-2.0 * jnp.arange(half, dtype=jnp.float32) / ROT)
    angle = offsets.astype(jnp.float32)[:, None] * freqs[None, :]
    return (jnp.cos(angle)[:, None, :], jnp.sin(angle)[:, None, :])


def rotate(values, cos_table, sin_table):
    half = ROT // 2
    front = values[..., :half]
    back = values[..., half:ROT]
    turned = [
        front * cos_table - back * sin_table,
        back * cos_table + front * sin_table,
        values[..., ROT:],
    ]
    return jnp.concatenate(turned, axis=-1)


def unrotate(values, cos_table, sin_table):
    half = ROT // 2
    front = values[..., :half]
    back = values[..., half:ROT]
    turned = [
        front * cos_table + back * sin_table,
        back * cos_table - front * sin_table,
        values[..., ROT:],
    ]
    return jnp.concatenate(turned, axis=-1)


def gelu_parts(pre_act):
    cumul = 0.5 * (1.0 + lax.erf(pre_act * (1.0 / math.sqrt(2.0))))
    density = jnp.exp(-0.5 * pre_act * pre_act) * (1.0 / math.sqrt(2.0 * math.pi))
    return (pre_act * cumul, cumul + pre_act * density)


def store_slot(buffer, update, slot_here, is_valid):
    previous = lax.dynamic_index_in_dim(buffer, slot_here, 0, keepdims=False)
    return lax.dynamic_update_index_in_dim(
        buffer, jnp.where(is_valid, update, previous), slot_here, 0
    )


def gather_keys(key_rows, value_rows):
    return (
        lax.all_gather(key_rows, "wide", axis=0, tiled=True),
        lax.all_gather(value_rows, "wide", axis=0, tiled=True),
    )


def forward_parts(inputs, lengths, weights, with_output):
    (
        norm_gain,
        norm_bias,
        qkv_weight,
        qkv_bias,
        dense_weight,
        dense_bias,
        up_weight,
        up_bias,
        down_weight,
        down_bias,
    ) = weights
    seq_len = SEQ
    group = inputs.shape[0] * lax.axis_size("tensor")
    head_count = qkv_weight.shape[1] // (3 * HEAD_DIM)
    factor = 1.0 / math.sqrt(HEAD_DIM)
    values = inputs.astype(jnp.float32)
    norm_first, normed_first, scale_first = norm_parts(values, norm_gain[0], norm_bias[0])
    norm_second, normed_second, scale_second = norm_parts(values, norm_gain[1], norm_bias[1])
    full_first, full_second = (
        lax.all_gather(norm_first.astype(jnp.bfloat16), "tensor", axis=0, tiled=True),
        lax.all_gather(norm_second.astype(jnp.bfloat16), "tensor", axis=0, tiled=True),
    )
    tok_index = lax.axis_index("wide") * group + jnp.arange(group, dtype=jnp.int32)
    doc_ids, offsets = doc_layout(lengths, tok_index)
    all_index = jnp.arange(seq_len, dtype=jnp.int32)
    all_docs = doc_layout(lengths, all_index)[0]
    cos_table, sin_table = rope_tables(offsets)
    packed = jnp.dot(full_first, qkv_weight, preferred_element_type=jnp.float32) + qkv_bias
    packed = packed.reshape(group, head_count, 3, HEAD_DIM)
    queries = rotate(packed[:, :, 0], cos_table, sin_table).astype(jnp.bfloat16)
    key_here = rotate(packed[:, :, 1], cos_table, sin_table).astype(jnp.bfloat16)
    value_here = packed[:, :, 2].astype(jnp.bfloat16)
    key_all, value_all = gather_keys(key_here.reshape(group, -1), value_here.reshape(group, -1))
    key_heads = key_all.reshape(seq_len, head_count, HEAD_DIM)
    value_heads = value_all.reshape(seq_len, head_count, HEAD_DIM)
    allowed = (doc_ids[:, None] == all_docs[None, :]) & (all_index[None, :] <= tok_index[:, None])
    raw_scores = jnp.einsum("qhd,khd->qhk", queries, key_heads, preferred_element_type=jnp.float32)
    scores = jnp.where(allowed[:, None, :], raw_scores * factor, -jnp.inf)
    row_max = jnp.max(scores, axis=-1, keepdims=True)
    log_total = row_max + jnp.log(jnp.sum(jnp.exp(scores - row_max), axis=-1, keepdims=True))
    attn_probs = jnp.exp(scores - log_total)
    probs_low = attn_probs.astype(jnp.bfloat16)
    mixed_out = jnp.einsum(
        "qhk,khd->qhd", probs_low, value_heads, preferred_element_type=jnp.float32
    )
    mixed_out = mixed_out.reshape(group, -1).astype(jnp.bfloat16)
    up_pre = jnp.dot(full_second, up_weight, preferred_element_type=jnp.float32) + up_bias
    up_act, gelu_slope = gelu_parts(up_pre)
    hidden = up_act.astype(jnp.bfloat16)
    output = None
    if with_output:
        partial_value = jnp.dot(mixed_out, dense_weight, preferred_element_type=jnp.float32)
        partial_value = partial_value + jnp.dot(
            hidden, down_weight, preferred_element_type=jnp.float32
        )
        branch = (
            lax.psum_scatter(
                partial_value.astype(jnp.bfloat16), "tensor", scatter_dimension=0, tiled=True
            ).astype(jnp.float32)
            + dense_bias
            + down_bias
        )
        output = (values + branch).astype(jnp.bfloat16)
    return dict(
        output=output,
        normed_first=normed_first,
        scale_first=scale_first,
        normed_second=normed_second,
        scale_second=scale_second,
        full_first=full_first,
        full_second=full_second,
        tok_index=tok_index,
        doc_ids=doc_ids,
        all_index=all_index,
        all_docs=all_docs,
        cos_table=cos_table,
        sin_table=sin_table,
        queries=queries,
        key_here=key_here,
        value_here=value_here,
        key_all=key_all,
        value_all=value_all,
        key_heads=key_heads,
        value_heads=value_heads,
        attn_probs=attn_probs,
        probs_low=probs_low,
        log_total=log_total,
        mixed_out=mixed_out,
        gelu_slope=gelu_slope,
        hidden=hidden,
    )


def backward_parts(inputs, grad_out, lengths, weights):
    (
        norm_gain,
        norm_bias,
        qkv_weight,
        qkv_bias,
        dense_weight,
        dense_bias,
        up_weight,
        up_bias,
        down_weight,
        down_bias,
    ) = weights
    parts = forward_parts(inputs, lengths, weights, False)
    seq_len = SEQ
    group = inputs.shape[0] * lax.axis_size("tensor")
    head_count = qkv_weight.shape[1] // (3 * HEAD_DIM)
    factor = 1.0 / math.sqrt(HEAD_DIM)
    cos_table = parts["cos_table"]
    sin_table = parts["sin_table"]
    grad_low = grad_out.astype(jnp.bfloat16)
    grad_rows = grad_low.astype(jnp.float32)
    grad_full = lax.all_gather(grad_low, "tensor", axis=0, tiled=True)
    dense_grad = jnp.einsum(
        "cf,cd->fd", parts["mixed_out"], grad_full, preferred_element_type=jnp.float32
    )
    down_grad = jnp.einsum(
        "cf,cd->fd", parts["hidden"], grad_full, preferred_element_type=jnp.float32
    )
    hidden_grad = jnp.einsum(
        "cd,fd->cf", grad_full, down_weight, preferred_element_type=jnp.float32
    )
    pre_grad = (hidden_grad * parts["gelu_slope"]).astype(jnp.bfloat16)
    up_grad = jnp.einsum(
        "cd,cf->df", parts["full_second"], pre_grad, preferred_element_type=jnp.float32
    )
    up_bias_grad = jnp.sum(pre_grad.astype(jnp.float32), axis=0)
    second_grad = jnp.einsum("cf,df->cd", pre_grad, up_weight, preferred_element_type=jnp.float32)
    mixed_grad = jnp.einsum(
        "cd,fd->cf", grad_full, dense_weight, preferred_element_type=jnp.float32
    )
    mixed_grad = mixed_grad.astype(jnp.bfloat16).reshape(group, head_count, HEAD_DIM)
    attn_probs = parts["attn_probs"]
    probs_grad = jnp.einsum(
        "qhd,khd->qhk", mixed_grad, parts["value_heads"], preferred_element_type=jnp.float32
    )
    inner = jnp.sum(attn_probs * probs_grad, axis=-1, keepdims=True)
    score_grad = (attn_probs * (probs_grad - inner) * factor).astype(jnp.bfloat16)
    query_grad = jnp.einsum(
        "qhk,khd->qhd", score_grad, parts["key_heads"], preferred_element_type=jnp.float32
    )
    key_sums = jnp.einsum(
        "qhk,qhd->khd", score_grad, parts["queries"], preferred_element_type=jnp.float32
    )
    value_sums = jnp.einsum(
        "qhk,qhd->khd", parts["probs_low"], mixed_grad, preferred_element_type=jnp.float32
    )
    key_flat, value_flat = (
        lax.psum_scatter(
            key_sums.reshape(seq_len, -1).astype(jnp.bfloat16),
            "wide",
            scatter_dimension=0,
            tiled=True,
        ).astype(jnp.float32),
        lax.psum_scatter(
            value_sums.reshape(seq_len, -1).astype(jnp.bfloat16),
            "wide",
            scatter_dimension=0,
            tiled=True,
        ).astype(jnp.float32),
    )
    key_grad = key_flat.reshape(group, head_count, HEAD_DIM)
    value_grad = value_flat.reshape(group, head_count, HEAD_DIM)
    query_back = unrotate(query_grad, cos_table, sin_table)
    key_back = unrotate(key_grad, cos_table, sin_table)
    packed_grad = (
        jnp.stack([query_back, key_back, value_grad], axis=2)
        .reshape(group, -1)
        .astype(jnp.bfloat16)
    )
    qkv_grad = jnp.einsum(
        "cd,cf->df", parts["full_first"], packed_grad, preferred_element_type=jnp.float32
    )
    qkv_bias_grad = jnp.sum(packed_grad.astype(jnp.float32), axis=0)
    first_grad = jnp.einsum(
        "cf,df->cd", packed_grad, qkv_weight, preferred_element_type=jnp.float32
    )
    norm_first_grad, norm_second_grad = (
        lax.psum_scatter(
            first_grad.astype(jnp.bfloat16), "tensor", scatter_dimension=0, tiled=True
        ).astype(jnp.float32),
        lax.psum_scatter(
            second_grad.astype(jnp.bfloat16), "tensor", scatter_dimension=0, tiled=True
        ).astype(jnp.float32),
    )
    gain_grad = jnp.stack(
        [
            jnp.sum(norm_first_grad * parts["normed_first"], axis=0),
            jnp.sum(norm_second_grad * parts["normed_second"], axis=0),
        ]
    )
    shift_grad = jnp.stack([jnp.sum(norm_first_grad, axis=0), jnp.sum(norm_second_grad, axis=0)])
    input_grad = grad_out + norm_back(
        norm_first_grad, parts["normed_first"], parts["scale_first"], norm_gain[0]
    )
    input_grad = input_grad + norm_back(
        norm_second_grad, parts["normed_second"], parts["scale_second"], norm_gain[1]
    )
    bias_rows = jnp.sum(grad_rows, axis=0)
    terms = (
        gain_grad,
        shift_grad,
        qkv_grad,
        qkv_bias_grad,
        dense_grad,
        bias_rows,
        up_grad,
        up_bias_grad,
        down_grad,
        bias_rows,
    )
    return (input_grad, terms)


def shards(
    block_input,
    doc_lengths,
    norm_gain,
    norm_bias,
    qkv_weight,
    qkv_bias,
    dense_weight,
    dense_bias,
    up_weight,
    up_bias,
    down_weight,
    down_bias,
    cotangent,
):
    weights = (
        norm_gain[0],
        norm_bias[0],
        qkv_weight[0],
        qkv_bias[0],
        dense_weight[0],
        dense_bias[0],
        up_weight[0],
        up_bias[0],
        down_weight[0],
        down_bias[0],
    )
    section_index = lax.axis_index("section")
    last_section = lax.axis_size("section") - 1
    micro_count = block_input.shape[0]
    row_count = block_input.shape[1]
    tick_count = micro_count + last_section

    def forward_tick(carry, tick_index):
        incoming, kept_inputs, outputs, kept_pairs = carry
        slot_raw = tick_index - section_index
        is_valid = (slot_raw >= 0) & (slot_raw < micro_count)
        slot_here = jnp.clip(slot_raw, 0, micro_count - 1)
        fresh = lax.dynamic_index_in_dim(
            block_input, jnp.clip(tick_index, 0, micro_count - 1), 0, keepdims=False
        )
        inputs = jnp.where(section_index == 0, fresh, incoming)
        lengths = lax.dynamic_index_in_dim(doc_lengths, slot_here, 0, keepdims=False)
        parts = forward_parts(inputs, lengths, weights, True)
        output = parts["output"]
        kept_inputs = store_slot(kept_inputs, inputs, slot_here, is_valid)
        outputs = store_slot(outputs, output, slot_here, is_valid)
        incoming = jax.tree.map(
            lambda part, own: part.astype(own.dtype),
            from_behind(shortened(output), "section", 1),
            output,
        )
        return ((incoming, kept_inputs, outputs, kept_pairs), None)

    pair_init = (jnp.zeros((1,), jnp.bfloat16), jnp.zeros((1,), jnp.bfloat16))
    zero_rows = jnp.zeros((row_count, block_input.shape[2]), jnp.bfloat16)
    zero_stack = jnp.zeros(block_input.shape, jnp.bfloat16)
    forward_init = (zero_rows, zero_stack, zero_stack, pair_init)
    forward_done = lax.scan(forward_tick, forward_init, jnp.arange(tick_count, dtype=jnp.int32))[0]
    kept_inputs = forward_done[1]
    outputs = forward_done[2]
    kept_pairs = forward_done[3]

    def add_masked(total, term, scale_mask):
        return total + scale_mask * term

    def backward_tick(carry, tick_index):
        incoming, grads, input_grads = carry
        slot_raw = tick_index - (last_section - section_index)
        is_valid = (slot_raw >= 0) & (slot_raw < micro_count)
        slot_here = jnp.clip(slot_raw, 0, micro_count - 1)
        top_grad = lax.dynamic_index_in_dim(cotangent, slot_here, 0, keepdims=False)
        grad_out = jnp.where(section_index == last_section, top_grad, incoming)
        inputs = lax.dynamic_index_in_dim(kept_inputs, slot_here, 0, keepdims=False)
        lengths = lax.dynamic_index_in_dim(doc_lengths, slot_here, 0, keepdims=False)
        input_grad, terms = backward_parts(inputs, grad_out, lengths, weights)
        scale_mask = is_valid.astype(jnp.float32)
        grads = tuple((add_masked(total, term, scale_mask) for total, term in zip(grads, terms)))
        input_grads = store_slot(input_grads, input_grad, slot_here, is_valid)
        incoming = from_behind(shortened(input_grad), "section", -1).astype(input_grad.dtype)
        return ((incoming, grads, input_grads), None)

    grad_init = tuple((jnp.zeros(weight.shape, jnp.float32) for weight in weights))
    backward_init = (
        jnp.zeros((row_count, block_input.shape[2]), jnp.float32),
        grad_init,
        jnp.zeros(block_input.shape, jnp.float32),
    )
    backward_done = lax.scan(backward_tick, backward_init, jnp.arange(tick_count, dtype=jnp.int32))[
        0
    ]
    grads = backward_done[1]
    input_grads = backward_done[2]
    wide_sums = (
        lax.psum(grads[2].astype(jnp.bfloat16), "wide").astype(jnp.float32),
        lax.psum(grads[3].astype(jnp.bfloat16), "wide").astype(jnp.float32),
        lax.psum(grads[4].astype(jnp.bfloat16), "wide").astype(jnp.float32),
        lax.psum(grads[6].astype(jnp.bfloat16), "wide").astype(jnp.float32),
        lax.psum(grads[7].astype(jnp.bfloat16), "wide").astype(jnp.float32),
        lax.psum(grads[8].astype(jnp.bfloat16), "wide").astype(jnp.float32),
    )
    shared = lax.psum((grads[0], grads[1], grads[5], grads[9]), ("tensor", "wide"))
    return (
        outputs[None],
        input_grads[None],
        shared[0][None],
        shared[1][None],
        wide_sums[0][None],
        wide_sums[1][None],
        wide_sums[2][None],
        shared[2][None],
        wide_sums[3][None],
        wide_sums[4][None],
        wide_sums[5][None],
        shared[3][None],
    )


def solution(mesh):
    placed = (
        P(None, ("wide", "tensor"), None),
        P(),
        P("section", None, None),
        P("section", None, None),
        P("section", None, "tensor"),
        P("section", "tensor"),
        P("section", "tensor", None),
        P("section", None),
        P("section", None, "tensor"),
        P("section", "tensor"),
        P("section", "tensor", None),
        P("section", None),
        P(None, ("wide", "tensor"), None),
    )
    return jax.shard_map(
        shards,
        mesh=mesh,
        in_specs=placed,
        out_specs=(
            P("section", None, ("wide", "tensor"), None),
            P("section", None, ("wide", "tensor"), None),
            P("section", None, None),
            P("section", None, None),
            P("section", None, "tensor"),
            P("section", "tensor"),
            P("section", "tensor", None),
            P("section", None),
            P("section", None, "tensor"),
            P("section", "tensor"),
            P("section", "tensor", None),
            P("section", None),
        ),
        check_vma=False,
    )
```

profile of v0, /device:TPU:0, one launch (start us, length us, event | category | flops | bytes accessed | tf_op | source)
XLA Modules:
  0.0 2170.8 jit_solution(3312942408855007990)
XLA Ops:
  9.4 616.0 %while.51 = (s32[]{:T(128)}, bf16[128,1024]{1,0:T(8,128)(2,1)S(1)}, bf16[4,128,1024]{2,1,0:T(8,128)(2,1)S(1)}, bf16[4,128,1024]{2,1,0:T(8,128)(2,1)}, pred[]{:T(...) while((s32[]{:T(128)}, bf16[128,1024]{1,0:T(8,128)(2,1)S(1)}, ...), condition=%wide.region_10.11_spmd, body=%wide.region_0.10_spmd.sunk | while | flops 4351912960 | bytes 123873424 | solution.py:385
  51.3 15.8 all-gather.7.cloned.1.call-done
  67.1 10.3 fusion.213
  86.6 12.0 all-gather.5.cloned.1.call-done
  98.6 10.3 fusion.214
  111.2 12.8 reduce-scatter.6.cloned.1.call-done
  173.5 16.3 all-gather.7.cloned.1.call-done
  189.9 10.3 fusion.213
  209.4 11.9 all-gather.5.cloned.1.call-done
  221.3 10.3 fusion.214
  233.8 12.8 reduce-scatter.6.cloned.1.call-done
  296.1 16.3 all-gather.7.cloned.1.call-done
  312.5 10.3 fusion.213
  331.9 12.0 all-gather.5.cloned.1.call-done
  344.0 10.3 fusion.214
  356.6 12.8 reduce-scatter.6.cloned.1.call-done
  418.9 16.3 all-gather.7.cloned.1.call-done
  435.2 10.3 fusion.213
  454.7 12.1 all-gather.5.cloned.1.call-done
  466.7 10.3 fusion.214
  479.3 12.8 reduce-scatter.6.cloned.1.call-done
  541.6 16.3 all-gather.7.cloned.1.call-done
  558.0 10.3 fusion.213
  577.5 11.9 all-gather.5.cloned.1.call-done
  589.3 10.3 fusion.214
  601.9 12.8 reduce-scatter.6.cloned.1.call-done
  627.5 1249.8 %while.52 = (s32[]{:T(128)}, f32[128,1024]{1,0:T(8,128)S(1)}, f32[2,1024]{1,0:T(2,128)S(1)}, f32[2,1024]{1,0:T(2,128)S(1)}, f32[1024,1536]{1,0:T(8,128)}, /*inde...) while((s32[]{:T(128)}, f32[128,1024]{1,0:T(8,128)S(1)}, ...), condition=%wide.region_36.37_spmd.clone, body=%wide.region_11.36_spmd.clone.sunk | while | flops 11745191936 | bytes 409961536 | solution.py:415
  686.9 19.3 all-gather.9.cloned.1.call-done
  706.2 10.3 fusion.250
  725.7 11.9 all-gather.11.cloned.1.call-done
  747.4 24.7 %fusion.252 = bf16[8,64,2048]{2,1,0:T(8,128)(2,1)} fusion(f32[8,2048,256]{2,1,0:T(8,128)} %fusion.251, f32[8,2048,256]{2,1,0:T(8,128)} %get-tuple-element.1225, f32[256,8]{0,1:T(8,128)S(1)} %log_add_fusion.5, pred[256,2048]{0,1:T(8,128)(4,1)S(1)} %fusion.244, bf16[256,8,48]{0,2,1:T(8,128)(2,1)S(1)} %copy-done.16, ...), kind=kOutput, calls=%fused_computation.92.clone.1 | convolution fusion | flops 584847360 | bytes 36446208 | tf_op jit(solution)/shard_map/while/body/eval_jaxpr/qhk,qhd->khd/dot_general | solution.py:254
  772.2 11.5 convolution_convert_fusion.11
  812.6 11.2 convolution_convert_fusion.14
  823.7 30.4 %fusion.253 = f32[256,8,64]{0,2,1:T(8,128)} fusion(bf16[2048,8,64]{0,2,1:T(8,128)(2,1)S(1)} %bitcast.522, f32[8,2048,256]{2,1,0:T(8,128)} %fusion.251, f32[8,2048,256]{2,1,0:T(8,128)} %get-tuple-element.1225, f32[256,8]{0,1:T(8,128)S(1)} %log_add_fusion.5, pred[256,2048]{0,1:T(8,128)(4,1)S(1)} %fusion.244), kind=kOutput, calls=%fused_computation.112.clone.1 | convolution fusion | flops 583012352 | bytes 36708352 | tf_op jit(solution)/shard_map/while/body/eval_jaxpr/qhk,khd->qhd/dot_general | solution.py:251
  927.4 17.4 all-gather.9.cloned.1.call-done
  944.7 10.2 fusion.250
  964.2 13.5 all-gather.11.cloned.1.call-done
  987.4 24.8 %fusion.252 = bf16[8,64,2048]{2,1,0:T(8,128)(2,1)} fusion(f32[8,2048,256]{2,1,0:T(8,128)} %fusion.251, f32[8,2048,256]{2,1,0:T(8,128)} %get-tuple-element.1225, f32[256,8]{0,1:T(8,128)S(1)} %log_add_fusion.5, pred[256,2048]{0,1:T(8,128)(4,1)S(1)} %fusion.244, bf16[256,8,48]{0,2,1:T(8,128)(2,1)S(1)} %copy-done.16, ...), kind=kOutput, calls=%fused_computation.92.clone.1 | convolution fusion | flops 584847360 | bytes 36446208 | tf_op jit(solution)/shard_map/while/body/eval_jaxpr/qhk,qhd->khd/dot_general | solution.py:254
  1012.3 11.5 convolution_convert_fusion.11
  1058.5 11.2 convolution_convert_fusion.14
  1069.7 30.4 %fusion.253 = f32[256,8,64]{0,2,1:T(8,128)} fusion(bf16[2048,8,64]{0,2,1:T(8,128)(2,1)S(1)} %bitcast.522, f32[8,2048,256]{2,1,0:T(8,128)} %fusion.251, f32[8,2048,256]{2,1,0:T(8,128)} %get-tuple-element.1225, f32[256,8]{0,1:T(8,128)S(1)} %log_add_fusion.5, pred[256,2048]{0,1:T(8,128)(4,1)S(1)} %fusion.244), kind=kOutput, calls=%fused_computation.112.clone.1 | convolution fusion | flops 583012352 | bytes 36708352 | tf_op jit(solution)/shard_map/while/body/eval_jaxpr/qhk,khd->qhd/dot_general | solution.py:251
  1173.4 17.4 all-gather.9.cloned.1.call-done
  1190.8 10.3 fusion.250
  1210.3 12.2 all-gather.11.cloned.1.call-done
  1232.1 24.7 %fusion.252 = bf16[8,64,2048]{2,1,0:T(8,128)(2,1)} fusion(f32[8,2048,256]{2,1,0:T(8,128)} %fusion.251, f32[8,2048,256]{2,1,0:T(8,128)} %get-tuple-element.1225, f32[256,8]{0,1:T(8,128)S(1)} %log_add_fusion.5, pred[256,2048]{0,1:T(8,128)(4,1)S(1)} %fusion.244, bf16[256,8,48]{0,2,1:T(8,128)(2,1)S(1)} %copy-done.16, ...), kind=kOutput, calls=%fused_computation.92.clone.1 | convolution fusion | flops 584847360 | bytes 36446208 | tf_op jit(solution)/shard_map/while/body/eval_jaxpr/qhk,qhd->khd/dot_general | solution.py:254
  1257.0 11.5 convolution_convert_fusion.11
  1303.2 11.2 convolution_convert_fusion.14
  1314.4 30.4 %fusion.253 = f32[256,8,64]{0,2,1:T(8,128)} fusion(bf16[2048,8,64]{0,2,1:T(8,128)(2,1)S(1)} %bitcast.522, f32[8,2048,256]{2,1,0:T(8,128)} %fusion.251, f32[8,2048,256]{2,1,0:T(8,128)} %get-tuple-element.1225, f32[256,8]{0,1:T(8,128)S(1)} %log_add_fusion.5, pred[256,2048]{0,1:T(8,128)(4,1)S(1)} %fusion.244), kind=kOutput, calls=%fused_computation.112.clone.1 | convolution fusion | flops 583012352 | bytes 36708352 | tf_op jit(solution)/shard_map/while/body/eval_jaxpr/qhk,khd->qhd/dot_general | solution.py:251
  1418.1 17.4 all-gather.9.cloned.1.call-done
  1435.5 10.3 fusion.250
  1455.0 12.2 all-gather.11.cloned.1.call-done
  1476.9 24.7 %fusion.252 = bf16[8,64,2048]{2,1,0:T(8,128)(2,1)} fusion(f32[8,2048,256]{2,1,0:T(8,128)} %fusion.251, f32[8,2048,256]{2,1,0:T(8,128)} %get-tuple-element.1225, f32[256,8]{0,1:T(8,128)S(1)} %log_add_fusion.5, pred[256,2048]{0,1:T(8,128)(4,1)S(1)} %fusion.244, bf16[256,8,48]{0,2,1:T(8,128)(2,1)S(1)} %copy-done.16, ...), kind=kOutput, calls=%fused_computation.92.clone.1 | convolution fusion | flops 584847360 | bytes 36446208 | tf_op jit(solution)/shard_map/while/body/eval_jaxpr/qhk,qhd->khd/dot_general | solution.py:254
  1501.7 11.5 convolution_convert_fusion.11
  1547.9 11.2 convolution_convert_fusion.14
  1559.2 30.4 %fusion.253 = f32[256,8,64]{0,2,1:T(8,128)} fusion(bf16[2048,8,64]{0,2,1:T(8,128)(2,1)S(1)} %bitcast.522, f32[8,2048,256]{2,1,0:T(8,128)} %fusion.251, f32[8,2048,256]{2,1,0:T(8,128)} %get-tuple-element.1225, f32[256,8]{0,1:T(8,128)S(1)} %log_add_fusion.5, pred[256,2048]{0,1:T(8,128)(4,1)S(1)} %fusion.244), kind=kOutput, calls=%fused_computation.112.clone.1 | convolution fusion | flops 583012352 | bytes 36708352 | tf_op jit(solution)/shard_map/while/body/eval_jaxpr/qhk,khd->qhd/dot_general | solution.py:251
  1662.8 17.4 all-gather.9.cloned.1.call-done
  1699.7 13.8 all-gather.11.cloned.1.call-done
  1723.2 24.7 %fusion.252 = bf16[8,64,2048]{2,1,0:T(8,128)(2,1)} fusion(f32[8,2048,256]{2,1,0:T(8,128)} %fusion.251, f32[8,2048,256]{2,1,0:T(8,128)} %get-tuple-element.1225, f32[256,8]{0,1:T(8,128)S(1)} %log_add_fusion.5, pred[256,2048]{0,1:T(8,128)(4,1)S(1)} %fusion.244, bf16[256,8,48]{0,2,1:T(8,128)(2,1)S(1)} %copy-done.16, ...), kind=kOutput, calls=%fused_computation.92.clone.1 | convolution fusion | flops 584847360 | bytes 36446208 | tf_op jit(solution)/shard_map/while/body/eval_jaxpr/qhk,qhd->khd/dot_general | solution.py:254
  1748.0 11.5 convolution_convert_fusion.11
  1794.3 11.2 convolution_convert_fusion.14
  1805.5 30.4 %fusion.253 = f32[256,8,64]{0,2,1:T(8,128)} fusion(bf16[2048,8,64]{0,2,1:T(8,128)(2,1)S(1)} %bitcast.522, f32[8,2048,256]{2,1,0:T(8,128)} %fusion.251, f32[8,2048,256]{2,1,0:T(8,128)} %get-tuple-element.1225, f32[256,8]{0,1:T(8,128)S(1)} %log_add_fusion.5, pred[256,2048]{0,1:T(8,128)(4,1)S(1)} %fusion.244), kind=kOutput, calls=%fused_computation.112.clone.1 | convolution fusion | flops 583012352 | bytes 36708352 | tf_op jit(solution)/shard_map/while/body/eval_jaxpr/qhk,khd->qhd/dot_general | solution.py:251
  1890.7 28.7 %all-reduce.1 = (bf16[1,1536]{1,0:T(2,128)(2,1)S(1)}, bf16[1,2048]{1,0:T(2,128)(2,1)S(1)}) all-reduce(bf16[1,1536]{1,0:T(2,128)(2,1)S(1)} %broadcast_in_dim.245, bf16[1,2048]{1,0:T(2,128)(2,1)S(1)} %broadcast_in_dim.252), channel_id=1, replica_groups=mesh['section'=2,'tensor'=2,'wide'=8] {'wide'}, use_global_device_ids=true, to_apply=%region_40.41 | all-reduce | flops 3584 | bytes 14336 | tf_op jit(solution)/shard_map/psum | solution.py:422
  1920.6 61.7 %all-reduce = (f32[1,2,1024]{2,1,0:T(2,128)}, f32[1,2,1024]{2,1,0:T(2,128)}, f32[1,1024]{1,0:T(1,128)}, f32[1,1024]{1,0:T(1,128)}) all-reduce(f32[1,2,1024]{2,1,0:T(2,128)S(1)} %bitcast.559, f32[1,2,1024]{2,1,0:T(2,128)S(1)} %bitcast.560, ...), channel_id=1, replica_groups=mesh['section'=2,'tensor'=2,'wide'=8] {'tensor','wide'}, use_global_device_ids=true, to_apply=%region_37.38 | all-reduce | flops 6144 | bytes 49152 | tf_op jit(solution)/shard_map/psum | solution.py:428
  1982.3 164.7 %all-reduce.5.cloned.1.call-done = (bf16[1,1024,1536]{2,1,0:T(8,128)(2,1)}, bf16[1,512,1024]{2,1,0:T(8,128)(2,1)}, bf16[1,1024,2048]{2,1,0:T(8,128)(2,1)}, bf16[1,2048,1024]{2,1,0:T(8,128)(2,1)}) async-done(((bf16[1,1024,1536]{2,1,0:T(8,128)(2,1)}, bf16[1,512,1024]{2,1,0:T(8,128)(2,1)}, bf16[1,1024,2048]{2,1,0:T(8,128)(2,1)}, bf16[1,2048,1024]{2,1,0:T(8,128)(2,1)}), (bf16[1,1024,1536]{2,1,0:T(8,128)(2,1)}, ...) | async-done | bytes 12582928 | tf_op jit(solution)/shard_map/psum | solution.py:421
  (954 shorter events, 968.7 us)
Async XLA Ops:
  9.4 57.7 %all-gather.7.cloned.1.call-start = ((), (), s32[]{:S(2)}) async-start(), calls=%async_computation.7 | async-start | bytes 2359296 | tf_op jit(solution)/shard_map/while/body/eval_jaxpr/all_gather | solution.py:103
  34.6 64.0 %all-gather.5.cloned.1.call-start = ((), (), s32[]{:S(2)}) async-start(), calls=%async_computation.6 | async-start | bytes 2359296 | tf_op jit(solution)/shard_map/while/body/eval_jaxpr/all_gather | solution.py:104
  35.4 88.6 %reduce-scatter.6.cloned.1.call-start = ((), (), s32[]{:S(2)}) async-start(), calls=%async_computation.8 | async-start | bytes 786432 | tf_op jit(solution)/shard_map/while/body/eval_jaxpr/reduce_scatter | solution.py:166
  108.9 25.8 %copy-start.4 = (bf16[4,128,1024]{2,1,0:T(8,128)(2,1)S(1)}, bf16[4,128,1024]{2,1,0:T(8,128)(2,1)}, u32[]{:S(2)}) copy-start(bf16[4,128,1024]{2,1,0:T(8,128)(2,1)} %copy-done.3) | copy-start | bytes 3145732 | tf_op jit(solution)/shard_map/while
  125.8 8.9 collective-permute-start
  134.7 55.1 %all-gather.7.cloned.1.call-start = ((), (), s32[]{:S(2)}) async-start(), calls=%async_computation.7 | async-start | bytes 2359296 | tf_op jit(solution)/shard_map/while/body/eval_jaxpr/all_gather | solution.py:103
  157.8 63.4 %all-gather.5.cloned.1.call-start = ((), (), s32[]{:S(2)}) async-start(), calls=%async_computation.6 | async-start | bytes 2359296 | tf_op jit(solution)/shard_map/while/body/eval_jaxpr/all_gather | solution.py:104
  158.6 88.0 %reduce-scatter.6.cloned.1.call-start = ((), (), s32[]{:S(2)}) async-start(), calls=%async_computation.8 | async-start | bytes 786432 | tf_op jit(solution)/shard_map/while/body/eval_jaxpr/reduce_scatter | solution.py:166
  231.5 25.8 %copy-start.4 = (bf16[4,128,1024]{2,1,0:T(8,128)(2,1)S(1)}, bf16[4,128,1024]{2,1,0:T(8,128)(2,1)}, u32[]{:S(2)}) copy-start(bf16[4,128,1024]{2,1,0:T(8,128)(2,1)} %copy-done.3) | copy-start | bytes 3145732 | tf_op jit(solution)/shard_map/while
  248.5 8.9 collective-permute-start
  257.4 55.1 %all-gather.7.cloned.1.call-start = ((), (), s32[]{:S(2)}) async-start(), calls=%async_computation.7 | async-start | bytes 2359296 | tf_op jit(solution)/shard_map/while/body/eval_jaxpr/all_gather | solution.py:103
  280.4 63.6 %all-gather.5.cloned.1.call-start = ((), (), s32[]{:S(2)}) async-start(), calls=%async_computation.6 | async-start | bytes 2359296 | tf_op jit(solution)/shard_map/while/body/eval_jaxpr/all_gather | solution.py:104
  281.3 88.1 %reduce-scatter.6.cloned.1.call-start = ((), (), s32[]{:S(2)}) async-start(), calls=%async_computation.8 | async-start | bytes 786432 | tf_op jit(solution)/shard_map/while/body/eval_jaxpr/reduce_scatter | solution.py:166
  354.3 25.8 %copy-start.4 = (bf16[4,128,1024]{2,1,0:T(8,128)(2,1)S(1)}, bf16[4,128,1024]{2,1,0:T(8,128)(2,1)}, u32[]{:S(2)}) copy-start(bf16[4,128,1024]{2,1,0:T(8,128)(2,1)} %copy-done.3) | copy-start | bytes 3145732 | tf_op jit(solution)/shard_map/while
  371.2 8.9 collective-permute-start
  380.1 55.1 %all-gather.7.cloned.1.call-start = ((), (), s32[]{:S(2)}) async-start(), calls=%async_computation.7 | async-start | bytes 2359296 | tf_op jit(solution)/shard_map/while/body/eval_jaxpr/all_gather | solution.py:103
  403.2 63.6 %all-gather.5.cloned.1.call-start = ((), (), s32[]{:S(2)}) async-start(), calls=%async_computation.6 | async-start | bytes 2359296 | tf_op jit(solution)/shard_map/while/body/eval_jaxpr/all_gather | solution.py:104
  404.0 88.1 %reduce-scatter.6.cloned.1.call-start = ((), (), s32[]{:S(2)}) async-start(), calls=%async_computation.8 | async-start | bytes 786432 | tf_op jit(solution)/shard_map/while/body/eval_jaxpr/reduce_scatter | solution.py:166
  477.0 25.8 %copy-start.4 = (bf16[4,128,1024]{2,1,0:T(8,128)(2,1)S(1)}, bf16[4,128,1024]{2,1,0:T(8,128)(2,1)}, u32[]{:S(2)}) copy-start(bf16[4,128,1024]{2,1,0:T(8,128)(2,1)} %copy-done.3) | copy-start | bytes 3145732 | tf_op jit(solution)/shard_map/while
  493.9 8.9 collective-permute-start
  502.8 55.1 %all-gather.7.cloned.1.call-start = ((), (), s32[]{:S(2)}) async-start(), calls=%async_computation.7 | async-start | bytes 2359296 | tf_op jit(solution)/shard_map/while/body/eval_jaxpr/all_gather | solution.py:103
  525.9 63.4 %all-gather.5.cloned.1.call-start = ((), (), s32[]{:S(2)}) async-start(), calls=%async_computation.6 | async-start | bytes 2359296 | tf_op jit(solution)/shard_map/while/body/eval_jaxpr/all_gather | solution.py:104
  526.7 88.0 %reduce-scatter.6.cloned.1.call-start = ((), (), s32[]{:S(2)}) async-start(), calls=%async_computation.8 | async-start | bytes 786432 | tf_op jit(solution)/shard_map/while/body/eval_jaxpr/reduce_scatter | solution.py:166
  599.6 25.8 %copy-start.4 = (bf16[4,128,1024]{2,1,0:T(8,128)(2,1)S(1)}, bf16[4,128,1024]{2,1,0:T(8,128)(2,1)}, u32[]{:S(2)}) copy-start(bf16[4,128,1024]{2,1,0:T(8,128)(2,1)} %copy-done.3) | copy-start | bytes 3145732 | tf_op jit(solution)/shard_map/while
  616.5 8.9 collective-permute-start
  651.0 55.2 %all-gather.9.cloned.1.call-start = ((), (), s32[]{:S(2)}) async-start(), calls=%async_computation.9 | async-start | bytes 2359296 | tf_op jit(solution)/shard_map/while/body/eval_jaxpr/all_gather | solution.py:103
  674.2 63.5 %all-gather.11.cloned.1.call-start = ((), (), s32[]{:S(2)}) async-start(), calls=%async_computation.11 | async-start | bytes 2359296 | tf_op jit(solution)/shard_map/while/body/eval_jaxpr/all_gather | solution.py:104
  675.0 180.2 %reduce-scatter.10.cloned.1.call-start = ((), (), s32[]{:S(2)}) async-start(), calls=%async_computation.12 | async-start | bytes 2359296 | tf_op jit(solution)/shard_map/while/body/eval_jaxpr/reduce_scatter | solution.py:261
  772.2 86.0 %reduce-scatter.8.cloned.1.call-start = ((), (), s32[]{:S(2)}) async-start(), calls=%async_computation.10 | async-start | bytes 2359296 | tf_op jit(solution)/shard_map/while/body/eval_jaxpr/reduce_scatter | solution.py:267
  783.7 86.7 %reduce-scatter.14.cloned.1.call-start = ((), (), s32[]{:S(2)}) async-start(), calls=%async_computation.14 | async-start | bytes 786432 | tf_op jit(solution)/shard_map/while/body/eval_jaxpr/reduce_scatter | solution.py:294
  801.6 75.5 %reduce-scatter.12.cloned.1.call-start = ((), (), s32[]{:S(2)}) async-start(), calls=%async_computation.13 | async-start | bytes 786432 | tf_op jit(solution)/shard_map/while/body/eval_jaxpr/reduce_scatter | solution.py:291
  881.4 9.9 collective-permute-start.1
  891.4 25.8 %copy-start.14 = (f32[128,1024]{1,0:T(8,128)}, f32[128,1024]{1,0:T(8,128)S(1)}, u32[]{:S(2)}) copy-start(f32[128,1024]{1,0:T(8,128)S(1)} %get-tuple-element.1368) | copy-start | bytes 1572868 | tf_op jit(solution)/shard_map/while
  891.4 53.3 %all-gather.9.cloned.1.call-start = ((), (), s32[]{:S(2)}) async-start(), calls=%async_computation.9 | async-start | bytes 2359296 | tf_op jit(solution)/shard_map/while/body/eval_jaxpr/all_gather | solution.py:103
  914.6 63.0 %all-gather.11.cloned.1.call-start = ((), (), s32[]{:S(2)}) async-start(), calls=%async_computation.11 | async-start | bytes 2359296 | tf_op jit(solution)/shard_map/while/body/eval_jaxpr/all_gather | solution.py:104
  915.5 185.7 %reduce-scatter.10.cloned.1.call-start = ((), (), s32[]{:S(2)}) async-start(), calls=%async_computation.12 | async-start | bytes 2359296 | tf_op jit(solution)/shard_map/while/body/eval_jaxpr/reduce_scatter | solution.py:261
  1012.2 91.9 %reduce-scatter.8.cloned.1.call-start = ((), (), s32[]{:S(2)}) async-start(), calls=%async_computation.10 | async-start | bytes 2359296 | tf_op jit(solution)/shard_map/while/body/eval_jaxpr/reduce_scatter | solution.py:267
  1023.8 94.8 %reduce-scatter.14.cloned.1.call-start = ((), (), s32[]{:S(2)}) async-start(), calls=%async_computation.14 | async-start | bytes 786432 | tf_op jit(solution)/shard_map/while/body/eval_jaxpr/reduce_scatter | solution.py:294
  1041.7 81.4 %reduce-scatter.12.cloned.1.call-start = ((), (), s32[]{:S(2)}) async-start(), calls=%async_computation.13 | async-start | bytes 786432 | tf_op jit(solution)/shard_map/while/body/eval_jaxpr/reduce_scatter | solution.py:291
  1127.5 9.9 collective-permute-start.1
  1137.5 25.8 %copy-start.14 = (f32[128,1024]{1,0:T(8,128)}, f32[128,1024]{1,0:T(8,128)S(1)}, u32[]{:S(2)}) copy-start(f32[128,1024]{1,0:T(8,128)S(1)} %get-tuple-element.1368) | copy-start | bytes 1572868 | tf_op jit(solution)/shard_map/while
  1137.5 53.3 %all-gather.9.cloned.1.call-start = ((), (), s32[]{:S(2)}) async-start(), calls=%async_computation.9 | async-start | bytes 2359296 | tf_op jit(solution)/shard_map/while/body/eval_jaxpr/all_gather | solution.py:103
  1160.7 61.7 %all-gather.11.cloned.1.call-start = ((), (), s32[]{:S(2)}) async-start(), calls=%async_computation.11 | async-start | bytes 2359296 | tf_op jit(solution)/shard_map/while/body/eval_jaxpr/all_gather | solution.py:104
  1161.5 184.4 %reduce-scatter.10.cloned.1.call-start = ((), (), s32[]{:S(2)}) async-start(), calls=%async_computation.12 | async-start | bytes 2359296 | tf_op jit(solution)/shard_map/while/body/eval_jaxpr/reduce_scatter | solution.py:261
  1256.9 91.9 %reduce-scatter.8.cloned.1.call-start = ((), (), s32[]{:S(2)}) async-start(), calls=%async_computation.10 | async-start | bytes 2359296 | tf_op jit(solution)/shard_map/while/body/eval_jaxpr/reduce_scatter | solution.py:267
  1268.5 94.9 %reduce-scatter.14.cloned.1.call-start = ((), (), s32[]{:S(2)}) async-start(), calls=%async_computation.14 | async-start | bytes 786432 | tf_op jit(solution)/shard_map/while/body/eval_jaxpr/reduce_scatter | solution.py:294
  1286.4 81.4 %reduce-scatter.12.cloned.1.call-start = ((), (), s32[]{:S(2)}) async-start(), calls=%async_computation.13 | async-start | bytes 786432 | tf_op jit(solution)/shard_map/while/body/eval_jaxpr/reduce_scatter | solution.py:291
  1372.2 9.9 collective-permute-start.1
  1382.2 53.3 %all-gather.9.cloned.1.call-start = ((), (), s32[]{:S(2)}) async-start(), calls=%async_computation.9 | async-start | bytes 2359296 | tf_op jit(solution)/shard_map/while/body/eval_jaxpr/all_gather | solution.py:103
  1405.4 61.7 %all-gather.11.cloned.1.call-start = ((), (), s32[]{:S(2)}) async-start(), calls=%async_computation.11 | async-start | bytes 2359296 | tf_op jit(solution)/shard_map/while/body/eval_jaxpr/all_gather | solution.py:104
  1406.3 184.4 %reduce-scatter.10.cloned.1.call-start = ((), (), s32[]{:S(2)}) async-start(), calls=%async_computation.12 | async-start | bytes 2359296 | tf_op jit(solution)/shard_map/while/body/eval_jaxpr/reduce_scatter | solution.py:261
  1501.6 91.9 %reduce-scatter.8.cloned.1.call-start = ((), (), s32[]{:S(2)}) async-start(), calls=%async_computation.10 | async-start | bytes 2359296 | tf_op jit(solution)/shard_map/while/body/eval_jaxpr/reduce_scatter | solution.py:267
  1513.2 94.9 %reduce-scatter.14.cloned.1.call-start = ((), (), s32[]{:S(2)}) async-start(), calls=%async_computation.14 | async-start | bytes 786432 | tf_op jit(solution)/shard_map/while/body/eval_jaxpr/reduce_scatter | solution.py:294
  1531.1 81.3 %reduce-scatter.12.cloned.1.call-start = ((), (), s32[]{:S(2)}) async-start(), calls=%async_computation.13 | async-start | bytes 786432 | tf_op jit(solution)/shard_map/while/body/eval_jaxpr/reduce_scatter | solution.py:291
  1616.9 9.9 collective-permute-start.1
  1626.9 25.8 %copy-start.14 = (f32[128,1024]{1,0:T(8,128)}, f32[128,1024]{1,0:T(8,128)S(1)}, u32[]{:S(2)}) copy-start(f32[128,1024]{1,0:T(8,128)S(1)} %get-tuple-element.1368) | copy-start | bytes 1572868 | tf_op jit(solution)/shard_map/while
  1626.9 53.3 %all-gather.9.cloned.1.call-start = ((), (), s32[]{:S(2)}) async-start(), calls=%async_computation.9 | async-start | bytes 2359296 | tf_op jit(solution)/shard_map/while/body/eval_jaxpr/all_gather | solution.py:103
  1650.1 63.3 %all-gather.11.cloned.1.call-start = ((), (), s32[]{:S(2)}) async-start(), calls=%async_computation.11 | async-start | bytes 2359296 | tf_op jit(solution)/shard_map/while/body/eval_jaxpr/all_gather | solution.py:104
  1650.9 186.0 %reduce-scatter.10.cloned.1.call-start = ((), (), s32[]{:S(2)}) async-start(), calls=%async_computation.12 | async-start | bytes 2359296 | tf_op jit(solution)/shard_map/while/body/eval_jaxpr/reduce_scatter | solution.py:261
  1748.0 91.9 %reduce-scatter.8.cloned.1.call-start = ((), (), s32[]{:S(2)}) async-start(), calls=%async_computation.10 | async-start | bytes 2359296 | tf_op jit(solution)/shard_map/while/body/eval_jaxpr/reduce_scatter | solution.py:267
  1759.5 94.9 %reduce-scatter.14.cloned.1.call-start = ((), (), s32[]{:S(2)}) async-start(), calls=%async_computation.14 | async-start | bytes 786432 | tf_op jit(solution)/shard_map/while/body/eval_jaxpr/reduce_scatter | solution.py:294
  1777.4 81.3 %reduce-scatter.12.cloned.1.call-start = ((), (), s32[]{:S(2)}) async-start(), calls=%async_computation.13 | async-start | bytes 786432 | tf_op jit(solution)/shard_map/while/body/eval_jaxpr/reduce_scatter | solution.py:291
  1863.2 9.9 collective-permute-start.1
  1877.3 269.8 %all-reduce.5.cloned.1.call-start = ((), (), s32[]{:S(2)}) async-start(), calls=%async_computation.5 | async-start | bytes 25165824 | tf_op jit(solution)/shard_map/psum | solution.py:421
  (129 other events, 1452.2 us)
Sparse Core Ops, SparseCore 0:
  34.8 32.3 all-gather.6
  68.7 29.8 all-gather.4
  110.4 13.6 reduce-scatter.5
  158.0 31.8 all-gather.6
  191.3 29.8 all-gather.4
  233.0 13.6 reduce-scatter.5
  280.6 31.8 all-gather.6
  314.1 29.8 all-gather.4
  355.7 13.6 reduce-scatter.5
  403.3 31.8 all-gather.6
  436.8 29.8 all-gather.4
  478.5 13.6 reduce-scatter.5
  526.0 31.8 all-gather.6
  559.4 29.8 all-gather.4
  601.0 13.6 reduce-scatter.5
  674.3 31.8 all-gather.8
  707.7 29.8 all-gather.10
  772.3 34.8 reduce-scatter.9
  809.5 34.4 reduce-scatter.7
  846.3 13.0 reduce-scatter.13
  863.5 13.5 reduce-scatter.11
  914.8 29.9 all-gather.8
  946.4 31.2 all-gather.10
  1012.3 34.8 reduce-scatter.9
  1049.6 34.4 reduce-scatter.7
  1086.3 13.1 reduce-scatter.13
  1109.4 13.5 reduce-scatter.11
  1160.8 29.9 all-gather.8
  1192.5 29.8 all-gather.10
  1257.0 34.9 reduce-scatter.9
  1294.4 34.3 reduce-scatter.7
  1331.1 13.0 reduce-scatter.13
  1354.2 13.5 reduce-scatter.11
  1405.5 29.9 all-gather.8
  1437.2 29.8 all-gather.10
  1501.8 34.8 reduce-scatter.9
  1538.9 34.4 reduce-scatter.7
  1575.7 13.1 reduce-scatter.13
  1598.9 13.5 reduce-scatter.11
  1650.2 29.9 all-gather.8
  1681.9 31.5 all-gather.10
  1748.1 34.8 reduce-scatter.9
  1785.2 34.3 reduce-scatter.7
  1822.0 13.1 reduce-scatter.13
  1845.2 13.4 reduce-scatter.11
Sparse Core Ops, SparseCore 1:
  1890.7 256.3 all-reduce.4
where the time goes:
time: 2190 us; the launch traced here: 2170 us
  matrix products  844 us (39%)
  waiting for transfers between devices  618 us (28%)
  blocking collectives  289 us (13%)
  other arithmetic  226 us (10%)
  local copies, waits for them, and re-layouts  112 us (5%)
  loops' own time  41.1 us (2%)
  starting transfers between devices  25 us (1%)
    all_gather x10, waiting for transfers between devices, gather_keys(): lax.all_gather(key_rows, 'wide', axis=0, tiled=True)  170 us
    psum x1, waiting for transfers between devices, shards(): lax.psum(grads[2].astype(jnp.bfloat16), 'wide').astype(jnp.float32)  165 us
    dot_general x5, matrix products, backward_parts(): jnp.einsum('qhk,khd->qhd', score_grad, parts['key_heads'], preferred_elem...  152 us
    dot_general x5, matrix products, backward_parts(): jnp.einsum('qhk,qhd->khd', score_grad, parts['queries'], preferred_elemen...  124 us
    all_gather x10, waiting for transfers between devices, gather_keys(): lax.all_gather(value_rows, 'wide', axis=0, tiled=True)  123 us
    dot_general x10, matrix products, forward_parts(): jnp.einsum('qhk,khd->qhd', probs_low, value_heads, preferred_element_type...  107 us
    dot_general x10, matrix products, forward_parts(): jnp.einsum('qhd,khd->qhk', queries, key_heads, preferred_element_type=jnp...  103 us
    reduce_sum x10, other arithmetic, forward_parts(): jnp.sum(jnp.exp(scores - row_max), axis=-1, keepdims=True)  91.9 us
  transfers between devices with their start and end apart: 56, of which 41 were waited for; matrix products, arithmetic and copies ran while one was open for 34% of the time, Pallas kernels for 0%

commit v1 on v0

--- a/solution.py
+++ b/solution.py
@@ -1,8 +1,11 @@
+import functools
 import math
 
 import jax
 import jax.numpy as jnp
 from jax import lax
+from jax.experimental import pallas as pl
+from jax.experimental.pallas import tpu as pltpu
 from jax.sharding import PartitionSpec as P
 
 HEAD_DIM = 64
@@ -12,6 +15,897 @@
 
 EPSILON = 1e-05
 ROPE_BASE = 10000.0
+
+MESH = pl.DeviceIdType.MESH
+F32 = jnp.float32
+BF16 = jnp.bfloat16
+LANES = 128
+BLOCK = 512
+COLS = 512
+NEG = -1e30
+SCORE_SCALE = math.log2(math.e) / math.sqrt(HEAD_DIM)
+
+
+def dot(a, b):
+    return jnp.dot(a, b, preferred_element_type=F32)
+
+
+def dot_t(a, b):
+    return lax.dot_general(a, b, (((1,), (1,)), ((), ())), preferred_element_type=F32)
+
+
+def t_dot(a, b):
+    return lax.dot_general(a, b, (((0,), (0,)), ((), ())), preferred_element_type=F32)
+
+
+def lane_low(rows):
+    return lax.broadcasted_iota(jnp.int32, (rows, LANES), 1) < HEAD_DIM
+
+
+def turn(values):
+    return pltpu.roll(values, HEAD_DIM, 1)
+
+
+def rotary(values, cos_ref, front_ref, back_ref, seq, sign):
+    cos, front, back = cos_ref[seq], front_ref[seq], back_ref[seq]
+    ahead = pltpu.roll(values, LANES - ROT // 2, 1)
+    behind = pltpu.roll(values, ROT // 2, 1)
+    return values * cos + sign * (ahead * front + behind * back)
+
+
+def pair_up(first, second, low):
+    half = first.shape[0]
+    top = jnp.where(low, first, turn(second))
+    bottom = jnp.where(low, turn(first), second)
+    del half
+    return top, bottom
+
+
+def relay_kernel(
+    dims,
+    ends,
+    x_hbm,
+    cot_hbm,
+    gain,
+    shift,
+    qkv_b,
+    up_b,
+    out_b,
+    wqkv_hbm,
+    wdense_hbm,
+    wup_hbm,
+    wdown_hbm,
+    cos,
+    front,
+    back,
+    out_hbm,
+    ig_hbm,
+    norm_hbm,
+    g_hbm,
+    mixed_hbm,
+    hid_hbm,
+    dpre_hbm,
+    dpk_hbm,
+    small,
+    wqkv,
+    wdense,
+    wup,
+    wdown,
+    xfull,
+    gfull,
+    cot,
+    qkv_r,
+    mix_r,
+    do_r,
+    dqkv_r,
+    rsf_r,
+    rsb_r,
+    qkv_st,
+    o_st,
+    do_st,
+    dqkv_st,
+    rsf_st,
+    rsb_st,
+    out_st,
+    gx_st,
+    ig_st,
+    norm_st,
+    mixed_st,
+    hid_st,
+    dpre_st,
+    dpk_st,
+    slope,
+    part,
+    dn1,
+    qm,
+    kr,
+    vx,
+    dox,
+    dq,
+    lse,
+    delta,
+    scores,
+    peak,
+    acc,
+    wsem,
+    ownx_sem,
+    yx_s,
+    yx_r,
+    owng_sem,
+    yg_s,
+    yg_r,
+    qkv_ss,
+    qkv_rs,
+    o_ss,
+    o_rs,
+    do_ss,
+    do_rs,
+    dqkv_ss,
+    dqkv_rs,
+    rsf_ss,
+    rsf_rs,
+    rsb_ss,
+    rsb_rs,
+    xs_ss,
+    gs_ss,
+    store_sem,
+):
+    micro, rows, group, wide, heads, d_model, ff = dims
+    sect = lax.axis_index("section")
+    tens = lax.axis_index("tensor")
+    me = lax.axis_index("wide")
+    pairs = heads // 2
+    per_source = group + group // 2
+    half = group // 2
+    q_blocks = SEQ // BLOCK
+    sources = BLOCK // group
+    my_rows = pl.ds(pl.multiple_of(tens * rows, rows), rows)
+    his_rows = pl.ds(pl.multiple_of((1 - tens) * rows, rows), rows)
+    x_dev = {"section": 1 - sect}
+    y_dev = {"tensor": 1 - tens}
+    low_half = lane_low(half)
+    low_group = lane_low(group)
+
+    def remote(src, dst, ss, rs, dev):
+        return pltpu.make_async_remote_copy(
+            src_ref=src, dst_ref=dst, send_sem=ss, recv_sem=rs, device_id=dev, device_id_type=MESH
+        )
+
+    def arrived(ref, sem):
+        pltpu.make_async_copy(ref, ref, sem).wait()
+
+    def y_send_x(s):
+        own = xfull.at[s, my_rows]
+        return remote(own, own, yx_s.at[s], yx_r.at[s], y_dev)
+
+    def y_send_g(s):
+        own = gfull.at[s, my_rows]
+        return remote(own, own, yg_s.at[s], yg_r.at[s], y_dev)
+
+    def spread(stage, target, seq, dest, ss, rs):
+        @pl.when(dest == me)
+        def _():
+            pltpu.make_async_copy(stage, target.at[seq, me], rs).start()
+
+        @pl.when(dest != me)
+        def _():
+            remote(stage, target.at[seq, me], ss, rs, {"wide": dest}).start()
+
+    loads = [
+        pltpu.make_async_copy(source, target, wsem.at[i])
+        for i, (source, target) in enumerate(
+            ((wqkv_hbm, wqkv), (wup_hbm, wup), (wdown_hbm, wdown), (wdense_hbm, wdense))
+        )
+    ]
+
+    barrier = pltpu.get_barrier_semaphore()
+    for dev in [x_dev, y_dev] + [{"wide": lax.rem(me + k, wide)} for k in range(1, wide)]:
+        pl.semaphore_signal(barrier, inc=1, device_id=dev, device_id_type=MESH)
+
+    @pl.when(sect == 0)
+    def _():
+        for s in range(micro):
+            pltpu.make_async_copy(x_hbm.at[s], xfull.at[s, my_rows], ownx_sem.at[s]).start()
+
+    for load in loads:
+        load.start()
+
+    @pl.when(sect == 1)
+    def _():
+        for s in range(micro):
+            pltpu.make_async_copy(cot_hbm.at[s], cot.at[s], owng_sem.at[s]).start()
+
+    small[...] = jnp.zeros_like(small)
+    pl.semaphore_wait(barrier, wide + 1)
+
+    @pl.when(sect == 0)
+    def _():
+        for s in range(micro):
+            arrived(xfull.at[s, my_rows], ownx_sem.at[s])
+            y_send_x(s).start()
+
+    @pl.when(sect == 1)
+    def _():
+        for s in range(micro):
+            arrived(cot.at[s], owng_sem.at[s])
+
+            def chunk(i, carry, s=s):
+                at = pl.ds(pl.multiple_of(i * 32, 32), 32)
+                there = pl.ds(pl.multiple_of(tens * rows + i * 32, 32), 32)
+                gfull[s, there, :] = cot[s, at, :].astype(BF16)
+                return carry
+
+            lax.fori_loop(0, rows // 32, chunk, 0)
+            y_send_g(s).start()
+
+    for load in loads:
+        load.wait()
+
+    def normed_rows(values):
+        center = jnp.mean(values, axis=-1, keepdims=True)
+        centred = values - center
+        spread_of = jnp.mean(centred * centred, axis=-1, keepdims=True)
+        inv = lax.rsqrt(spread_of + EPSILON)
+        return centred * inv, inv
+
+    def starts_of(s, tokens):
+        found = jnp.zeros_like(tokens)
+        for j in range(ends.shape[1]):
+            end = ends[s, j]
+            found = jnp.where(tokens >= end, end, found)
+        return found
+
+    def unpack_heads(s):
+        def step(src, carry):
+            qk = qkv_r[s, src, 0:group, :].astype(F32)
+            at = pl.multiple_of(src * group, group)
+            qm[pl.ds(at, group), :] = jnp.where(low_group, qk, 0.0).astype(BF16)
+            kr[pl.ds(at, group), :] = turn(qk).astype(BF16)
+            packed_v = qkv_r[s, src, group:per_source, :].astype(F32)
+            ones = jnp.where(
+                lax.broadcasted_iota(jnp.int32, (half, LANES), 1) == HEAD_DIM, 1.0, 0.0
+            )
+            vx[pl.ds(at, half), :] = jnp.where(low_half, packed_v, ones).astype(BF16)
+            vx[pl.ds(pl.multiple_of(at + half, half), half), :] = jnp.where(
+                low_half, turn(packed_v), ones
+            ).astype(BF16)
+            return carry
+
+        lax.fori_loop(0, wide, step, 0)
+
+    def forward(s):
+        @pl.when(sect == 1)
+        def _():
+            arrived(xfull.at[s, my_rows], ownx_sem.at[s])
+            y_send_x(s).start()
+
+        arrived(xfull.at[s, his_rows], yx_r.at[s])
+
+        def norm_step(i, carry):
+            at = pl.ds(pl.multiple_of(i * 32, 32), 32)
+            a, _ = normed_rows(xfull[s, at, :].astype(F32))
+            norm_st[0, at, :] = (a * gain[0:1, :] + shift[0:1, :]).astype(BF16)
+            norm_st[1, at, :] = (a * gain[1:2, :] + shift[1:2, :]).astype(BF16)
+            return carry
+
+        lax.fori_loop(0, group // 32, norm_step, 0)
+        pltpu.make_async_copy(norm_st.at[0], norm_hbm.at[0, s], store_sem.at[0]).start()
+        pltpu.make_async_copy(norm_st.at[1], norm_hbm.at[1, s], store_sem.at[1]).start()
+
+        def qkv_step(k, carry):
+            pair = lax.rem(me // 2 + 1 + k, pairs)
+            cols = pl.ds(pl.multiple_of(pair * 3 * LANES, LANES), 3 * LANES)
+            packed = dot(norm_st[0], wqkv[:, cols]) + qkv_b[:, cols]
+            first, middle, last = (packed[:, i * LANES : (i + 1) * LANES] for i in range(3))
+            qk0 = rotary(first, cos, front, back, s, 1.0)
+            qk1 = rotary(
+                turn(jnp.where(low_group, last, middle)), cos, front, back, s, 1.0
+            )
+            vv = jnp.where(low_group, middle, last)
+            v0 = jnp.where(low_half, vv[:half], turn(vv[half:]))
+            v1 = jnp.where(low_half, turn(vv[:half]), vv[half:])
+            for i, (qk, v) in enumerate(((qk0, v0), (qk1, v1))):
+                qkv_st[2 * pair + i, 0:group, :] = qk.astype(BF16)
+                qkv_st[2 * pair + i, group:per_source, :] = v.astype(BF16)
+            for i in range(2):
+                dest = 2 * pair + i
+                spread(qkv_st.at[dest], qkv_r, s, dest, qkv_ss.at[0], qkv_rs.at[s])
+            return carry
+
+        lax.fori_loop(0, pairs, qkv_step, 0)
+
+    def forward_ff(s):
+        def ff_step(j, carry):
+            cols = pl.ds(pl.multiple_of(j * COLS, COLS), COLS)
+            pre = dot(norm_st[1], wup[:, cols]) + up_b[:, cols]
+            cumul = 0.5 * (1.0 + lax.erf(pre * (1.0 / math.sqrt(2.0))))
+            density = jnp.exp(-0.5 * pre * pre) * (1.0 / math.sqrt(2.0 * math.pi))
+            hid = (pre * cumul).astype(BF16)
+            hid_st[:, cols] = hid
+            slope[s, :, cols] = (cumul + pre * density).astype(BF16)
+            term = dot(hid, wdown[cols, :])
+
+            @pl.when(j == 0)
+            def _():
+                part[...] = term
+
+            @pl.when(j > 0)
+            def _():
+                part[...] += term
+
+            return carry
+
+        lax.fori_loop(0, ff // COLS, ff_step, 0)
+        pltpu.make_async_copy(hid_st, hid_hbm.at[s], store_sem.at[2]).start()
+
+    def forward_attention(s):
+        arrived(qkv_r.at[s], qkv_rs.at[s])
+        arrived(qkv_st.at[pl.ds(0, wide - 1)], qkv_ss.at[0])
+        unpack_heads(s)
+
+        def q_step(i, carry):
+            q_at = pl.ds(pl.multiple_of(i * BLOCK, BLOCK), BLOCK)
+            tokens = i * BLOCK + lax.broadcasted_iota(jnp.int32, (BLOCK, LANES), 0)
+            begin = starts_of(s, tokens)[:, 0:1]
+            token = tokens[:, 0:1]
+            peak[...] = jnp.full(peak.shape, NEG, F32)
+
+            def score_step(j, inner):
+                k_at = pl.ds(pl.multiple_of(j * BLOCK, BLOCK), BLOCK)
+                raw = dot_t(qm[q_at, :], kr[k_at, :])
+                u = j * BLOCK + lax.broadcasted_iota(jnp.int32, (BLOCK, BLOCK), 1)
+                raw = jnp.where((u >= begin) & (u <= token), raw, NEG)
+                scores[:, k_at] = raw
+                best = peak[...]
+                for k in range(BLOCK // LANES):
+                    best = jnp.maximum(best, raw[:, k * LANES : (k + 1) * LANES])
+                peak[...] = best
+                return inner
+
+            lax.fori_loop(0, i + 1, score_step, 0)
+            top = jnp.max(peak[...], axis=1, keepdims=True) * SCORE_SCALE
+            acc[...] = jnp.zeros_like(acc)
+
+            def value_step(j, inner):
+                k_at = pl.ds(pl.multiple_of(j * BLOCK, BLOCK), BLOCK)
+                probs = jnp.exp2(scores[:, k_at] * SCORE_SCALE - top)
+                acc[...] += dot(probs.astype(BF16), vx[k_at, :])
+                return inner
+
+            lax.fori_loop(0, i + 1, value_step, 0)
+            total = acc[:, HEAD_DIM : HEAD_DIM + 1]
+            out = acc[...] / total
+            log_total = top + jnp.log2(total)
+            lse[s, i] = jnp.broadcast_to(log_total, (BLOCK, LANES)).T[0:8, :]
+            for k in range(sources):
+                first = out[k * group : k * group + half]
+                second = out[k * group + half : (k + 1) * group]
+                source = i * sources + k
+                o_st[s, source] = jnp.where(low_half, first, turn(second)).astype(BF16)
+                spread(o_st.at[s, source], mix_r, s, source, o_ss.at[s], o_rs.at[s])
+            return carry
+
+        lax.fori_loop(0, q_blocks, q_step, 0)
+
+    def forward_out(s):
+        arrived(mix_r.at[s], o_rs.at[s])
+        arrived(o_st.at[s, pl.ds(0, wide - 1)], o_ss.at[s])
+        for pair in range(pairs):
+            top, bottom = pair_up(
+                mix_r[s, 2 * pair].astype(F32), mix_r[s, 2 * pair + 1].astype(F32), low_half
+            )
+            mixed_st[0:half, pair * LANES : (pair + 1) * LANES] = top.astype(BF16)
+            mixed_st[half:group, pair * LANES : (pair + 1) * LANES] = bottom.astype(BF16)
+        pltpu.make_async_copy(mixed_st, mixed_hbm.at[s], store_sem.at[3]).start()
+        part[...] += dot(mixed_st[...], wdense[...])
+        rsf_st[...] = part[his_rows, :].astype(BF16)
+        remote(rsf_st, rsf_r.at[s], rsf_ss.at[0], rsf_rs.at[s], y_dev).start()
+
+    def forward_end(s):
+        arrived(rsf_r.at[s], rsf_rs.at[s])
+
+        def out_step(i, carry):
+            at = pl.ds(pl.multiple_of(i * 32, 32), 32)
+            there = pl.ds(pl.multiple_of(tens * rows + i * 32, 32), 32)
+            branch = part[there, :] + rsf_r[s, at, :].astype(F32) + out_b[...]
+            out_st[s, at, :] = (xfull[s, there, :].astype(F32) + branch).astype(BF16)
+            return carry
+
+        lax.fori_loop(0, rows // 32, out_step, 0)
+
+        @pl.when(sect == 0)
+        def _():
+            remote(
+                out_st.at[s], xfull.at[s, my_rows], xs_ss.at[s], ownx_sem.at[s], x_dev
+            ).start()
+
+        pltpu.make_async_copy(out_st.at[s], out_hbm.at[s], store_sem.at[4]).start()
+        arrived(rsf_st, rsf_ss.at[0])
+        arrived(norm_st.at[0], store_sem.at[0])
+        arrived(norm_st.at[1], store_sem.at[1])
+        arrived(hid_st, store_sem.at[2])
+        arrived(mixed_st, store_sem.at[3])
+        arrived(out_st.at[s], store_sem.at[4])
+
+    def backward(s):
+        @pl.when(sect == 0)
+        def _():
+            arrived(gfull.at[s, my_rows], owng_sem.at[s])
+            y_send_g(s).start()
+
+        arrived(gfull.at[s, his_rows], yg_r.at[s])
+        pltpu.make_async_copy(gfull.at[s], g_hbm.at[s], store_sem.at[5]).start()
+
+        def mixed_step(k, carry):
+            pair = lax.rem(me // 2 + 1 + k, pairs)
+            at = pl.ds(pl.multiple_of(pair * LANES, LANES), LANES)
+            both = dot_t(gfull[s], wdense[at, :])
+            first = jnp.where(low_half, both[:half], turn(both[half:]))
+            second = jnp.where(low_half, turn(both[:half]), both[half:])
+            do_st[2 * pair] = first.astype(BF16)
+            do_st[2 * pair + 1] = second.astype(BF16)
+            for i in range(2):
+                dest = 2 * pair + i
+                spread(do_st.at[dest], do_r, s, dest, do_ss.at[0], do_rs.at[s])
+            return carry
+
+        lax.fori_loop(0, pairs, mixed_step, 0)
+
+    def backward_ff(s):
+        def ff_step(j, carry):
+            cols = pl.ds(pl.multiple_of(j * COLS, COLS), COLS)
+            grad = dot_t(gfull[s], wdown[cols, :])
+            grad = (grad * slope[s, :, cols].astype(F32)).astype(BF16)
+            dpre_st[:, cols] = grad
+            term = dot_t(grad, wup[:, cols])
+
+            @pl.when(j == 0)
+            def _():
+                dn1[...] = term
+
+            @pl.when(j > 0)
+            def _():
+                dn1[...] += term
+
+            return carry
+
+        lax.fori_loop(0, ff // COLS, ff_step, 0)
+        pltpu.make_async_copy(dpre_st, dpre_hbm.at[s], store_sem.at[6]).start()
+
+    def backward_attention(s):
+        arrived(do_r.at[s], do_rs.at[s])
+        arrived(do_st.at[pl.ds(0, wide - 1)], do_ss.at[0])
+        unpack_heads(s)
+
+        def unpack_step(src, carry):
+            at = pl.multiple_of(src * group, group)
+            grad = do_r[s, src].astype(F32)
+            dox[pl.ds(at, half), :] = jnp.where(low_half, grad, 0.0).astype(BF16)
+            dox[pl.ds(pl.multiple_of(at + half, half), half), :] = jnp.where(
+                low_half, turn(grad), 0.0
+            ).astype(BF16)
+            product = grad * o_st[s, src].astype(F32)
+            left = jnp.sum(jnp.where(low_half, product, 0.0), axis=1, keepdims=True)
+            right = jnp.sum(jnp.where(low_half, 0.0, product), axis=1, keepdims=True)
+            delta[src, :, 0:half] = jnp.broadcast_to(left, (half, LANES)).T[0:8, :]
+            delta[src, :, half:group] = jnp.broadcast_to(right, (half, LANES)).T[0:8, :]
+            return carry
+
+        lax.fori_loop(0, wide, unpack_step, 0)
+        dq[...] = jnp.zeros_like(dq)
+
+        def k_step(j, carry):
+            k_at = pl.ds(pl.multiple_of(j * BLOCK, BLOCK), BLOCK)
+            acc[...] = jnp.zeros_like(acc)
+            peak[...] = jnp.zeros_like(peak)
+
+            def q_step(i, inner):
+                q_at = pl.ds(pl.multiple_of(i * BLOCK, BLOCK), BLOCK)
+                tokens = i * BLOCK + lax.broadcasted_iota(jnp.int32, (8, BLOCK), 1)
+                begin = starts_of(s, tokens)[0:1, :]
+                token = tokens[0:1, :]
+                raw = dot_t(kr[k_at, :], qm[q_at, :])
+                u = j * BLOCK + lax.broadcasted_iota(jnp.int32, (BLOCK, BLOCK), 0)
+                probs = jnp.exp2(raw * SCORE_SCALE - lse[s, i, 0:1, :])
+                probs = jnp.where((u >= begin) & (u <= token), probs, 0.0)
+                probs_grad = dot_t(vx[k_at, :], dox[q_at, :])
+                inner_sum = jnp.concatenate(
+                    [delta[i * sources + k, 0:1, :] for k in range(sources)], axis=1
+                )
+                score_grad = (
+                    probs * (probs_grad - inner_sum) * (1.0 / math.sqrt(HEAD_DIM))
+                ).astype(BF16)
+                acc[...] += dot(probs.astype(BF16), dox[q_at, :])
+                peak[...] += dot(score_grad, qm_turned[q_at, :])
+                dq[q_at, :] += t_dot(score_grad, kr[k_at, :])
+                return inner
+
+            qm_turned = kr
+            lax.fori_loop(j, q_blocks, q_step, 0)
+            for k in range(sources):
+                source = j * sources + k
+                mine = slice(k * group, (k + 1) * group)
+                at = pl.ds(pl.multiple_of(source * group, group), group)
+                both = jnp.where(low_group, dq[at, :], peak[mine, :])
+                value = acc[mine, :]
+                value = jnp.where(low_half, value[:half], turn(value[half:]))
+                dqkv_st[source, 0:group, :] = both.astype(BF16)
+                dqkv_st[source, group:per_source, :] = value.astype(BF16)
+                spread(dqkv_st.at[source], dqkv_r, s, source, dqkv_ss.at[0], dqkv_rs.at[s])
+            return carry
+
+        lax.fori_loop(0, q_blocks, k_step, 0)
+
+    def backward_norm(s):
+        arrived(dqkv_r.at[s], dqkv_rs.at[s])
+        arrived(dqkv_st.at[pl.ds(0, wide - 1)], dqkv_ss.at[0])
+
+        def pair_step(pair, carry):
+            qk0 = rotary(
+                dqkv_r[s, 2 * pair, 0:group, :].astype(F32), cos, front, back, s, -1.0
+            )
+            qk1 = turn(
+                rotary(
+                    dqkv_r[s, 2 * pair + 1, 0:group, :].astype(F32), cos, front, back, s, -1.0
+                )
+            )
+            top, bottom = pair_up(
+                dqkv_r[s, 2 * pair, group:per_source, :].astype(F32),
+                dqkv_r[s, 2 * pair + 1, group:per_source, :].astype(F32),
+                low_half,
+            )
+            vv = jnp.concatenate([top, bottom], axis=0)
+            at = pl.multiple_of(pair * 3 * LANES, LANES)
+            dpk_st[:, pl.ds(at, LANES)] = qk0.astype(BF16)
+            dpk_st[:, pl.ds(pl.multiple_of(at + LANES, LANES), LANES)] = jnp.where(
+                low_group, vv, qk1
+            ).astype(BF16)
+            dpk_st[:, pl.ds(pl.multiple_of(at + 2 * LANES, LANES), LANES)] = jnp.where(
+                low_group, qk1, vv
+            ).astype(BF16)
+            return carry
+
+        lax.fori_loop(0, pairs, pair_step, 0)
+        pltpu.make_async_copy(dpk_st, dpk_hbm.at[s], store_sem.at[7]).start()
+        part[...] = dot_t(dpk_st[...], wqkv[...])
+
+        def fold(values):
+            total = values[0:8]
+            for k in range(1, values.shape[0] // 8):
+                total = total + values[k * 8 : (k + 1) * 8]
+            return total
+
+        def e_step(i, carry):
+            at = pl.ds(pl.multiple_of(i * 32, 32), 32)
+            a, _ = normed_rows(xfull[s, at, :].astype(F32))
+            first = part[at, :]
+            second = dn1[at, :]
+            small[0] += fold(first * a)
+            small[1] += fold(second * a)
+            small[2] += fold(first)
+            small[3] += fold(second)
+            part[at, :] = first * gain[0:1, :] + second * gain[1:2, :]
+            return carry
+
+        lax.fori_loop(0, group // 32, e_step, 0)
+        rsb_st[...] = part[his_rows, :].astype(BF16)
+        remote(rsb_st, rsb_r.at[s], rsb_ss.at[0], rsb_rs.at[s], y_dev).start()
+
+    def backward_end(s):
+        def fold(values):
+            total = values[0:8]
+            for k in range(1, values.shape[0] // 8):
+                total = total + values[k * 8 : (k + 1) * 8]
+            return total
+
+        arrived(rsb_r.at[s], rsb_rs.at[s])
+
+        def in_step(i, carry):
+            at = pl.ds(pl.multiple_of(i * 32, 32), 32)
+            there = pl.ds(pl.multiple_of(tens * rows + i * 32, 32), 32)
+            a, inv = normed_rows(xfull[s, there, :].astype(F32))
+            e = part[there, :] + rsb_r[s, at, :].astype(F32)
+            mean_e = jnp.mean(e, axis=-1, keepdims=True)
+            cross = jnp.mean(e * a, axis=-1, keepdims=True)
+            g_low = gfull[s, there, :].astype(F32)
+            small[4] += fold(g_low)
+            g = jnp.where(sect == 1, cot[s, at, :], g_low)
+            grad = g + inv * (e - mean_e - a * cross)
+            ig_st[at, :] = grad
+            gx_st[s, at, :] = grad.astype(BF16)
+            return carry
+
+        lax.fori_loop(0, rows // 32, in_step, 0)
+
+        @pl.when(sect == 1)
+        def _():
+            remote(
+                gx_st.at[s], gfull.at[s, my_rows], gs_ss.at[s], owng_sem.at[s], x_dev
+            ).start()
+
+        pltpu.make_async_copy(ig_st, ig_hbm.at[s], store_sem.at[8]).start()
+        arrived(rsb_st, rsb_ss.at[0])
+        arrived(gfull.at[s], store_sem.at[5])
+        arrived(dpre_st, store_sem.at[6])
+        arrived(dpk_st, store_sem.at[7])
+        arrived(ig_st, store_sem.at[8])
+
+    def tick(step, carry):
+        f_seq = step - sect
+        b_seq = step - (3 - sect)
+        f_on = (f_seq >= 0) & (f_seq < micro)
+        b_on = (b_seq >= 0) & (b_seq < micro)
+        pl.when(f_on)(lambda: forward(f_seq))
+        pl.when(b_on)(lambda: backward(b_seq))
+        pl.when(f_on)(lambda: forward_ff(f_seq))
+        pl.when(b_on)(lambda: backward_ff(b_seq))
+        pl.when(f_on)(lambda: forward_attention(f_seq))
+        pl.when(b_on)(lambda: backward_attention(b_seq))
+
+        @pl.when(f_on)
+        def _():
+            forward_out(f_seq)
+            forward_end(f_seq)
+
+        @pl.when(b_on)
+        def _():
+            backward_norm(b_seq)
+            backward_end(b_seq)
+
+        return carry
+
+    lax.fori_loop(0, micro + 3, tick, 0)
+
+    for s in range(micro):
+        arrived(xfull.at[s, my_rows], yx_s.at[s])
+        arrived(gfull.at[s, my_rows], yg_s.at[s])
+
+    @pl.when(sect == 0)
+    def _():
+        for s in range(micro):
+            arrived(out_st.at[s], xs_ss.at[s])
+
+    @pl.when(sect == 1)
+    def _():
+        for s in range(micro):
+            arrived(gx_st.at[s], gs_ss.at[s])
+
+
+def rotary_tables(doc_lengths, tokens):
+    ends = jnp.cumsum(doc_lengths, axis=1)
+    starts = ends - doc_lengths
+    inside = (tokens[None, :, None] >= starts[:, None, :]) & (
+        tokens[None, :, None] < ends[:, None, :]
+    )
+    begins = jnp.sum(jnp.where(inside, starts[:, None, :], 0), axis=2)
+    offsets = (tokens[None, :] - begins).astype(F32)
+    part_of = ROT // 2
+    freqs = ROPE_BASE ** (-2.0 * jnp.arange(part_of, dtype=F32) / ROT)
+    angle = offsets[:, :, None] * freqs
+    cos, sin = jnp.cos(angle), jnp.sin(angle)
+    ones = jnp.ones(offsets.shape + (HEAD_DIM - ROT,), F32)
+    zeros = jnp.zeros_like(sin)
+
+    def lanes(parts):
+        return jnp.concatenate(parts + parts, axis=2)
+
+    return (
+        ends.astype(jnp.int32),
+        lanes([cos, cos, ones]),
+        lanes([-sin, zeros, 0.0 * ones]),
+        lanes([zeros, sin, 0.0 * ones]),
+    )
+
+
+def relay(dims, doc_lengths, block_input, cotangent, weights, collective_id):
+    micro, rows, group, wide, heads, d_model, ff = dims
+    (
+        norm_gain,
+        norm_bias,
+        qkv_weight,
+        qkv_bias,
+        dense_weight,
+        dense_bias,
+        up_weight,
+        up_bias,
+        down_weight,
+        down_bias,
+    ) = weights
+    tokens = lax.axis_index("wide") * group + jnp.arange(group, dtype=jnp.int32)
+    ends, cos, front, back = rotary_tables(doc_lengths, tokens)
+    inner = heads * HEAD_DIM
+    per_source = group + group // 2
+    anywhere = pl.BlockSpec(memory_space=pl.ANY)
+    local = pl.BlockSpec(memory_space=pltpu.VMEM)
+    scalars = pl.BlockSpec(memory_space=pltpu.SMEM)
+    dma = pltpu.SemaphoreType.DMA
+    vmem = pltpu.VMEM
+    outs = [
+        jax.ShapeDtypeStruct((micro, rows, d_model), BF16),
+        jax.ShapeDtypeStruct((micro, rows, d_model), F32),
+        jax.ShapeDtypeStruct((2, micro, group, d_model), BF16),
+        jax.ShapeDtypeStruct((micro, group, d_model), BF16),
+        jax.ShapeDtypeStruct((micro, group, inner), BF16),
+        jax.ShapeDtypeStruct((micro, group, ff), BF16),
+        jax.ShapeDtypeStruct((micro, group, ff), BF16),
+        jax.ShapeDtypeStruct((micro, group, 3 * inner), BF16),
+        jax.ShapeDtypeStruct((5, 8, d_model), F32),
+    ]
+    scratch = [
+        vmem(qkv_weight.shape, BF16),
+        vmem(dense_weight.shape, BF16),
+        vmem(up_weight.shape, BF16),
+        vmem(down_weight.shape, BF16),
+        vmem((micro, group, d_model), BF16),
+        vmem((micro, group, d_model), BF16),
+        vmem((micro, rows, d_model), F32),
+        vmem((micro, wide, per_source, LANES), BF16),
+        vmem((micro, wide, group // 2, LANES), BF16),
+        vmem((micro, wide, group // 2, LANES), BF16),
+        vmem((micro, wide, per_source, LANES), BF16),
+        vmem((micro, rows, d_model), BF16),
+        vmem((micro, rows, d_model), BF16),
+        vmem((wide, per_source, LANES), BF16),
+        vmem((micro, wide, group // 2, LANES), BF16),
+        vmem((wide, group // 2, LANES), BF16),
+        vmem((wide, per_source, LANES), BF16),
+        vmem((rows, d_model), BF16),
+        vmem((rows, d_model), BF16),
+        vmem((micro, rows, d_model), BF16),
+        vmem((micro, rows, d_model), BF16),
+        vmem((rows, d_model), F32),
+        vmem((2, group, d_model), BF16),
+        vmem((group, inner), BF16),
+        vmem((group, ff), BF16),
+        vmem((group, ff), BF16),
+        vmem((group, 3 * inner), BF16),
+        vmem((micro, group, ff), BF16),
+        vmem((group, d_model), F32),
+        vmem((group, d_model), F32),
+        vmem((SEQ, LANES), BF16),
+        vmem((SEQ, LANES), BF16),
+        vmem((SEQ, LANES), BF16),
+        vmem((SEQ, LANES), BF16),
+        vmem((SEQ, LANES), F32),
+        vmem((micro, SEQ // BLOCK, 8, BLOCK), F32),
+        vmem((wide, 8, group), F32),
+        vmem((BLOCK, SEQ), F32),
+        vmem((BLOCK, LANES), F32),
+        vmem((BLOCK, LANES), F32),
+        dma((4,)),
+        dma((micro,)),
+        dma((micro,)),
+        dma((micro,)),
+        dma((micro,)),
+        dma((micro,)),
+        dma((micro,)),
+        dma((1,)),
+        dma((micro,)),
+        dma((micro,)),
+        dma((micro,)),
+        dma((1,)),
+        dma((micro,)),
+        dma((1,)),
+        dma((micro,)),
+        dma((1,)),
+        dma((micro,)),
+        dma((1,)),
+        dma((micro,)),
+        dma((micro,)),
+        dma((micro,)),
+        dma((9,)),
+    ]
+    return pl.pallas_call(
+        functools.partial(relay_kernel, dims),
+        out_shape=outs,
+        in_specs=[scalars, anywhere, anywhere]
+        + [local] * 5
+        + [anywhere] * 4
+        + [local] * 3,
+        out_specs=[anywhere] * 8 + [local],
+        scratch_shapes=scratch,
+        compiler_params=pltpu.CompilerParams(
+            collective_id=collective_id, has_side_effects=True, vmem_limit_bytes=63 << 20
+        ),
+        name="relay",
+    )(
+        ends,
+        block_input,
+        cotangent,
+        norm_gain,
+        norm_bias,
+        qkv_bias[None],
+        up_bias[None],
+        (dense_bias + down_bias)[None],
+        qkv_weight,
+        dense_weight,
+        up_weight,
+        down_weight,
+        cos,
+        front,
+        back,
+    )
+
+
+def token_sum(left, right):
+    return lax.dot_general(left, right, (((0,), (0,)), ((), ())), preferred_element_type=F32)
+
+
+def relay_shards(
+    block_input,
+    doc_lengths,
+    norm_gain,
+    norm_bias,
+    qkv_weight,
+    qkv_bias,
+    dense_weight,
+    dense_bias,
+    up_weight,
+    up_bias,
+    down_weight,
+    down_bias,
+    cotangent,
+):
+    weights = tuple(
+        array[0]
+        for array in (
+            norm_gain,
+            norm_bias,
+            qkv_weight,
+            qkv_bias,
+            dense_weight,
+            dense_bias,
+            up_weight,
+            up_bias,
+            down_weight,
+            down_bias,
+        )
+    )
+    micro, rows, d_model = block_input.shape
+    group = rows * lax.axis_size("tensor")
+    wide = lax.axis_size("wide")
+    heads = qkv_weight.shape[2] // (3 * HEAD_DIM)
+    ff = up_weight.shape[2]
+    dims = (micro, rows, group, wide, heads, d_model, ff)
+    out, input_grad, normed, g_low, mixed, hidden, d_pre, d_packed, small = relay(
+        dims, doc_lengths, block_input, cotangent, weights, 1
+    )
+    count = micro * group
+    normed = normed.reshape(2, count, d_model)
+    g_low = g_low.reshape(count, d_model)
+    mixed = mixed.reshape(count, -1)
+    hidden = hidden.reshape(count, -1)
+    d_pre = d_pre.reshape(count, -1)
+    d_packed = d_packed.reshape(count, -1)
+    grads = (
+        token_sum(normed[0], d_packed),
+        token_sum(mixed, g_low),
+        token_sum(normed[1], d_pre),
+        token_sum(hidden, g_low),
+    )
+    qkv_grad, dense_grad, up_grad, down_grad = (
+        lax.psum(grad.astype(BF16), "wide").astype(F32)[None] for grad in grads
+    )
+    biases = jnp.concatenate(
+        [jnp.sum(d_packed.astype(F32), axis=0), jnp.sum(d_pre.astype(F32), axis=0)]
+    )
+    biases = lax.psum(biases, "wide")
+    small = lax.psum(jnp.sum(small, axis=1), ("tensor", "wide"))
+    qkv_width = d_packed.shape[1]
+    return (
+        out[None],
+        input_grad[None],
+        small[0:2][None],
+        small[2:4][None],
+        qkv_grad,
+        biases[:qkv_width][None],
+        dense_grad,
+        small[4][None],
+        up_grad,
+        biases[qkv_width:][None],
+        down_grad,
+        small[4][None],
+    )
 
 
 def shortened(shard):
@@ -324,7 +1218,7 @@
     return (input_grad, terms)
 
 
-def shards(
+def general_shards(
     block_input,
     doc_lengths,
     norm_gain,
@@ -458,23 +1352,28 @@
         P("section", None),
         P(None, ("wide", "tensor"), None),
     )
-    return jax.shard_map(
-        shards,
-        mesh=mesh,
-        in_specs=placed,
-        out_specs=(
-            P("section", None, ("wide", "tensor"), None),
-            P("section", None, ("wide", "tensor"), None),
-            P("section", None, None),
-            P("section", None, None),
-            P("section", None, "tensor"),
-            P("section", "tensor"),
-            P("section", "tensor", None),
-            P("section", None),
-            P("section", None, "tensor"),
-            P("section", "tensor"),
-            P("section", "tensor", None),
-            P("section", None),
-        ),
-        check_vma=False,
-    )
+    results = (
+        P("section", None, ("wide", "tensor"), None),
+        P("section", None, ("wide", "tensor"), None),
+        P("section", None, None),
+        P("section", None, None),
+        P("section", None, "tensor"),
+        P("section", "tensor"),
+        P("section", "tensor", None),
+        P("section", None),
+        P("section", None, "tensor"),
+        P("section", "tensor"),
+        P("section", "tensor", None),
+        P("section", None),
+    )
+
+    def program(*args):
+        heads = args[4].shape[2] // (3 * HEAD_DIM * mesh.shape["tensor"])
+        one_head_each = heads == mesh.shape["wide"] and heads % 2 == 0
+        two_by_two = mesh.shape["section"] == 2 and mesh.shape["tensor"] == 2
+        body = relay_shards if one_head_each and two_by_two else general_shards
+        return jax.shard_map(
+            body, mesh=mesh, in_specs=placed, out_specs=results, check_vma=False
+        )(*args)
+
+    return program

time: 2190 us -> 785 us (0.36)
  matrix products: 844 us -> 24 us
  waiting for transfers between devices: 618 us -> 160 us
  Pallas kernels: 0 us -> 453 us
  other arithmetic: 226 us -> 22.9 us
  blocking collectives: 289 us -> 98.6 us
  local copies, waits for them, and re-layouts: 112 us -> 12.4 us
  loops' own time: 41.1 us -> 0 us
  starting transfers between devices: 25 us -> 0.04 us
    dot_general x105 -> x4, matrix products: 844 us -> 24 us  [token_sum(): lax.dot_general(left, right, (((0,), (0,)), ((), ())), preferred_element_...]
    pallas_call x0 -> x1, Pallas kernels: none -> 453 us  [relay(): pl.pallas_call(functools.partial(relay_kernel, dims), out_shape=outs, in_...]
    all_gather x20 -> x0, waiting for transfers between devices: 293 us -> none  [the longest x10 170 us: gather_keys(): lax.all_gather(key_rows, 'wide', axis=0, tiled=True)]
    all_gather x25 -> x0, blocking collectives: 198 us -> none  [the longest x10 82.7 us: forward_parts(): lax.all_gather(norm_second.astype(jnp.bfloat16), 'tensor', axis=0, tiled=...]
    reduce_sum x75 -> x4, other arithmetic: 119 us -> 3.46 us  [the longest x1 2.83 us: relay_shards(): jnp.sum(d_pre.astype(F32), axis=0)]
    reduce_scatter x25 -> x0, waiting for transfers between devices: 88.6 us -> none  [the longest x5 64 us: forward_parts(): lax.psum_scatter(partial_value.astype(jnp.bfloat16), 'tensor', scatter_di...]
    ppermute x10 -> x0, waiting for transfers between devices: 70.5 us -> none  [from_behind(): return lax.ppermute(block, axis, route)]
    slice x55 -> x4, local copies, waits for them, and re-layouts: 48 us -> 1.05 us  [the longest x1 0.6 us: relay_shards(): biases[qkv_width:][None]]
  transfers between devices with their start and end apart: 56 -> 1, of which waited for: 41 -> 1; matrix products, arithmetic and copies ran while one was open for 34% -> 1% of each run, Pallas kernels for 0% -> 0%
where the time goes in v1:
time: 785 us
  Pallas kernels  453 us (58%)
  waiting for transfers between devices  160 us (20%)
  blocking collectives  98.6 us (13%)
  matrix products  24 us (3%)
  other arithmetic  22.9 us (3%)
  between operations  14.2 us (2%)
  local copies, waits for them, and re-layouts  12.4 us (2%)
    pallas_call x1, Pallas kernels, relay(): pl.pallas_call(functools.partial(relay_kernel, dims), out_shape=outs, in_...  453 us
    psum x1, waiting for transfers between devices, relay_shards(): lax.psum(grad.astype(BF16), 'wide').astype(F32)[None]  160 us
    psum x1, blocking collectives, relay_shards(): small = lax.psum(jnp.sum(small, axis=1), ('tensor', 'wide'))  62.3 us
    psum x1, blocking collectives, relay_shards(): biases = lax.psum(biases, 'wide')  36.3 us
    dot_general x4, matrix products, token_sum(): lax.dot_general(left, right, (((0,), (0,)), ((), ())), preferred_element_...  24 us
  transfers between devices with their start and end apart: 1, of which 1 were waited for; matrix products, arithmetic and copies ran while one was open for 1% of the time, Pallas kernels for 0%

profile of v1, /device:TPU:0, one launch (start us, length us, event | category | flops | bytes accessed | tf_op | source)
XLA Modules:
  0.0 784.9 jit_solution(5801976383370378018)
XLA Ops:
  7.2 0.0 all-reduce.3.cloned.1.call-start
  7.3 0.9 reduce_window_sum.11.ends
  8.1 0.0 copy-start.10
  8.1 0.7 sub.16
  8.8 0.1 select_reduce_fusion
  8.9 1.9 multiply_sine_fusion
  10.9 0.0 copy-start.12
  10.9 0.0 copy-start.13
  10.9 1.7 concatenate.14.back
  12.7 0.0 copy-done.10
  12.7 1.7 concatenate.13.front
  14.4 0.0 copy-done.12
  14.4 0.0 copy-done.13
  14.4 0.6 add.30.out_b
  15.1 1.7 concatenate.12.cos
  16.8 453.1 %relay.1 = (bf16[4,128,1024]{2,1,0:T(8,128)(2,1)}, f32[4,128,1024]{2,1,0:T(8,128)}, bf16[2,4,256,1024]{3,2,1,0:T(8,128)(2,1)}, bf16[4,256,1024]{2,1,0:T(8,128)(2...) custom-call(s32[4,8]{1,0:T(4,128)} %copy-done.10, ...), custom_call_target="tpu_custom_call" | custom-call | tf_op jit(solution)/shard_map/relay/pallas_call | solution.py:798
  469.9 0.0 copy-start.7
  469.9 4.3 fusion.2
  474.2 0.0 copy-done.7
  474.2 0.0 copy-start.3
  474.2 8.5 %fusion = bf16[1,2048,1024]{2,1,0:T(8,128)(2,1)} fusion(bf16[4,256,2048]{2,1,0:T(8,128)(2,1)} %get-tuple-element.29, bf16[4,256,1024]{2,1,0:T(8,128)(2,1)S(1)} %copy-done.7), kind=kOutput, calls=%fused_computation.5 | convolution fusion | flops 4297064448 | bytes 10485760 | tf_op jit(solution)/shard_map/dot_general | solution.py:831
  482.7 0.0 copy-done.3
  482.7 0.0 copy-start.2
  482.7 0.4 fusion.4
  483.1 1.7 copy-done.2
  484.9 0.0 copy-start.4
  484.9 6.2 convert_bitcast_fusion
  491.1 0.0 copy-done.4
  491.1 5.0 fusion.1
  496.1 0.0 all-reduce.3.cloned.1.call-update
  496.1 0.0 copy-start.9
  496.1 0.5 convert_reduce_fusion.1
  496.6 2.8 convert_reduce_fusion
  499.4 36.3 %psum.44 = f32[3584]{0:T(1024)S(1)} all-reduce(f32[3584]{0:T(1024)S(1)} %pad_maximum_fusion), channel_id=1, replica_groups=mesh['section'=2,'tensor'=2,'wide'=8] {'wide'}, use_global_device_ids=true, to_apply=%region_7.8 | all-reduce | flops 3584 | bytes 28672 | tf_op jit(solution)/shard_map/psum | solution.py:892
  535.7 0.6 slice.35
  536.3 0.6 broadcast_in_dim.76
  536.9 0.0 copy-done.9
  537.0 62.3 %psum.42 = f32[5,1024]{1,0:T(8,128)S(1)} all-reduce(f32[5,1024]{1,0:T(8,128)S(1)} %reduce_sum.37), channel_id=1, replica_groups=mesh['section'=2,'tensor'=2,'wide'=8] {'tensor','wide'}, use_global_device_ids=true, to_apply=%region_3.4 | all-reduce | flops 5120 | bytes 40960 | tf_op jit(solution)/shard_map/psum | solution.py:893
  599.3 0.0 copy-start.11
  599.3 0.6 slice_bitcast_fusion
  599.9 159.8 %all-reduce.3.cloned.1.call-done = (bf16[1,1024,1536]{2,1,0:T(8,128)(2,1)}, bf16[1,512,1024]{2,1,0:T(8,128)(2,1)}, bf16[1,1024,2048]{2,1,0:T(8,128)(2,1)}, bf16[1,2048,1024]{2,1,0:T(8,128)(2,1)}) async-done(((bf16[1,1024,1536]{2,1,0:T(8,128)(2,1)}, bf16[1,512,1024]{2,1,0:T(8,128)(2,1)}, bf16[1,1024,2048]{2,1,0:T(8,128)(2,1)}, bf16[1,2048,1024]{2,1,0:T(8,128)(2,1)}), (bf16[1,1024,1536]{2,1,0:T(8,128)(2,1)}, ...) | async-done | bytes 12582928 | tf_op jit(solution)/shard_map/psum | solution.py:887
  759.7 0.0 copy-start.5
  759.7 2.9 broadcast_in_dim.78
  762.6 0.0 copy-done.5
  762.6 0.0 copy-start.1
  762.6 3.6 broadcast_in_dim.75
  766.2 0.0 copy-done.1
  766.2 0.0 copy-start
  766.2 4.4 broadcast_in_dim.80
  770.6 0.0 copy-done
  770.6 0.0 copy-start.8
  770.6 4.4 broadcast_in_dim.83
  775.1 0.0 copy-start.6
  775.1 0.0 copy-done.11
  775.1 0.6 copy.38
  775.7 0.0 copy-done.8
  775.7 1.0 copy.39
  776.6 0.1 copy-done.6
  776.7 1.3 copy.40
  (10 shorter events, 0.2 us)
Async XLA Ops:
  7.2 752.5 %all-reduce.3.cloned.1.call-start = ((), (), s32[]{:S(2)}) async-start(), calls=%async_computation | async-start | bytes 25165824 | tf_op jit(solution)/shard_map/psum | solution.py:887
  8.1 4.6 copy-start.10
  10.9 3.5 copy-start.12
  10.9 3.5 copy-start.13
  469.9 4.3 copy-start.7
  474.2 8.5 %copy-start.3 = (bf16[2,4,256,1024]{3,2,1,0:T(8,128)(2,1)S(1)}, bf16[2,4,256,1024]{3,2,1,0:T(8,128)(2,1)}, u32[]{:S(2)}) copy-start(bf16[2,4,256,1024]{3,2,1,0:T(8,128)(2,1)} %get-tuple-element.24) | copy-start | bytes 12582916
  482.7 2.2 copy-start.2
  484.9 6.2 copy-start.4
  496.1 40.8 %copy-start.9 = (f32[5,8,1024]{2,1,0:T(8,128)S(1)}, f32[5,8,1024]{2,1,0:T(8,128)}, u32[]{:S(2)}) copy-start(f32[5,8,1024]{2,1,0:T(8,128)} %get-tuple-element.23) | copy-start | bytes 491524
  599.3 175.8 %copy-start.11 = (f32[1,1024]{1,0:T(1,128)}, f32[1,1024]{1,0:T(1,128)S(1)}, u32[]{:S(2)}) copy-start(f32[1,1024]{1,0:T(1,128)S(1)} %slice.34) | copy-start | bytes 12292
  759.7 2.9 copy-start.5
  762.6 3.6 copy-start.1
  766.2 4.5 copy-start
  770.6 5.0 copy-start.8
  775.1 1.6 copy-start.6
Sparse Core Ops, SparseCore 0:
  496.2 263.3 all-reduce.2

commit v2 on v1

--- a/solution.py
+++ b/solution.py
@@ -54,11 +54,7 @@
 
 
 def pair_up(first, second, low):
-    half = first.shape[0]
-    top = jnp.where(low, first, turn(second))
-    bottom = jnp.where(low, turn(first), second)
-    del half
-    return top, bottom
+    return jnp.where(low, first, turn(second)), jnp.where(low, turn(first), second)
 
 
 def relay_kernel(
@@ -87,6 +83,7 @@
     dpre_hbm,
     dpk_hbm,
     small,
+    bias_sums,
     wqkv,
     wdense,
     wup,
@@ -174,6 +171,9 @@
     def arrived(ref, sem):
         pltpu.make_async_copy(ref, ref, sem).wait()
 
+    def tokens_of(s):
+        return pl.ds(pl.multiple_of(s * group, group), group)
+
     def y_send_x(s):
         own = xfull.at[s, my_rows]
         return remote(own, own, yx_s.at[s], yx_r.at[s], y_dev)
@@ -216,6 +216,7 @@
             pltpu.make_async_copy(cot_hbm.at[s], cot.at[s], owng_sem.at[s]).start()
 
     small[...] = jnp.zeros_like(small)
+    bias_sums[...] = jnp.zeros_like(bias_sums)
     pl.semaphore_wait(barrier, wide + 1)
 
     @pl.when(sect == 0)
@@ -240,6 +241,12 @@
 
     for load in loads:
         load.wait()
+
+    def fold(values):
+        total = values[0:8]
+        for k in range(1, values.shape[0] // 8):
+            total = total + values[k * 8 : (k + 1) * 8]
+        return total
 
     def normed_rows(values):
         center = jnp.mean(values, axis=-1, keepdims=True)
@@ -289,8 +296,8 @@
             return carry
 
         lax.fori_loop(0, group // 32, norm_step, 0)
-        pltpu.make_async_copy(norm_st.at[0], norm_hbm.at[0, s], store_sem.at[0]).start()
-        pltpu.make_async_copy(norm_st.at[1], norm_hbm.at[1, s], store_sem.at[1]).start()
+        pltpu.make_async_copy(norm_st.at[0], norm_hbm.at[0, tokens_of(s)], store_sem.at[0]).start()
+        pltpu.make_async_copy(norm_st.at[1], norm_hbm.at[1, tokens_of(s)], store_sem.at[1]).start()
 
         def qkv_step(k, carry):
             pair = lax.rem(me // 2 + 1 + k, pairs)
@@ -336,7 +343,7 @@
             return carry
 
         lax.fori_loop(0, ff // COLS, ff_step, 0)
-        pltpu.make_async_copy(hid_st, hid_hbm.at[s], store_sem.at[2]).start()
+        pltpu.make_async_copy(hid_st, hid_hbm.at[tokens_of(s)], store_sem.at[2]).start()
 
     def forward_attention(s):
         arrived(qkv_r.at[s], qkv_rs.at[s])
@@ -396,7 +403,7 @@
             )
             mixed_st[0:half, pair * LANES : (pair + 1) * LANES] = top.astype(BF16)
             mixed_st[half:group, pair * LANES : (pair + 1) * LANES] = bottom.astype(BF16)
-        pltpu.make_async_copy(mixed_st, mixed_hbm.at[s], store_sem.at[3]).start()
+        pltpu.make_async_copy(mixed_st, mixed_hbm.at[tokens_of(s)], store_sem.at[3]).start()
         part[...] += dot(mixed_st[...], wdense[...])
         rsf_st[...] = part[his_rows, :].astype(BF16)
         remote(rsf_st, rsf_r.at[s], rsf_ss.at[0], rsf_rs.at[s], y_dev).start()
@@ -434,7 +441,7 @@
             y_send_g(s).start()
 
         arrived(gfull.at[s, his_rows], yg_r.at[s])
-        pltpu.make_async_copy(gfull.at[s], g_hbm.at[s], store_sem.at[5]).start()
+        pltpu.make_async_copy(gfull.at[s], g_hbm.at[tokens_of(s)], store_sem.at[5]).start()
 
         def mixed_step(k, carry):
             pair = lax.rem(me // 2 + 1 + k, pairs)
@@ -457,6 +464,8 @@
             grad = dot_t(gfull[s], wdown[cols, :])
             grad = (grad * slope[s, :, cols].astype(F32)).astype(BF16)
             dpre_st[:, cols] = grad
+            sums_at = pl.ds(pl.multiple_of(3 * heads * HEAD_DIM + j * COLS, COLS), COLS)
+            bias_sums[:, sums_at] += fold(grad.astype(F32))
             term = dot_t(grad, wup[:, cols])
 
             @pl.when(j == 0)
@@ -470,7 +479,7 @@
             return carry
 
         lax.fori_loop(0, ff // COLS, ff_step, 0)
-        pltpu.make_async_copy(dpre_st, dpre_hbm.at[s], store_sem.at[6]).start()
+        pltpu.make_async_copy(dpre_st, dpre_hbm.at[tokens_of(s)], store_sem.at[6]).start()
 
     def backward_attention(s):
         arrived(do_r.at[s], do_rs.at[s])
@@ -555,25 +564,17 @@
                 low_half,
             )
             vv = jnp.concatenate([top, bottom], axis=0)
-            at = pl.multiple_of(pair * 3 * LANES, LANES)
-            dpk_st[:, pl.ds(at, LANES)] = qk0.astype(BF16)
-            dpk_st[:, pl.ds(pl.multiple_of(at + LANES, LANES), LANES)] = jnp.where(
-                low_group, vv, qk1
-            ).astype(BF16)
-            dpk_st[:, pl.ds(pl.multiple_of(at + 2 * LANES, LANES), LANES)] = jnp.where(
-                low_group, qk1, vv
-            ).astype(BF16)
+            columns = (qk0, jnp.where(low_group, vv, qk1), jnp.where(low_group, qk1, vv))
+            for k, column in enumerate(columns):
+                at = pl.ds(pl.multiple_of((pair * 3 + k) * LANES, LANES), LANES)
+                column = column.astype(BF16)
+                dpk_st[:, at] = column
+                bias_sums[:, at] += fold(column.astype(F32))
             return carry
 
         lax.fori_loop(0, pairs, pair_step, 0)
-        pltpu.make_async_copy(dpk_st, dpk_hbm.at[s], store_sem.at[7]).start()
+        pltpu.make_async_copy(dpk_st, dpk_hbm.at[tokens_of(s)], store_sem.at[7]).start()
         part[...] = dot_t(dpk_st[...], wqkv[...])
-
-        def fold(values):
-            total = values[0:8]
-            for k in range(1, values.shape[0] // 8):
-                total = total + values[k * 8 : (k + 1) * 8]
-            return total
 
         def e_step(i, carry):
             at = pl.ds(pl.multiple_of(i * 32, 32), 32)
@@ -592,12 +593,6 @@
         remote(rsb_st, rsb_r.at[s], rsb_ss.at[0], rsb_rs.at[s], y_dev).start()
 
     def backward_end(s):
-        def fold(values):
-            total = values[0:8]
-            for k in range(1, values.shape[0] // 8):
-                total = total + values[k * 8 : (k + 1) * 8]
-            return total
-
         arrived(rsb_r.at[s], rsb_rs.at[s])
 
         def in_step(i, carry):
@@ -723,13 +718,14 @@
     outs = [
         jax.ShapeDtypeStruct((micro, rows, d_model), BF16),
         jax.ShapeDtypeStruct((micro, rows, d_model), F32),
-        jax.ShapeDtypeStruct((2, micro, group, d_model), BF16),
-        jax.ShapeDtypeStruct((micro, group, d_model), BF16),
-        jax.ShapeDtypeStruct((micro, group, inner), BF16),
-        jax.ShapeDtypeStruct((micro, group, ff), BF16),
-        jax.ShapeDtypeStruct((micro, group, ff), BF16),
-        jax.ShapeDtypeStruct((micro, group, 3 * inner), BF16),
+        jax.ShapeDtypeStruct((2, micro * group, d_model), BF16),
+        jax.ShapeDtypeStruct((micro * group, d_model), BF16),
+        jax.ShapeDtypeStruct((micro * group, inner), BF16),
+        jax.ShapeDtypeStruct((micro * group, ff), BF16),
+        jax.ShapeDtypeStruct((micro * group, ff), BF16),
+        jax.ShapeDtypeStruct((micro * group, 3 * inner), BF16),
         jax.ShapeDtypeStruct((5, 8, d_model), F32),
+        jax.ShapeDtypeStruct((8, 3 * inner + ff), F32),
     ]
     scratch = [
         vmem(qkv_weight.shape, BF16),
@@ -802,7 +798,7 @@
         + [local] * 5
         + [anywhere] * 4
         + [local] * 3,
-        out_specs=[anywhere] * 8 + [local],
+        out_specs=[anywhere] * 8 + [local] * 2,
         scratch_shapes=scratch,
         compiler_params=pltpu.CompilerParams(
             collective_id=collective_id, has_side_effects=True, vmem_limit_bytes=63 << 20
@@ -827,8 +823,387 @@
     )
 
 
-def token_sum(left, right):
-    return lax.dot_general(left, right, (((0,), (0,)), ((), ())), preferred_element_type=F32)
+TILE = 256
+RING = 8
+TOTALS = 4
+
+
+def gradient_kinds(d_model, inner, ff):
+    return ((d_model, ff), (ff, d_model), (inner, d_model), (d_model, 3 * inner))
+
+
+def gradient_kernel(
+    dims,
+    norm_hbm,
+    g_hbm,
+    mixed_hbm,
+    hid_hbm,
+    dpre_hbm,
+    dpk_hbm,
+    small,
+    biases,
+    up_out,
+    down_out,
+    dense_out,
+    qkv_out,
+    sums,
+    left_op,
+    right_op,
+    own,
+    core_r,
+    outer_r,
+    inner_r,
+    core_st,
+    red_st,
+    tot,
+    sums_r,
+    op_sem,
+    core_ss,
+    core_rs,
+    outer_rs,
+    inner_rs,
+    red_ss,
+    bc_rs,
+    tot_ss,
+    fwd_ss,
+    share_ss,
+    fin_rs,
+    sum_ss,
+    sum_rs,
+    core_free,
+    outer_free,
+    inner_free,
+):
+    micro, rows, group, wide, heads, d_model, ff = dims
+    tens = lax.axis_index("tensor")
+    me = lax.axis_index("wide")
+    chip, core = me // 2, lax.rem(me, 2)
+    partner = {"wide": me + 1 - 2 * core}
+    up_dev = {"wide": lax.rem(me + 2, wide)}
+    down_dev = {"wide": lax.rem(me + wide - 2, wide)}
+    at_bottom, at_top = chip == 0, chip == wide // 2 - 1
+    at_end = at_bottom | at_top
+    middle = jnp.logical_not(at_end)
+    lower = chip == 1
+    outer_of = {"wide": jnp.where(lower, me - 2, lax.rem(me + 2, wide))}
+    inner_of = {"wide": jnp.where(lower, me + 2, lax.rem(me + wide - 2, wide))}
+    end_of = {"wide": jnp.where(at_bottom, me + 2, lax.rem(me + wide - 2, wide))}
+    inner = heads * HEAD_DIM
+    kinds = gradient_kinds(d_model, inner, ff)
+    targets = (up_out, down_out, dense_out, qkv_out)
+    operands = (
+        (norm_hbm.at[1], dpre_hbm),
+        (hid_hbm, g_hbm),
+        (mixed_hbm, g_hbm),
+        (norm_hbm.at[0], dpk_hbm),
+    )
+    ranges, first = [], 0
+    for height, width in kinds:
+        count = (height // TILE) * (width // (2 * TILE))
+        ranges.append((first, first + count, width // (2 * TILE)))
+        first += count
+    steps = first
+
+    def remote(src, dst, ss, rs, dev):
+        return pltpu.make_async_remote_copy(
+            src_ref=src, dst_ref=dst, send_sem=ss, recv_sem=rs, device_id=dev, device_id_type=MESH
+        )
+
+    def arrived(ref, sem):
+        pltpu.make_async_copy(ref, ref, sem).wait()
+
+    tile_ref = tot.at[0]
+
+    def by_kind(m, body):
+        for kind, (low, high, across) in enumerate(ranges):
+
+            @pl.when((m >= low) & (m < high))
+            def _(kind=kind, low=low, across=across):
+                at = m - low
+                body(kind, at // across, lax.rem(at, across))
+
+    def tile_of(kind, row, col, which):
+        return targets[kind].at[
+            pl.ds(pl.multiple_of(row * TILE, TILE), TILE),
+            pl.ds(pl.multiple_of((2 * col + which) * TILE, TILE), TILE),
+        ]
+
+    def fetch(m):
+        def body(kind, row, col):
+            left, right = operands[kind]
+            slot = lax.rem(m, 2)
+            pltpu.make_async_copy(
+                left.at[:, pl.ds(pl.multiple_of(row * TILE, TILE), TILE)],
+                left_op.at[slot],
+                op_sem.at[0, slot],
+            ).start()
+            pltpu.make_async_copy(
+                right.at[:, pl.ds(pl.multiple_of(col * 2 * TILE, 2 * TILE), 2 * TILE)],
+                right_op.at[slot],
+                op_sem.at[1, slot],
+            ).start()
+
+        by_kind(m, body)
+
+    def is_root(m):
+        return middle & (chip == 1 + lax.rem(m, 2))
+
+    def products(m):
+        slot, ring = lax.rem(m, 2), lax.rem(m, RING)
+        arrived(left_op.at[slot], op_sem.at[0, slot])
+        arrived(right_op.at[slot], op_sem.at[1, slot])
+        left = left_op[slot]
+        mine = pl.ds(pl.multiple_of(core * TILE, TILE), TILE)
+        other = pl.ds(pl.multiple_of((1 - core) * TILE, TILE), TILE)
+
+        @pl.when(m >= RING)
+        def _():
+            arrived(tile_ref, core_ss.at[ring])
+            pl.semaphore_wait(core_free, 1)
+
+        core_st[ring] = t_dot(left, right_op[slot, :, other]).astype(BF16)
+        remote(
+            core_st.at[ring], core_r.at[ring], core_ss.at[ring], core_rs.at[ring], partner
+        ).start()
+        own[ring] = t_dot(left, right_op[slot, :, mine])
+
+    def send_red(m, value, target, sem, dev, free):
+        ring = lax.rem(m, RING)
+
+        @pl.when(m >= RING)
+        def _():
+            pl.semaphore_wait(free, 1)
+
+        red_st[ring] = value.astype(BF16)
+        remote(red_st.at[ring], target.at[ring], red_ss.at[ring], sem.at[ring], dev).start()
+
+    def chip_sum(m):
+        ring = lax.rem(m, RING)
+        arrived(tile_ref, core_rs.at[ring])
+        total = own[ring] + core_r[ring].astype(F32)
+
+        @pl.when(m + RING < steps)
+        def _():
+            pl.semaphore_signal(core_free, inc=1, device_id=partner, device_id_type=MESH)
+
+        @pl.when(at_end)
+        def _():
+            @pl.when(m >= RING)
+            def _():
+                arrived(tile_ref, red_ss.at[ring])
+
+            send_red(m, total, outer_r, outer_rs, end_of, outer_free.at[lax.rem(m, 2)])
+
+        @pl.when(middle)
+        def _():
+            own[ring] = total
+
+    def take_outer(m):
+        ring = lax.rem(m, RING)
+        arrived(tile_ref, outer_rs.at[ring])
+        total = own[ring] + outer_r[ring].astype(F32)
+
+        @pl.when(m + RING < steps)
+        def _():
+            pl.semaphore_signal(
+                outer_free.at[lax.rem(m, 2)], inc=1, device_id=outer_of, device_id_type=MESH
+            )
+
+        return total
+
+    def pass_in(m):
+        ring = lax.rem(m, RING)
+        total = take_outer(m)
+
+        @pl.when(m >= RING)
+        def _():
+            arrived(tile_ref, red_ss.at[ring])
+
+        send_red(m, total, inner_r, inner_rs, inner_of, inner_free)
+
+    def finish(m):
+        ring = lax.rem(m, RING)
+        slot = lax.rem(m // 2, TOTALS)
+        total = take_outer(m)
+        arrived(tile_ref, inner_rs.at[ring])
+        total = total + inner_r[ring].astype(F32)
+
+        @pl.when(m + RING < steps)
+        def _():
+            pl.semaphore_signal(inner_free, inc=1, device_id=inner_of, device_id_type=MESH)
+
+        @pl.when(m >= 2 * TOTALS)
+        def _():
+            for k in range(4):
+                arrived(tile_ref, tot_ss.at[k, slot])
+
+        tot[slot] = total.astype(BF16)
+
+        def body(kind, row, col):
+            here = tile_of(kind, row, col, core)
+            remote(tot.at[slot], here, tot_ss.at[0, slot], bc_rs.at[m], outer_of).start()
+            remote(tot.at[slot], here, tot_ss.at[1, slot], bc_rs.at[m], inner_of).start()
+            remote(tot.at[slot], here, tot_ss.at[2, slot], fin_rs.at[kind], partner).start()
+            pltpu.make_async_copy(tot.at[slot], here, tot_ss.at[3, slot]).start()
+
+        by_kind(m, body)
+
+    def hand_on(m):
+        arrived(tile_ref, bc_rs.at[m])
+
+        def body(kind, row, col):
+            here = tile_of(kind, row, col, core)
+
+            @pl.when(middle)
+            def _():
+                remote(here, here, fwd_ss.at[m], bc_rs.at[m], outer_of).start()
+
+            remote(here, here, share_ss.at[m], fin_rs.at[kind], partner).start()
+
+        by_kind(m, body)
+
+    exchanges = (
+        {"tensor": 1 - tens},
+        partner,
+        {"wide": me + 2 - 4 * lax.rem(chip, 2)},
+        {"wide": me + 4 - 8 * (chip // 2)},
+    )
+
+    barrier = pltpu.get_barrier_semaphore()
+    for dev in exchanges:
+        pl.semaphore_signal(barrier, inc=1, device_id=dev, device_id_type=MESH)
+
+    @pl.when(middle)
+    def _():
+        pl.semaphore_signal(barrier, inc=1, device_id=inner_of, device_id_type=MESH)
+
+    fetch(jnp.int32(0))
+    sums[:, 0:d_model] = jnp.concatenate(
+        [jnp.sum(small[k], axis=0, keepdims=True) for k in range(5)]
+        + [jnp.zeros((3, d_model), F32)],
+        axis=0,
+    )
+    total = jnp.sum(biases[...], axis=0, keepdims=True)
+    lines = [total[:, k * COLS : (k + 1) * COLS] for k in range(total.shape[1] // COLS)]
+    lines.append(jnp.zeros((8 - len(lines), COLS), F32))
+    sums[:, d_model:] = jnp.concatenate(lines, axis=0)
+    pl.when(middle)(lambda: pl.semaphore_wait(barrier, len(exchanges) + 1))
+    pl.when(at_end)(lambda: pl.semaphore_wait(barrier, len(exchanges)))
+
+    def exchange_start(k):
+        if k > 0:
+            arrived(sums, sum_ss.at[0])
+        sums_r[0] = sums[...]
+        remote(sums_r.at[0], sums_r.at[k + 1], sum_ss.at[0], sum_rs.at[k], exchanges[k]).start()
+
+    def exchange_end(k):
+        arrived(sums, sum_rs.at[k])
+        if k == 0:
+            sums[:, 0:d_model] += sums_r[1, :, 0:d_model]
+        else:
+            sums[...] += sums_r[k + 1]
+
+    def step(i, carry):
+        pl.when(i + 1 < steps)(lambda: fetch(i + 1))
+        pl.when(i < steps)(lambda: products(i))
+        for k in range(4):
+            pl.when(i == 4 * k + 2)(lambda k=k: exchange_start(k))
+            pl.when(i == 4 * k + 5)(lambda k=k: exchange_end(k))
+
+        def at(lag, allowed, body):
+            m = i - lag
+            pl.when((m >= 0) & (m < steps) & allowed(m))(lambda: body(m))
+
+        at(1, lambda m: m >= 0, chip_sum)
+        at(3, lambda m: middle & jnp.logical_not(is_root(m)), pass_in)
+        at(5, is_root, finish)
+        at(8, lambda m: middle & jnp.logical_not(is_root(m)), hand_on)
+        at(10, lambda m: at_end, hand_on)
+        return carry
+
+    lax.fori_loop(0, steps + 10, step, 0)
+
+    arrived(sums, sum_ss.at[0])
+    for ring in range(RING):
+        arrived(tile_ref, core_ss.at[ring])
+
+    def drain(m, carry):
+        ring = lax.rem(m, RING)
+        root = is_root(m)
+        last = m + RING >= steps
+        pl.when(at_end & last)(lambda: arrived(tile_ref, red_ss.at[ring]))
+        pl.when(middle & jnp.logical_not(root) & last)(
+            lambda: arrived(tile_ref, red_ss.at[ring])
+        )
+
+        @pl.when(root & (m + 2 * TOTALS >= steps))
+        def _():
+            for k in range(4):
+                arrived(tile_ref, tot_ss.at[k, lax.rem(m // 2, TOTALS)])
+
+        @pl.when(middle & jnp.logical_not(root))
+        def _():
+            arrived(tile_ref, fwd_ss.at[m])
+
+        pl.when(jnp.logical_not(root))(lambda: arrived(tile_ref, share_ss.at[m]))
+        return carry
+
+    lax.fori_loop(0, steps, drain, 0)
+    for kind, (height, width) in enumerate(kinds):
+        arrived(targets[kind].at[pl.ds(0, height // 2)], fin_rs.at[kind])
+
+
+def gradient_sums(dims, operands, small, biases, collective_id):
+    micro, rows, group, wide, heads, d_model, ff = dims
+    inner = heads * HEAD_DIM
+    kinds = gradient_kinds(d_model, inner, ff)
+    steps = sum((height // TILE) * (width // (2 * TILE)) for height, width in kinds)
+    count = micro * group
+    anywhere = pl.BlockSpec(memory_space=pl.ANY)
+    local = pl.BlockSpec(memory_space=pltpu.VMEM)
+    dma = pltpu.SemaphoreType.DMA
+    regular = pltpu.SemaphoreType.REGULAR
+    vmem = pltpu.VMEM
+    width = d_model + COLS
+    return pl.pallas_call(
+        functools.partial(gradient_kernel, dims),
+        out_shape=[jax.ShapeDtypeStruct(kind, BF16) for kind in kinds]
+        + [jax.ShapeDtypeStruct((8, width), F32)],
+        in_specs=[anywhere] * 6 + [local] * 2,
+        out_specs=[anywhere] * 4 + [local],
+        scratch_shapes=[
+            vmem((2, count, TILE), BF16),
+            vmem((2, count, 2 * TILE), BF16),
+            vmem((RING, TILE, TILE), F32),
+            vmem((RING, TILE, TILE), BF16),
+            vmem((RING, TILE, TILE), BF16),
+            vmem((RING, TILE, TILE), BF16),
+            vmem((RING, TILE, TILE), BF16),
+            vmem((RING, TILE, TILE), BF16),
+            vmem((TOTALS, TILE, TILE), BF16),
+            vmem((5, 8, width), F32),
+            dma((2, 2)),
+            dma((RING,)),
+            dma((RING,)),
+            dma((RING,)),
+            dma((RING,)),
+            dma((RING,)),
+            dma((steps,)),
+            dma((4, TOTALS)),
+            dma((steps,)),
+            dma((steps,)),
+            dma((4,)),
+            dma((1,)),
+            dma((4,)),
+            regular,
+            regular((2,)),
+            regular,
+        ],
+        compiler_params=pltpu.CompilerParams(
+            collective_id=collective_id, has_side_effects=True, vmem_limit_bytes=40 << 20
+        ),
+        name="gradient_sums",
+    )(*operands, small, biases)
 
 
 def relay_shards(
@@ -867,44 +1242,31 @@
     heads = qkv_weight.shape[2] // (3 * HEAD_DIM)
     ff = up_weight.shape[2]
     dims = (micro, rows, group, wide, heads, d_model, ff)
-    out, input_grad, normed, g_low, mixed, hidden, d_pre, d_packed, small = relay(
+    out, input_grad, *operands, small, bias_sums = relay(
         dims, doc_lengths, block_input, cotangent, weights, 1
     )
-    count = micro * group
-    normed = normed.reshape(2, count, d_model)
-    g_low = g_low.reshape(count, d_model)
-    mixed = mixed.reshape(count, -1)
-    hidden = hidden.reshape(count, -1)
-    d_pre = d_pre.reshape(count, -1)
-    d_packed = d_packed.reshape(count, -1)
-    grads = (
-        token_sum(normed[0], d_packed),
-        token_sum(mixed, g_low),
-        token_sum(normed[1], d_pre),
-        token_sum(hidden, g_low),
-    )
-    qkv_grad, dense_grad, up_grad, down_grad = (
-        lax.psum(grad.astype(BF16), "wide").astype(F32)[None] for grad in grads
-    )
-    biases = jnp.concatenate(
-        [jnp.sum(d_packed.astype(F32), axis=0), jnp.sum(d_pre.astype(F32), axis=0)]
-    )
-    biases = lax.psum(biases, "wide")
-    small = lax.psum(jnp.sum(small, axis=1), ("tensor", "wide"))
-    qkv_width = d_packed.shape[1]
+    up_grad, down_grad, dense_grad, qkv_grad, sums = gradient_sums(
+        dims, operands, small, bias_sums, 2
+    )
+    up_grad, down_grad, dense_grad, qkv_grad = (
+        grad.astype(F32)[None] for grad in (up_grad, down_grad, dense_grad, qkv_grad)
+    )
+    biases = sums[:, d_model:].reshape(1, -1)
+    qkv_width = qkv_weight.shape[2]
+    out_bias_grad = sums[4:5, :d_model]
     return (
         out[None],
         input_grad[None],
-        small[0:2][None],
-        small[2:4][None],
+        sums[None, 0:2, :d_model],
+        sums[None, 2:4, :d_model],
         qkv_grad,
-        biases[:qkv_width][None],
+        biases[:, :qkv_width],
         dense_grad,
-        small[4][None],
+        out_bias_grad,
         up_grad,
-        biases[qkv_width:][None],
+        biases[:, qkv_width : qkv_width + ff],
         down_grad,
-        small[4][None],
+        out_bias_grad,
     )
 
 

time: 785 us -> 657 us (0.84)
  Pallas kernels: 453 us -> 620 us
  waiting for transfers between devices: 160 us -> 0 us
  blocking collectives: 98.6 us -> 0 us
  matrix products: 24 us -> 0 us
  between operations: 14.2 us -> 0.76 us
    pallas_call x0 -> x1, Pallas kernels: none -> 169 us  [gradient_sums(): pl.pallas_call(functools.partial(gradient_kernel, dims), out_shape=[jax.S...]
    psum x1 -> x0, waiting for transfers between devices: 160 us -> none  [relay_shards(): lax.psum(grad.astype(BF16), 'wide').astype(F32)[None]]
    psum x2 -> x0, blocking collectives: 98.6 us -> none  [the longest x1 62.3 us: relay_shards(): small = lax.psum(jnp.sum(small, axis=1), ('tensor', 'wide'))]
    dot_general x4 -> x0, matrix products: 24 us -> none  [token_sum(): lax.dot_general(left, right, (((0,), (0,)), ((), ())), preferred_element_...]
  transfers between devices with their start and end apart: 1 -> 0, of which waited for: 1 -> 0; matrix products, arithmetic and copies ran while one was open for 1% -> 0% of each run, Pallas kernels for 0% -> 0%
where the time goes in v2:
time: 657 us; the launch traced here: 656 us
  Pallas kernels  620 us (94%)
  other arithmetic  18.9 us (3%)
  local copies, waits for them, and re-layouts  16.6 us (3%)
    pallas_call x1, Pallas kernels, relay(): pl.pallas_call(functools.partial(relay_kernel, dims), out_shape=outs, in_...  451 us
    pallas_call x1, Pallas kernels, gradient_sums(): pl.pallas_call(functools.partial(gradient_kernel, dims), out_shape=[jax.S...  169 us
    broadcast_in_dim x4, other arithmetic, relay_shards(): grad.astype(F32)[None]  14 us

profile of v2, /device:TPU:0, one launch (start us, length us, event | category | flops | bytes accessed | tf_op | source)
XLA Modules:
  0.0 656.3 jit_solution(6473057986726801440)
XLA Ops:
  0.7 0.9 reduce_window_sum.11.ends
  1.5 0.0 copy-start.9
  1.5 0.7 sub.16
  2.2 0.1 select_reduce_fusion
  2.3 1.3 add.18.out_b
  3.6 1.9 multiply_sine_fusion
  5.6 1.7 concatenate.9.cos
  7.4 1.7 concatenate.11.back
  9.2 0.0 copy-done.9
  9.2 1.7 concatenate.10.front
  10.9 451.5 %relay.1 = (bf16[4,128,1024]{2,1,0:T(8,128)(2,1)}, f32[4,128,1024]{2,1,0:T(8,128)}, bf16[2,1024,1024]{2,1,0:T(8,128)(2,1)}, bf16[1024,1024]{1,0:T(8,128)(2,1)}, ...) custom-call(s32[4,8]{1,0:T(4,128)} %copy-done.9, ...), custom_call_target="tpu_custom_call" | custom-call | tf_op jit(solution)/shard_map/relay/pallas_call | solution.py:794
  462.4 0.0 copy-start
  462.4 1.9 copy-done
  464.3 0.0 copy-start.1
  464.3 1.6 copy-done.1
  465.9 0.0 copy-start.2
  465.9 1.2 copy-done.2
  467.1 0.0 copy-start.3
  467.1 0.9 copy-done.3
  468.0 0.0 copy-start.4
  468.0 0.9 copy-done.4
  468.9 168.6 %gradient_sums.1 = (bf16[1024,2048]{1,0:T(8,128)(2,1)}, bf16[2048,1024]{1,0:T(8,128)(2,1)}, bf16[512,1024]{1,0:T(8,128)(2,1)S(1)}, bf16[1024,1536]{1,0:T(8,128)(2,1)S(1)}, f32[8,1536]{1,0:T(8,128)S(1)}) custom-call(bf16[2,1024,1024]{2,1,0:T(8,128)(2,1)} %get-tuple-element.29.norm_hbm, bf16[1024,1024]{1,0:T(8,128)(2,1)S(1)} %copy-done.1, ...), custom_call_target="tpu_custom_call" | custom-call | tf_op jit(solution)/shard_map/gradient_sums/pallas_call | solution.py:1168
  637.5 0.0 copy-start.10
  637.5 0.6 slice_bitcast_fusion.1
  638.2 0.6 slice.24
  638.8 0.6 slice.25
  639.4 1.6 bitcast_convert_fusion.3
  640.9 0.0 copy-start.6
  640.9 3.6 bitcast_convert_fusion.2
  644.5 0.0 copy-done.6
  644.5 0.0 copy-start.5
  644.5 4.4 bitcast_convert_fusion.1
  649.0 0.0 copy-done.5
  649.0 0.0 copy-start.8
  649.0 0.0 copy-start.7
  649.0 4.4 bitcast_convert_fusion
  653.4 0.0 copy-done.10
  653.4 0.6 copy.29
  654.0 0.0 copy-done.8
  654.0 1.0 copy.30
  655.0 0.0 copy-done.7
  655.0 1.3 copy.31
  (9 shorter events, 0.2 us)
Async XLA Ops:
  1.5 7.6 %copy-start.9 = (s32[4,8]{1,0:T(4,128)}, s32[4,8]{1,0:T(4,128)S(1)}, u32[]{:S(2)}) copy-start(s32[4,8]{1,0:T(4,128)S(1)} %reduce_window_sum.11.ends) | copy-start | bytes 388
  462.4 1.9 copy-start
  464.3 1.6 copy-start.1
  465.9 1.2 copy-start.2
  467.1 0.9 copy-start.3
  468.0 0.9 copy-start.4
  637.5 15.9 %copy-start.10 = (f32[1,1024]{1,0:T(1,128)}, f32[1,1024]{1,0:T(1,128)S(1)}, u32[]{:S(2)}) copy-start(f32[1,1024]{1,0:T(1,128)S(1)} %slice.22) | copy-start | bytes 12292
  640.9 3.6 copy-start.6
  644.5 4.5 copy-start.5
  649.0 5.0 copy-start.8
  649.0 6.0 copy-start.7

commit v3 on v2

--- a/solution.py
+++ b/solution.py
@@ -113,6 +113,7 @@
     dpk_st,
     slope,
     part,
+    part_b,
     dn1,
     qm,
     kr,
@@ -146,6 +147,7 @@
     xs_ss,
     gs_ss,
     store_sem,
+    g_store,
 ):
     micro, rows, group, wide, heads, d_model, ff = dims
     sect = lax.axis_index("section")
@@ -239,9 +241,6 @@
             lax.fori_loop(0, rows // 32, chunk, 0)
             y_send_g(s).start()
 
-    for load in loads:
-        load.wait()
-
     def fold(values):
         total = values[0:8]
         for k in range(1, values.shape[0] // 8):
@@ -294,6 +293,11 @@
             norm_st[0, at, :] = (a * gain[0:1, :] + shift[0:1, :]).astype(BF16)
             norm_st[1, at, :] = (a * gain[1:2, :] + shift[1:2, :]).astype(BF16)
             return carry
+
+        @pl.when(s > 0)
+        def _():
+            arrived(norm_st.at[0], store_sem.at[0])
+            arrived(norm_st.at[1], store_sem.at[1])
 
         lax.fori_loop(0, group // 32, norm_step, 0)
         pltpu.make_async_copy(norm_st.at[0], norm_hbm.at[0, tokens_of(s)], store_sem.at[0]).start()
@@ -319,9 +323,19 @@
                 spread(qkv_st.at[dest], qkv_r, s, dest, qkv_ss.at[0], qkv_rs.at[s])
             return carry
 
+        pl.when(s == 0)(loads[0].wait)
         lax.fori_loop(0, pairs, qkv_step, 0)
 
     def forward_ff(s):
+        @pl.when(s == 0)
+        def _():
+            loads[1].wait()
+            loads[2].wait()
+
+        @pl.when(s > 0)
+        def _():
+            arrived(hid_st, store_sem.at[2])
+
         def ff_step(j, carry):
             cols = pl.ds(pl.multiple_of(j * COLS, COLS), COLS)
             pre = dot(norm_st[1], wup[:, cols]) + up_b[:, cols]
@@ -397,6 +411,8 @@
     def forward_out(s):
         arrived(mix_r.at[s], o_rs.at[s])
         arrived(o_st.at[s, pl.ds(0, wide - 1)], o_ss.at[s])
+        pl.when((s == 0) & (sect == 0))(loads[3].wait)
+        pl.when(s > 0)(lambda: arrived(mixed_st, store_sem.at[3]))
         for pair in range(pairs):
             top, bottom = pair_up(
                 mix_r[s, 2 * pair].astype(F32), mix_r[s, 2 * pair + 1].astype(F32), low_half
@@ -410,29 +426,27 @@
 
     def forward_end(s):
         arrived(rsf_r.at[s], rsf_rs.at[s])
+        arrived(rsf_st, rsf_ss.at[0])
+
+        @pl.when(s > 0)
+        def _():
+            arrived(out_st, store_sem.at[4])
+            pl.when(sect == 0)(lambda: arrived(out_st, xs_ss.at[0]))
 
         def out_step(i, carry):
             at = pl.ds(pl.multiple_of(i * 32, 32), 32)
             there = pl.ds(pl.multiple_of(tens * rows + i * 32, 32), 32)
             branch = part[there, :] + rsf_r[s, at, :].astype(F32) + out_b[...]
-            out_st[s, at, :] = (xfull[s, there, :].astype(F32) + branch).astype(BF16)
+            out_st[at, :] = (xfull[s, there, :].astype(F32) + branch).astype(BF16)
             return carry
 
         lax.fori_loop(0, rows // 32, out_step, 0)
 
         @pl.when(sect == 0)
         def _():
-            remote(
-                out_st.at[s], xfull.at[s, my_rows], xs_ss.at[s], ownx_sem.at[s], x_dev
-            ).start()
-
-        pltpu.make_async_copy(out_st.at[s], out_hbm.at[s], store_sem.at[4]).start()
-        arrived(rsf_st, rsf_ss.at[0])
-        arrived(norm_st.at[0], store_sem.at[0])
-        arrived(norm_st.at[1], store_sem.at[1])
-        arrived(hid_st, store_sem.at[2])
-        arrived(mixed_st, store_sem.at[3])
-        arrived(out_st.at[s], store_sem.at[4])
+            remote(out_st, xfull.at[s, my_rows], xs_ss.at[0], ownx_sem.at[s], x_dev).start()
+
+        pltpu.make_async_copy(out_st, out_hbm.at[s], store_sem.at[4]).start()
 
     def backward(s):
         @pl.when(sect == 0)
@@ -441,7 +455,8 @@
             y_send_g(s).start()
 
         arrived(gfull.at[s, his_rows], yg_r.at[s])
-        pltpu.make_async_copy(gfull.at[s], g_hbm.at[tokens_of(s)], store_sem.at[5]).start()
+        pl.when((s == 0) & (sect == 1))(loads[3].wait)
+        pltpu.make_async_copy(gfull.at[s], g_hbm.at[tokens_of(s)], g_store.at[s]).start()
 
         def mixed_step(k, carry):
             pair = lax.rem(me // 2 + 1 + k, pairs)
@@ -449,16 +464,18 @@
             both = dot_t(gfull[s], wdense[at, :])
             first = jnp.where(low_half, both[:half], turn(both[half:]))
             second = jnp.where(low_half, turn(both[:half]), both[half:])
-            do_st[2 * pair] = first.astype(BF16)
-            do_st[2 * pair + 1] = second.astype(BF16)
+            do_st[s, 2 * pair] = first.astype(BF16)
+            do_st[s, 2 * pair + 1] = second.astype(BF16)
             for i in range(2):
                 dest = 2 * pair + i
-                spread(do_st.at[dest], do_r, s, dest, do_ss.at[0], do_rs.at[s])
+                spread(do_st.at[s, dest], do_r, s, dest, do_ss.at[s], do_rs.at[s])
             return carry
 
         lax.fori_loop(0, pairs, mixed_step, 0)
 
     def backward_ff(s):
+        pl.when(s > 0)(lambda: arrived(dpre_st, store_sem.at[6]))
+
         def ff_step(j, carry):
             cols = pl.ds(pl.multiple_of(j * COLS, COLS), COLS)
             grad = dot_t(gfull[s], wdown[cols, :])
@@ -483,8 +500,8 @@
 
     def backward_attention(s):
         arrived(do_r.at[s], do_rs.at[s])
-        arrived(do_st.at[pl.ds(0, wide - 1)], do_ss.at[0])
-        unpack_heads(s)
+        arrived(do_st.at[s, pl.ds(0, wide - 1)], do_ss.at[s])
+        pl.when(sect == 0)(lambda: unpack_heads(s))
 
         def unpack_step(src, carry):
             at = pl.multiple_of(src * group, group)
@@ -502,6 +519,7 @@
 
         lax.fori_loop(0, wide, unpack_step, 0)
         dq[...] = jnp.zeros_like(dq)
+        slot = lax.rem(s, 2)
 
         def k_step(j, carry):
             k_at = pl.ds(pl.multiple_of(j * BLOCK, BLOCK), BLOCK)
@@ -538,16 +556,20 @@
                 both = jnp.where(low_group, dq[at, :], peak[mine, :])
                 value = acc[mine, :]
                 value = jnp.where(low_half, value[:half], turn(value[half:]))
-                dqkv_st[source, 0:group, :] = both.astype(BF16)
-                dqkv_st[source, group:per_source, :] = value.astype(BF16)
-                spread(dqkv_st.at[source], dqkv_r, s, source, dqkv_ss.at[0], dqkv_rs.at[s])
+                dqkv_st[slot, source, 0:group, :] = both.astype(BF16)
+                dqkv_st[slot, source, group:per_source, :] = value.astype(BF16)
+                spread(
+                    dqkv_st.at[slot, source], dqkv_r, s, source, dqkv_ss.at[slot], dqkv_rs.at[s]
+                )
             return carry
 
         lax.fori_loop(0, q_blocks, k_step, 0)
 
     def backward_norm(s):
         arrived(dqkv_r.at[s], dqkv_rs.at[s])
-        arrived(dqkv_st.at[pl.ds(0, wide - 1)], dqkv_ss.at[0])
+        slot = lax.rem(s, 2)
+        arrived(dqkv_st.at[slot, pl.ds(0, wide - 1)], dqkv_ss.at[slot])
+        pl.when(s > 0)(lambda: arrived(dpk_st, store_sem.at[7]))
 
         def pair_step(pair, carry):
             qk0 = rotary(
@@ -574,32 +596,38 @@
 
         lax.fori_loop(0, pairs, pair_step, 0)
         pltpu.make_async_copy(dpk_st, dpk_hbm.at[tokens_of(s)], store_sem.at[7]).start()
-        part[...] = dot_t(dpk_st[...], wqkv[...])
+        part_b[...] = dot_t(dpk_st[...], wqkv[...])
 
         def e_step(i, carry):
             at = pl.ds(pl.multiple_of(i * 32, 32), 32)
             a, _ = normed_rows(xfull[s, at, :].astype(F32))
-            first = part[at, :]
+            first = part_b[at, :]
             second = dn1[at, :]
             small[0] += fold(first * a)
             small[1] += fold(second * a)
             small[2] += fold(first)
             small[3] += fold(second)
-            part[at, :] = first * gain[0:1, :] + second * gain[1:2, :]
+            part_b[at, :] = first * gain[0:1, :] + second * gain[1:2, :]
             return carry
 
         lax.fori_loop(0, group // 32, e_step, 0)
-        rsb_st[...] = part[his_rows, :].astype(BF16)
+        rsb_st[...] = part_b[his_rows, :].astype(BF16)
         remote(rsb_st, rsb_r.at[s], rsb_ss.at[0], rsb_rs.at[s], y_dev).start()
 
     def backward_end(s):
         arrived(rsb_r.at[s], rsb_rs.at[s])
+        arrived(rsb_st, rsb_ss.at[0])
+
+        @pl.when(s > 0)
+        def _():
+            arrived(ig_st, store_sem.at[8])
+            pl.when(sect == 1)(lambda: arrived(gx_st, gs_ss.at[0]))
 
         def in_step(i, carry):
             at = pl.ds(pl.multiple_of(i * 32, 32), 32)
             there = pl.ds(pl.multiple_of(tens * rows + i * 32, 32), 32)
             a, inv = normed_rows(xfull[s, there, :].astype(F32))
-            e = part[there, :] + rsb_r[s, at, :].astype(F32)
+            e = part_b[there, :] + rsb_r[s, at, :].astype(F32)
             mean_e = jnp.mean(e, axis=-1, keepdims=True)
             cross = jnp.mean(e * a, axis=-1, keepdims=True)
             g_low = gfull[s, there, :].astype(F32)
@@ -607,63 +635,60 @@
             g = jnp.where(sect == 1, cot[s, at, :], g_low)
             grad = g + inv * (e - mean_e - a * cross)
             ig_st[at, :] = grad
-            gx_st[s, at, :] = grad.astype(BF16)
+            gx_st[at, :] = grad.astype(BF16)
             return carry
 
         lax.fori_loop(0, rows // 32, in_step, 0)
 
         @pl.when(sect == 1)
         def _():
-            remote(
-                gx_st.at[s], gfull.at[s, my_rows], gs_ss.at[s], owng_sem.at[s], x_dev
-            ).start()
+            remote(gx_st, gfull.at[s, my_rows], gs_ss.at[0], owng_sem.at[s], x_dev).start()
 
         pltpu.make_async_copy(ig_st, ig_hbm.at[s], store_sem.at[8]).start()
-        arrived(rsb_st, rsb_ss.at[0])
-        arrived(gfull.at[s], store_sem.at[5])
-        arrived(dpre_st, store_sem.at[6])
-        arrived(dpk_st, store_sem.at[7])
-        arrived(ig_st, store_sem.at[8])
-
-    def tick(step, carry):
-        f_seq = step - sect
-        b_seq = step - (3 - sect)
-        f_on = (f_seq >= 0) & (f_seq < micro)
-        b_on = (b_seq >= 0) & (b_seq < micro)
-        pl.when(f_on)(lambda: forward(f_seq))
-        pl.when(b_on)(lambda: backward(b_seq))
-        pl.when(f_on)(lambda: forward_ff(f_seq))
-        pl.when(b_on)(lambda: backward_ff(b_seq))
-        pl.when(f_on)(lambda: forward_attention(f_seq))
-        pl.when(b_on)(lambda: backward_attention(b_seq))
-
-        @pl.when(f_on)
-        def _():
-            forward_out(f_seq)
-            forward_end(f_seq)
-
-        @pl.when(b_on)
-        def _():
-            backward_norm(b_seq)
-            backward_end(b_seq)
-
+
+    def at(seq, allowed, body):
+        pl.when(allowed & (seq >= 0) & (seq < micro))(lambda: body(seq))
+
+    @pl.when(sect == 1)
+    def _():
+        lax.fori_loop(0, micro, lambda s, carry: (backward(s), carry)[1], 0)
+
+    first = jnp.int32(0)
+    forward(first)
+    forward_ff(first)
+    always = sect >= 0
+
+    def step(i, carry):
+        f = i
+        b = jnp.where(sect == 1, i, i - micro)
+        at(b, sect == 0, backward)
+        at(f, always, forward_attention)
+        at(f + 1, always, forward)
+        at(b, always, backward_attention)
+        at(f, always, forward_out)
+        at(b - 1, always, backward_norm)
+        at(b, always, backward_ff)
+        at(f, always, forward_end)
+        at(b - 1, always, backward_end)
+        at(f + 1, always, forward_ff)
         return carry
 
-    lax.fori_loop(0, micro + 3, tick, 0)
+    lax.fori_loop(0, jnp.where(sect == 1, micro + 1, 2 * micro + 1), step, 0)
 
     for s in range(micro):
         arrived(xfull.at[s, my_rows], yx_s.at[s])
         arrived(gfull.at[s, my_rows], yg_s.at[s])
-
-    @pl.when(sect == 0)
-    def _():
-        for s in range(micro):
-            arrived(out_st.at[s], xs_ss.at[s])
-
-    @pl.when(sect == 1)
-    def _():
-        for s in range(micro):
-            arrived(gx_st.at[s], gs_ss.at[s])
+        arrived(gfull.at[s], g_store.at[s])
+    arrived(norm_st.at[0], store_sem.at[0])
+    arrived(norm_st.at[1], store_sem.at[1])
+    arrived(hid_st, store_sem.at[2])
+    arrived(mixed_st, store_sem.at[3])
+    arrived(out_st, store_sem.at[4])
+    arrived(dpre_st, store_sem.at[6])
+    arrived(dpk_st, store_sem.at[7])
+    arrived(ig_st, store_sem.at[8])
+    pl.when(sect == 0)(lambda: arrived(out_st, xs_ss.at[0]))
+    pl.when(sect == 1)(lambda: arrived(gx_st, gs_ss.at[0]))
 
 
 def rotary_tables(doc_lengths, tokens):
@@ -743,12 +768,12 @@
         vmem((micro, rows, d_model), BF16),
         vmem((wide, per_source, LANES), BF16),
         vmem((micro, wide, group // 2, LANES), BF16),
-        vmem((wide, group // 2, LANES), BF16),
-        vmem((wide, per_source, LANES), BF16),
+        vmem((micro, wide, group // 2, LANES), BF16),
+        vmem((2, wide, per_source, LANES), BF16),
         vmem((rows, d_model), BF16),
         vmem((rows, d_model), BF16),
-        vmem((micro, rows, d_model), BF16),
-        vmem((micro, rows, d_model), BF16),
+        vmem((rows, d_model), BF16),
+        vmem((rows, d_model), BF16),
         vmem((rows, d_model), F32),
         vmem((2, group, d_model), BF16),
         vmem((group, inner), BF16),
@@ -756,6 +781,7 @@
         vmem((group, ff), BF16),
         vmem((group, 3 * inner), BF16),
         vmem((micro, group, ff), BF16),
+        vmem((group, d_model), F32),
         vmem((group, d_model), F32),
         vmem((group, d_model), F32),
         vmem((SEQ, LANES), BF16),
@@ -779,17 +805,18 @@
         dma((micro,)),
         dma((micro,)),
         dma((micro,)),
-        dma((1,)),
+        dma((micro,)),
+        dma((micro,)),
+        dma((2,)),
         dma((micro,)),
         dma((1,)),
         dma((micro,)),
         dma((1,)),
         dma((micro,)),
         dma((1,)),
+        dma((1,)),
+        dma((9,)),
         dma((micro,)),
-        dma((micro,)),
-        dma((micro,)),
-        dma((9,)),
     ]
     return pl.pallas_call(
         functools.partial(relay_kernel, dims),

time: 657 us -> 576 us (0.88)
  Pallas kernels: 620 us -> 539 us
    pallas_call x1, Pallas kernels: 451 us -> 373 us  [relay(): pl.pallas_call(functools.partial(relay_kernel, dims), out_shape=outs, in_...]
where the time goes in v3:
time: 576 us; the launch traced here: 575 us
  Pallas kernels  539 us (94%)
  other arithmetic  18.9 us (3%)
  local copies, waits for them, and re-layouts  16.6 us (3%)
    pallas_call x1, Pallas kernels, relay(): pl.pallas_call(functools.partial(relay_kernel, dims), out_shape=outs, in_...  373 us
    pallas_call x1, Pallas kernels, gradient_sums(): pl.pallas_call(functools.partial(gradient_kernel, dims), out_shape=[jax.S...  166 us
    broadcast_in_dim x4, other arithmetic, relay_shards(): grad.astype(F32)[None]  14 us

profile of v3, /device:TPU:0, one launch (start us, length us, event | category | flops | bytes accessed | tf_op | source)
XLA Modules:
  0.0 575.0 jit_solution(2017858544915314087)
XLA Ops:
  0.7 0.9 reduce_window_sum.11.ends
  1.5 0.0 copy-start.9
  1.5 0.7 sub.16
  2.2 0.1 select_reduce_fusion
  2.3 1.3 add.18.out_b
  3.6 1.9 multiply_sine_fusion
  5.6 1.7 concatenate.9.cos
  7.4 1.7 concatenate.11.back
  9.2 0.0 copy-done.9
  9.2 1.7 concatenate.10.front
  10.9 373.1 %relay.1 = (bf16[4,128,1024]{2,1,0:T(8,128)(2,1)}, f32[4,128,1024]{2,1,0:T(8,128)}, bf16[2,1024,1024]{2,1,0:T(8,128)(2,1)}, bf16[1024,1024]{1,0:T(8,128)(2,1)}, ...) custom-call(s32[4,8]{1,0:T(4,128)} %copy-done.9, ...), custom_call_target="tpu_custom_call" | custom-call | tf_op jit(solution)/shard_map/relay/pallas_call | solution.py:821
  384.0 0.0 copy-start
  384.1 1.9 copy-done
  385.9 0.0 copy-start.1
  385.9 1.6 copy-done.1
  387.5 0.0 copy-start.2
  387.5 1.2 copy-done.2
  388.8 0.0 copy-start.3
  388.8 0.9 copy-done.3
  389.7 0.0 copy-start.4
  389.7 0.9 copy-done.4
  390.6 165.6 %gradient_sums.1 = (bf16[1024,2048]{1,0:T(8,128)(2,1)}, bf16[2048,1024]{1,0:T(8,128)(2,1)}, bf16[512,1024]{1,0:T(8,128)(2,1)S(1)}, bf16[1024,1536]{1,0:T(8,128)(2,1)S(1)}, f32[8,1536]{1,0:T(8,128)S(1)}) custom-call(bf16[2,1024,1024]{2,1,0:T(8,128)(2,1)} %get-tuple-element.29.norm_hbm, bf16[1024,1024]{1,0:T(8,128)(2,1)S(1)} %copy-done.1, ...), custom_call_target="tpu_custom_call" | custom-call | tf_op jit(solution)/shard_map/gradient_sums/pallas_call | solution.py:1195
  556.2 0.0 copy-start.10
  556.2 0.6 slice_bitcast_fusion.1
  556.8 0.6 slice.24
  557.4 0.6 slice.25
  558.0 1.6 bitcast_convert_fusion.3
  559.6 0.0 copy-start.6
  559.6 3.6 bitcast_convert_fusion.2
  563.2 0.0 copy-done.6
  563.2 0.0 copy-start.5
  563.2 4.4 bitcast_convert_fusion.1
  567.6 0.0 copy-done.5
  567.6 0.0 copy-start.8
  567.6 0.0 copy-start.7
  567.6 4.4 bitcast_convert_fusion
  572.1 0.0 copy-done.10
  572.1 0.6 copy.29
  572.7 0.0 copy-done.8
  572.7 1.0 copy.30
  573.7 0.0 copy-done.7
  573.7 1.3 copy.31
  (9 shorter events, 0.2 us)
Async XLA Ops:
  1.5 7.6 %copy-start.9 = (s32[4,8]{1,0:T(4,128)}, s32[4,8]{1,0:T(4,128)S(1)}, u32[]{:S(2)}) copy-start(s32[4,8]{1,0:T(4,128)S(1)} %reduce_window_sum.11.ends) | copy-start | bytes 388
  384.0 1.9 copy-start
  385.9 1.6 copy-start.1
  387.5 1.2 copy-start.2
  388.8 0.9 copy-start.3
  389.7 0.9 copy-start.4
  556.2 15.9 %copy-start.10 = (f32[1,1024]{1,0:T(1,128)}, f32[1,1024]{1,0:T(1,128)S(1)}, u32[]{:S(2)}) copy-start(f32[1,1024]{1,0:T(1,128)S(1)} %slice.22) | copy-start | bytes 12292
  559.6 3.6 copy-start.6
  563.2 4.5 copy-start.5
  567.6 5.0 copy-start.8
  567.6 6.0 %copy-start.7 = (f32[4,128,1024]{2,1,0:T(8,128)S(1)}, f32[4,128,1024]{2,1,0:T(8,128)}, u32[]{:S(2)}) copy-start(f32[4,128,1024]{2,1,0:T(8,128)} %get-tuple-element.28) | copy-start | bytes 6291460

commit v4 on v3

--- a/solution.py
+++ b/solution.py
@@ -277,7 +277,7 @@
             ).astype(BF16)
             return carry
 
-        lax.fori_loop(0, wide, step, 0)
+        lax.fori_loop(0, wide, step, 0, unroll=True)
 
     def forward(s):
         @pl.when(sect == 1)
@@ -299,7 +299,7 @@
             arrived(norm_st.at[0], store_sem.at[0])
             arrived(norm_st.at[1], store_sem.at[1])
 
-        lax.fori_loop(0, group // 32, norm_step, 0)
+        lax.fori_loop(0, group // 32, norm_step, 0, unroll=True)
         pltpu.make_async_copy(norm_st.at[0], norm_hbm.at[0, tokens_of(s)], store_sem.at[0]).start()
         pltpu.make_async_copy(norm_st.at[1], norm_hbm.at[1, tokens_of(s)], store_sem.at[1]).start()
 
@@ -324,7 +324,7 @@
             return carry
 
         pl.when(s == 0)(loads[0].wait)
-        lax.fori_loop(0, pairs, qkv_step, 0)
+        lax.fori_loop(0, pairs, qkv_step, 0, unroll=True)
 
     def forward_ff(s):
         @pl.when(s == 0)
@@ -356,7 +356,7 @@
 
             return carry
 
-        lax.fori_loop(0, ff // COLS, ff_step, 0)
+        lax.fori_loop(0, ff // COLS, ff_step, 0, unroll=True)
         pltpu.make_async_copy(hid_st, hid_hbm.at[tokens_of(s)], store_sem.at[2]).start()
 
     def forward_attention(s):
@@ -364,38 +364,30 @@
         arrived(qkv_st.at[pl.ds(0, wide - 1)], qkv_ss.at[0])
         unpack_heads(s)
 
-        def q_step(i, carry):
-            q_at = pl.ds(pl.multiple_of(i * BLOCK, BLOCK), BLOCK)
+        for i in range(q_blocks):
+            q_at = slice(i * BLOCK, (i + 1) * BLOCK)
             tokens = i * BLOCK + lax.broadcasted_iota(jnp.int32, (BLOCK, LANES), 0)
             begin = starts_of(s, tokens)[:, 0:1]
-            token = tokens[:, 0:1]
-            peak[...] = jnp.full(peak.shape, NEG, F32)
-
-            def score_step(j, inner):
-                k_at = pl.ds(pl.multiple_of(j * BLOCK, BLOCK), BLOCK)
+            best = jnp.full((BLOCK, LANES), NEG, F32)
+            for j in range(i + 1):
+                k_at = slice(j * BLOCK, (j + 1) * BLOCK)
                 raw = dot_t(qm[q_at, :], kr[k_at, :])
                 u = j * BLOCK + lax.broadcasted_iota(jnp.int32, (BLOCK, BLOCK), 1)
-                raw = jnp.where((u >= begin) & (u <= token), raw, NEG)
+                seen = u >= begin
+                if i == j:
+                    seen = seen & (u <= tokens[:, 0:1])
+                raw = jnp.where(seen, raw, NEG)
                 scores[:, k_at] = raw
-                best = peak[...]
                 for k in range(BLOCK // LANES):
                     best = jnp.maximum(best, raw[:, k * LANES : (k + 1) * LANES])
-                peak[...] = best
-                return inner
-
-            lax.fori_loop(0, i + 1, score_step, 0)
-            top = jnp.max(peak[...], axis=1, keepdims=True) * SCORE_SCALE
-            acc[...] = jnp.zeros_like(acc)
-
-            def value_step(j, inner):
-                k_at = pl.ds(pl.multiple_of(j * BLOCK, BLOCK), BLOCK)
+            top = jnp.max(best, axis=1, keepdims=True) * SCORE_SCALE
+            out = jnp.zeros((BLOCK, LANES), F32)
+            for j in range(i + 1):
+                k_at = slice(j * BLOCK, (j + 1) * BLOCK)
                 probs = jnp.exp2(scores[:, k_at] * SCORE_SCALE - top)
-                acc[...] += dot(probs.astype(BF16), vx[k_at, :])
-                return inner
-
-            lax.fori_loop(0, i + 1, value_step, 0)
-            total = acc[:, HEAD_DIM : HEAD_DIM + 1]
-            out = acc[...] / total
+                out = out + dot(probs.astype(BF16), vx[k_at, :])
+            total = out[:, HEAD_DIM : HEAD_DIM + 1]
+            out = out / total
             log_total = top + jnp.log2(total)
             lse[s, i] = jnp.broadcast_to(log_total, (BLOCK, LANES)).T[0:8, :]
             for k in range(sources):
@@ -404,9 +396,6 @@
                 source = i * sources + k
                 o_st[s, source] = jnp.where(low_half, first, turn(second)).astype(BF16)
                 spread(o_st.at[s, source], mix_r, s, source, o_ss.at[s], o_rs.at[s])
-            return carry
-
-        lax.fori_loop(0, q_blocks, q_step, 0)
 
     def forward_out(s):
         arrived(mix_r.at[s], o_rs.at[s])
@@ -440,7 +429,7 @@
             out_st[at, :] = (xfull[s, there, :].astype(F32) + branch).astype(BF16)
             return carry
 
-        lax.fori_loop(0, rows // 32, out_step, 0)
+        lax.fori_loop(0, rows // 32, out_step, 0, unroll=True)
 
         @pl.when(sect == 0)
         def _():
@@ -471,7 +460,7 @@
                 spread(do_st.at[s, dest], do_r, s, dest, do_ss.at[s], do_rs.at[s])
             return carry
 
-        lax.fori_loop(0, pairs, mixed_step, 0)
+        lax.fori_loop(0, pairs, mixed_step, 0, unroll=True)
 
     def backward_ff(s):
         pl.when(s > 0)(lambda: arrived(dpre_st, store_sem.at[6]))
@@ -495,7 +484,7 @@
 
             return carry
 
-        lax.fori_loop(0, ff // COLS, ff_step, 0)
+        lax.fori_loop(0, ff // COLS, ff_step, 0, unroll=True)
         pltpu.make_async_copy(dpre_st, dpre_hbm.at[tokens_of(s)], store_sem.at[6]).start()
 
     def backward_attention(s):
@@ -517,43 +506,48 @@
             delta[src, :, half:group] = jnp.broadcast_to(right, (half, LANES)).T[0:8, :]
             return carry
 
-        lax.fori_loop(0, wide, unpack_step, 0)
-        dq[...] = jnp.zeros_like(dq)
+        lax.fori_loop(0, wide, unpack_step, 0, unroll=True)
         slot = lax.rem(s, 2)
-
-        def k_step(j, carry):
-            k_at = pl.ds(pl.multiple_of(j * BLOCK, BLOCK), BLOCK)
-            acc[...] = jnp.zeros_like(acc)
-            peak[...] = jnp.zeros_like(peak)
-
-            def q_step(i, inner):
-                q_at = pl.ds(pl.multiple_of(i * BLOCK, BLOCK), BLOCK)
-                tokens = i * BLOCK + lax.broadcasted_iota(jnp.int32, (8, BLOCK), 1)
-                begin = starts_of(s, tokens)[0:1, :]
-                token = tokens[0:1, :]
+        rows_of = []
+        for i in range(q_blocks):
+            tokens = i * BLOCK + lax.broadcasted_iota(jnp.int32, (8, BLOCK), 1)
+            inner_sum = jnp.concatenate(
+                [delta[i * sources + k, 0:1, :] for k in range(sources)], axis=1
+            )
+            rows_of.append((starts_of(s, tokens)[0:1, :], tokens[0:1, :], inner_sum))
+        for j in range(q_blocks):
+            k_at = slice(j * BLOCK, (j + 1) * BLOCK)
+            for i in range(j, q_blocks):
+                q_at = slice(i * BLOCK, (i + 1) * BLOCK)
+                begin, token, inner_sum = rows_of[i]
                 raw = dot_t(kr[k_at, :], qm[q_at, :])
                 u = j * BLOCK + lax.broadcasted_iota(jnp.int32, (BLOCK, BLOCK), 0)
                 probs = jnp.exp2(raw * SCORE_SCALE - lse[s, i, 0:1, :])
-                probs = jnp.where((u >= begin) & (u <= token), probs, 0.0)
+                seen = u >= begin
+                if i == j:
+                    seen = seen & (u <= token)
+                probs = jnp.where(seen, probs, 0.0)
                 probs_grad = dot_t(vx[k_at, :], dox[q_at, :])
-                inner_sum = jnp.concatenate(
-                    [delta[i * sources + k, 0:1, :] for k in range(sources)], axis=1
-                )
-                score_grad = (
-                    probs * (probs_grad - inner_sum) * (1.0 / math.sqrt(HEAD_DIM))
-                ).astype(BF16)
-                acc[...] += dot(probs.astype(BF16), dox[q_at, :])
-                peak[...] += dot(score_grad, qm_turned[q_at, :])
-                dq[q_at, :] += t_dot(score_grad, kr[k_at, :])
-                return inner
-
-            qm_turned = kr
-            lax.fori_loop(j, q_blocks, q_step, 0)
+                score_grad = (probs * (probs_grad - inner_sum)).astype(BF16)
+                value_term = dot(probs.astype(BF16), dox[q_at, :])
+                key_term = dot(score_grad, kr[q_at, :])
+                query_term = t_dot(score_grad, kr[k_at, :])
+                if i == j:
+                    acc[...] = value_term
+                    peak[...] = key_term
+                else:
+                    acc[...] += value_term
+                    peak[...] += key_term
+                if j == 0:
+                    dq[q_at, :] = query_term
+                else:
+                    dq[q_at, :] += query_term
             for k in range(sources):
                 source = j * sources + k
                 mine = slice(k * group, (k + 1) * group)
-                at = pl.ds(pl.multiple_of(source * group, group), group)
+                at = slice(source * group, (source + 1) * group)
                 both = jnp.where(low_group, dq[at, :], peak[mine, :])
+                both = both * (1.0 / math.sqrt(HEAD_DIM))
                 value = acc[mine, :]
                 value = jnp.where(low_half, value[:half], turn(value[half:]))
                 dqkv_st[slot, source, 0:group, :] = both.astype(BF16)
@@ -561,9 +555,6 @@
                 spread(
                     dqkv_st.at[slot, source], dqkv_r, s, source, dqkv_ss.at[slot], dqkv_rs.at[s]
                 )
-            return carry
-
-        lax.fori_loop(0, q_blocks, k_step, 0)
 
     def backward_norm(s):
         arrived(dqkv_r.at[s], dqkv_rs.at[s])
@@ -594,7 +585,7 @@
                 bias_sums[:, at] += fold(column.astype(F32))
             return carry
 
-        lax.fori_loop(0, pairs, pair_step, 0)
+        lax.fori_loop(0, pairs, pair_step, 0, unroll=True)
         pltpu.make_async_copy(dpk_st, dpk_hbm.at[tokens_of(s)], store_sem.at[7]).start()
         part_b[...] = dot_t(dpk_st[...], wqkv[...])
 
@@ -610,7 +601,7 @@
             part_b[at, :] = first * gain[0:1, :] + second * gain[1:2, :]
             return carry
 
-        lax.fori_loop(0, group // 32, e_step, 0)
+        lax.fori_loop(0, group // 32, e_step, 0, unroll=True)
         rsb_st[...] = part_b[his_rows, :].astype(BF16)
         remote(rsb_st, rsb_r.at[s], rsb_ss.at[0], rsb_rs.at[s], y_dev).start()
 
@@ -638,7 +629,7 @@
             gx_st[at, :] = grad.astype(BF16)
             return carry
 
-        lax.fori_loop(0, rows // 32, in_step, 0)
+        lax.fori_loop(0, rows // 32, in_step, 0, unroll=True)
 
         @pl.when(sect == 1)
         def _():

time: 576 us -> 538 us (0.934); the launches traced: 575 us -> 531 us
  Pallas kernels: 539 us -> 494 us
    pallas_call x1, Pallas kernels: 373 us -> 327 us  [relay(): pl.pallas_call(functools.partial(relay_kernel, dims), out_shape=outs, in_...]
where the time goes in v4:
time: 538 us; the launch traced here: 531 us
  Pallas kernels  494 us (92%)
  other arithmetic  18.9 us (4%)
  local copies, waits for them, and re-layouts  16.6 us (3%)
    pallas_call x1, Pallas kernels, relay(): pl.pallas_call(functools.partial(relay_kernel, dims), out_shape=outs, in_...  327 us
    pallas_call x1, Pallas kernels, gradient_sums(): pl.pallas_call(functools.partial(gradient_kernel, dims), out_shape=[jax.S...  167 us
    broadcast_in_dim x4, other arithmetic, relay_shards(): grad.astype(F32)[None]  14 us

profile of v4, /device:TPU:0, one launch (start us, length us, event | category | flops | bytes accessed | tf_op | source)
XLA Modules:
  0.0 530.8 jit_solution(8164124106719713264)
XLA Ops:
  0.7 0.9 reduce_window_sum.11.ends
  1.5 0.0 copy-start.9
  1.5 0.7 sub.16
  2.2 0.1 select_reduce_fusion
  2.3 1.3 add.18.out_b
  3.6 1.9 multiply_sine_fusion
  5.6 1.7 concatenate.9.cos
  7.4 1.7 concatenate.11.back
  9.2 0.0 copy-done.9
  9.2 1.7 concatenate.10.front
  10.9 326.8 %relay.1 = (bf16[4,128,1024]{2,1,0:T(8,128)(2,1)}, f32[4,128,1024]{2,1,0:T(8,128)}, bf16[2,1024,1024]{2,1,0:T(8,128)(2,1)}, bf16[1024,1024]{1,0:T(8,128)(2,1)}, ...) custom-call(s32[4,8]{1,0:T(4,128)} %copy-done.9, ...), custom_call_target="tpu_custom_call" | custom-call | tf_op jit(solution)/shard_map/relay/pallas_call | solution.py:812
  337.7 0.0 copy-start
  337.8 1.9 copy-done
  339.6 0.0 copy-start.1
  339.6 1.6 copy-done.1
  341.2 0.0 copy-start.2
  341.2 1.2 copy-done.2
  342.5 0.0 copy-start.3
  342.5 0.9 copy-done.3
  343.4 0.0 copy-start.4
  343.4 0.9 copy-done.4
  344.3 167.5 %gradient_sums.1 = (bf16[1024,2048]{1,0:T(8,128)(2,1)}, bf16[2048,1024]{1,0:T(8,128)(2,1)}, bf16[512,1024]{1,0:T(8,128)(2,1)S(1)}, bf16[1024,1536]{1,0:T(8,128)(2,1)S(1)}, f32[8,1536]{1,0:T(8,128)S(1)}) custom-call(bf16[2,1024,1024]{2,1,0:T(8,128)(2,1)} %get-tuple-element.29.norm_hbm, bf16[1024,1024]{1,0:T(8,128)(2,1)S(1)} %copy-done.1, ...), custom_call_target="tpu_custom_call" | custom-call | tf_op jit(solution)/shard_map/gradient_sums/pallas_call | solution.py:1186
  511.8 0.0 copy-start.10
  511.8 0.6 slice_bitcast_fusion.1
  512.4 0.6 slice.24
  513.0 0.6 slice.25
  513.6 1.6 bitcast_convert_fusion.3
  515.2 0.0 copy-start.6
  515.2 3.6 bitcast_convert_fusion.2
  518.8 0.0 copy-done.6
  518.8 0.0 copy-start.5
  518.8 4.4 bitcast_convert_fusion.1
  523.2 0.0 copy-done.5
  523.2 0.0 copy-start.8
  523.2 0.0 copy-start.7
  523.2 4.4 bitcast_convert_fusion
  527.7 0.0 copy-done.10
  527.7 0.6 copy.29
  528.3 0.0 copy-done.8
  528.3 1.0 copy.30
  529.3 0.0 copy-done.7
  529.3 1.3 copy.31
  (9 shorter events, 0.2 us)
Async XLA Ops:
  1.5 7.6 %copy-start.9 = (s32[4,8]{1,0:T(4,128)}, s32[4,8]{1,0:T(4,128)S(1)}, u32[]{:S(2)}) copy-start(s32[4,8]{1,0:T(4,128)S(1)} %reduce_window_sum.11.ends) | copy-start | bytes 388
  337.7 1.9 copy-start
  339.6 1.6 copy-start.1
  341.2 1.2 copy-start.2
  342.5 0.9 copy-start.3
  343.4 0.9 copy-start.4
  511.8 15.9 %copy-start.10 = (f32[1,1024]{1,0:T(1,128)}, f32[1,1024]{1,0:T(1,128)S(1)}, u32[]{:S(2)}) copy-start(f32[1,1024]{1,0:T(1,128)S(1)} %slice.22) | copy-start | bytes 12292
  515.2 3.6 copy-start.6
  518.8 4.5 copy-start.5
  523.2 5.0 copy-start.8
  523.2 6.0 %copy-start.7 = (f32[4,128,1024]{2,1,0:T(8,128)S(1)}, f32[4,128,1024]{2,1,0:T(8,128)}, u32[]{:S(2)}) copy-start(f32[4,128,1024]{2,1,0:T(8,128)} %get-tuple-element.28) | copy-start | bytes 6291460

commit v5 on v4

--- a/solution.py
+++ b/solution.py
@@ -26,6 +26,19 @@
 SCORE_SCALE = math.log2(math.e) / math.sqrt(HEAD_DIM)
 
 
+TILE = 256
+ACROSS = 256
+AHEAD = 3
+RING = 8
+TOTALS = 8
+LAGS = (1, 3, 5, 8, 10)
+EARLY = 16
+
+
+def gradient_kinds(d_model, inner, ff):
+    return ((d_model, ff), (ff, d_model), (inner, d_model), (d_model, 3 * inner))
+
+
 def dot(a, b):
     return jnp.dot(a, b, preferred_element_type=F32)
 
@@ -59,21 +72,19 @@
 
 def relay_kernel(
     dims,
-    ends,
+    lengths,
     x_hbm,
     cot_hbm,
     gain,
     shift,
     qkv_b,
     up_b,
-    out_b,
+    dense_b,
+    down_b,
     wqkv_hbm,
     wdense_hbm,
     wup_hbm,
     wdown_hbm,
-    cos,
-    front,
-    back,
     out_hbm,
     ig_hbm,
     norm_hbm,
@@ -82,8 +93,16 @@
     hid_hbm,
     dpre_hbm,
     dpk_hbm,
+    up_out,
+    down_out,
+    dense_out,
+    qkv_out,
+    sums,
     small,
     bias_sums,
+    cos,
+    front,
+    back,
     wqkv,
     wdense,
     wup,
@@ -148,6 +167,26 @@
     gs_ss,
     store_sem,
     g_store,
+    core_r,
+    outer_r,
+    inner_r,
+    sums_r,
+    op_sem,
+    core_ss,
+    core_rs,
+    outer_rs,
+    inner_rs,
+    red_ss,
+    bc_rs,
+    tot_ss,
+    fwd_ss,
+    share_ss,
+    fin_rs,
+    sum_ss,
+    sum_rs,
+    core_free,
+    outer_free,
+    inner_free,
 ):
     micro, rows, group, wide, heads, d_model, ff = dims
     sect = lax.axis_index("section")
@@ -217,6 +256,31 @@
         for s in range(micro):
             pltpu.make_async_copy(cot_hbm.at[s], cot.at[s], owng_sem.at[s]).start()
 
+    def starts_of(s, tokens):
+        found = jnp.zeros_like(tokens)
+        end = jnp.int32(0)
+        for j in range(lengths.shape[1]):
+            end = end + lengths[s, j]
+            found = jnp.where(tokens >= end, end, found)
+        return found
+
+    lane = lax.rem(lax.broadcasted_iota(jnp.int32, (8, LANES), 1), HEAD_DIM)
+    number = lax.rem(lane, ROT // 2)
+    freq = jnp.zeros((8, LANES), F32)
+    for k in range(ROT // 2):
+        freq = jnp.where(number == k, ROPE_BASE ** (-2.0 * k / ROT), freq)
+    lane, freq = lane[0:1, :], freq[0:1, :]
+
+    def table_step(s, carry):
+        tokens = me * group + lax.broadcasted_iota(jnp.int32, (group, LANES), 0)
+        angle = (tokens - starts_of(s, tokens)).astype(F32) * freq
+        sine = jnp.sin(angle)
+        cos[s] = jnp.where(lane < ROT, jnp.cos(angle), 1.0)
+        front[s] = jnp.where(lane < ROT // 2, -sine, 0.0)
+        back[s] = jnp.where((lane >= ROT // 2) & (lane < ROT), sine, 0.0)
+        return carry
+
+    lax.fori_loop(0, micro, table_step, 0)
     small[...] = jnp.zeros_like(small)
     bias_sums[...] = jnp.zeros_like(bias_sums)
     pl.semaphore_wait(barrier, wide + 1)
@@ -253,13 +317,6 @@
         spread_of = jnp.mean(centred * centred, axis=-1, keepdims=True)
         inv = lax.rsqrt(spread_of + EPSILON)
         return centred * inv, inv
-
-    def starts_of(s, tokens):
-        found = jnp.zeros_like(tokens)
-        for j in range(ends.shape[1]):
-            end = ends[s, j]
-            found = jnp.where(tokens >= end, end, found)
-        return found
 
     def unpack_heads(s):
         def step(src, carry):
@@ -279,12 +336,15 @@
 
         lax.fori_loop(0, wide, step, 0, unroll=True)
 
+    def forward_meet(s):
+        arrived(xfull.at[s, my_rows], ownx_sem.at[s])
+        y_send_x(s).start()
+
+    def backward_meet(s):
+        arrived(gfull.at[s, my_rows], owng_sem.at[s])
+        y_send_g(s).start()
+
     def forward(s):
-        @pl.when(sect == 1)
-        def _():
-            arrived(xfull.at[s, my_rows], ownx_sem.at[s])
-            y_send_x(s).start()
-
         arrived(xfull.at[s, his_rows], yx_r.at[s])
 
         def norm_step(i, carry):
@@ -425,7 +485,7 @@
         def out_step(i, carry):
             at = pl.ds(pl.multiple_of(i * 32, 32), 32)
             there = pl.ds(pl.multiple_of(tens * rows + i * 32, 32), 32)
-            branch = part[there, :] + rsf_r[s, at, :].astype(F32) + out_b[...]
+            branch = part[there, :] + rsf_r[s, at, :].astype(F32) + (dense_b[...] + down_b[...])
             out_st[at, :] = (xfull[s, there, :].astype(F32) + branch).astype(BF16)
             return carry
 
@@ -438,11 +498,6 @@
         pltpu.make_async_copy(out_st, out_hbm.at[s], store_sem.at[4]).start()
 
     def backward(s):
-        @pl.when(sect == 0)
-        def _():
-            arrived(gfull.at[s, my_rows], owng_sem.at[s])
-            y_send_g(s).start()
-
         arrived(gfull.at[s, his_rows], yg_r.at[s])
         pl.when((s == 0) & (sect == 1))(loads[3].wait)
         pltpu.make_async_copy(gfull.at[s], g_hbm.at[tokens_of(s)], g_store.at[s]).start()
@@ -637,6 +692,268 @@
 
         pltpu.make_async_copy(ig_st, ig_hbm.at[s], store_sem.at[8]).start()
 
+    chip, core = me // 2, lax.rem(me, 2)
+    partner = {"wide": me + 1 - 2 * core}
+    up_dev = {"wide": lax.rem(me + 2, wide)}
+    down_dev = {"wide": lax.rem(me + wide - 2, wide)}
+    at_bottom, at_top = chip == 0, chip == wide // 2 - 1
+    at_end = at_bottom | at_top
+    middle = jnp.logical_not(at_end)
+    lower = chip == 1
+    outer_of = {"wide": jnp.where(lower, me - 2, lax.rem(me + 2, wide))}
+    inner_of = {"wide": jnp.where(lower, me + 2, lax.rem(me + wide - 2, wide))}
+    end_of = {"wide": jnp.where(at_bottom, me + 2, lax.rem(me + wide - 2, wide))}
+    kinds = gradient_kinds(d_model, heads * HEAD_DIM, ff)
+    targets = (up_out, down_out, dense_out, qkv_out)
+    operands = (
+        (norm_hbm.at[1], dpre_hbm),
+        (hid_hbm, g_hbm),
+        (mixed_hbm, g_hbm),
+        (norm_hbm.at[0], dpk_hbm),
+    )
+    ranges, first = [], 0
+    for height, width in kinds:
+        count = (height // TILE) * (width // (2 * ACROSS))
+        ranges.append((first, first + count, width // (2 * ACROSS)))
+        first += count
+    steps = first
+
+    def own_at(ring):
+        return scores.at[0:TILE, pl.ds(pl.multiple_of(ring * ACROSS, ACROSS), ACROSS)]
+
+    def core_st_at(ring):
+        return hid_st.at[:, pl.ds(pl.multiple_of(ring * ACROSS, ACROSS), ACROSS)]
+
+    def red_st_at(ring):
+        return dpre_st.at[:, pl.ds(pl.multiple_of(ring * ACROSS, ACROSS), ACROSS)]
+
+    def tot_at(slot):
+        cols = pl.ds(pl.multiple_of(lax.rem(slot, 4) * ACROSS, ACROSS), ACROSS)
+        return norm_st.at[slot // 4, :, cols]
+
+    def left_at(slot):
+        return wup.at[:, pl.ds(pl.multiple_of(slot * TILE, TILE), TILE)]
+
+    def right_at(slot):
+        return wdown.at[
+            pl.ds(pl.multiple_of((slot // 2) * d_model, d_model), d_model),
+            pl.ds(pl.multiple_of(lax.rem(slot, 2) * 2 * ACROSS, 2 * ACROSS), 2 * ACROSS),
+        ]
+
+    tile_ref = core_r.at[0]
+
+    def by_kind(m, body):
+        for kind, (low, high, across) in enumerate(ranges):
+
+            @pl.when((m >= low) & (m < high))
+            def _(kind=kind, low=low, across=across):
+                at = m - low
+                body(kind, at // across, lax.rem(at, across))
+
+    def tile_of(kind, row, col, which):
+        return targets[kind].at[
+            pl.ds(pl.multiple_of(row * TILE, TILE), TILE),
+            pl.ds(pl.multiple_of((2 * col + which) * ACROSS, ACROSS), ACROSS),
+        ]
+
+    def fetch(m):
+        pl.when(m == ranges[3][0])(lambda: arrived(dpk_st, store_sem.at[7]))
+
+        def body(kind, row, col):
+            left, right = operands[kind]
+            slot = lax.rem(m, AHEAD + 1)
+            pltpu.make_async_copy(
+                left.at[:, pl.ds(pl.multiple_of(row * TILE, TILE), TILE)],
+                left_at(slot),
+                op_sem.at[0, slot],
+            ).start()
+            pltpu.make_async_copy(
+                right.at[:, pl.ds(pl.multiple_of(col * 2 * ACROSS, 2 * ACROSS), 2 * ACROSS)],
+                right_at(slot),
+                op_sem.at[1, slot],
+            ).start()
+
+        by_kind(m, body)
+
+    def is_root(m):
+        return middle & (chip == 1 + lax.rem(m, 2))
+
+    def products(m):
+        slot, ring = lax.rem(m, AHEAD + 1), lax.rem(m, RING)
+        arrived(left_at(slot), op_sem.at[0, slot])
+        arrived(right_at(slot), op_sem.at[1, slot])
+        left, right = left_at(slot), right_at(slot)
+        mine = pl.ds(pl.multiple_of(core * ACROSS, ACROSS), ACROSS)
+        other = pl.ds(pl.multiple_of((1 - core) * ACROSS, ACROSS), ACROSS)
+
+        @pl.when(m >= RING)
+        def _():
+            arrived(tile_ref, core_ss.at[ring])
+            pl.semaphore_wait(core_free, 1)
+
+        core_st_at(ring)[...] = t_dot(left[...], right[:, other]).astype(BF16)
+        remote(
+            core_st_at(ring), core_r.at[ring], core_ss.at[ring], core_rs.at[ring], partner
+        ).start()
+        own_at(ring)[...] = t_dot(left[...], right[:, mine])
+
+    def send_red(m, value, target, sem, dev, free):
+        ring = lax.rem(m, RING)
+
+        @pl.when(m >= RING)
+        def _():
+            pl.semaphore_wait(free, 1)
+
+        red_st_at(ring)[...] = value.astype(BF16)
+        remote(red_st_at(ring), target.at[ring], red_ss.at[ring], sem.at[ring], dev).start()
+
+    def chip_sum(m):
+        ring = lax.rem(m, RING)
+        arrived(tile_ref, core_rs.at[ring])
+        total = own_at(ring)[...] + core_r[ring].astype(F32)
+
+        @pl.when(m + RING < steps)
+        def _():
+            pl.semaphore_signal(core_free, inc=1, device_id=partner, device_id_type=MESH)
+
+        @pl.when(at_end)
+        def _():
+            @pl.when(m >= RING)
+            def _():
+                arrived(tile_ref, red_ss.at[ring])
+
+            send_red(m, total, outer_r, outer_rs, end_of, outer_free.at[lax.rem(m, 2)])
+
+        @pl.when(middle)
+        def _():
+            own_at(ring)[...] = total
+
+    def take_outer(m):
+        ring = lax.rem(m, RING)
+        arrived(tile_ref, outer_rs.at[ring])
+        total = own_at(ring)[...] + outer_r[ring].astype(F32)
+
+        @pl.when(m + RING < steps)
+        def _():
+            pl.semaphore_signal(
+                outer_free.at[lax.rem(m, 2)], inc=1, device_id=outer_of, device_id_type=MESH
+            )
+
+        return total
+
+    def pass_in(m):
+        ring = lax.rem(m, RING)
+        total = take_outer(m)
+
+        @pl.when(m >= RING)
+        def _():
+            arrived(tile_ref, red_ss.at[ring])
+
+        send_red(m, total, inner_r, inner_rs, inner_of, inner_free)
+
+    def finish(m):
+        ring = lax.rem(m, RING)
+        slot = lax.rem(m // 2, TOTALS)
+        total = take_outer(m)
+        arrived(tile_ref, inner_rs.at[ring])
+        total = total + inner_r[ring].astype(F32)
+
+        @pl.when(m + RING < steps)
+        def _():
+            pl.semaphore_signal(inner_free, inc=1, device_id=inner_of, device_id_type=MESH)
+
+        @pl.when(m >= 2 * TOTALS)
+        def _():
+            for k in range(4):
+                arrived(tile_ref, tot_ss.at[k, slot])
+
+        tot_at(slot)[...] = total.astype(BF16)
+
+        def body(kind, row, col):
+            here = tile_of(kind, row, col, core)
+            remote(tot_at(slot), here, tot_ss.at[0, slot], bc_rs.at[m], outer_of).start()
+            remote(tot_at(slot), here, tot_ss.at[1, slot], bc_rs.at[m], inner_of).start()
+            remote(tot_at(slot), here, tot_ss.at[2, slot], fin_rs.at[kind], partner).start()
+            pltpu.make_async_copy(tot_at(slot), here, tot_ss.at[3, slot]).start()
+
+        by_kind(m, body)
+
+    def hand_on(m):
+        arrived(tile_ref, bc_rs.at[m])
+
+        def body(kind, row, col):
+            here = tile_of(kind, row, col, core)
+
+            @pl.when(middle)
+            def _():
+                remote(here, here, fwd_ss.at[m], bc_rs.at[m], outer_of).start()
+
+            remote(here, here, share_ss.at[m], fin_rs.at[kind], partner).start()
+
+        by_kind(m, body)
+
+    exchanges = (
+        {"tensor": 1 - tens},
+        partner,
+        {"wide": me + 2 - 4 * lax.rem(chip, 2)},
+        {"wide": me + 4 - 8 * (chip // 2)},
+    )
+
+    def sums_begin():
+        sums[:, 0:d_model] = jnp.concatenate(
+            [jnp.sum(small[k], axis=0, keepdims=True) for k in range(5)]
+            + [jnp.zeros((3, d_model), F32)],
+            axis=0,
+        )
+        total = jnp.sum(bias_sums[...], axis=0, keepdims=True)
+        lines = [total[:, k * COLS : (k + 1) * COLS] for k in range(total.shape[1] // COLS)]
+        lines.append(jnp.zeros((8 - len(lines), COLS), F32))
+        sums[:, d_model:] = jnp.concatenate(lines, axis=0)
+
+    def exchange_start(k):
+        if k == 0:
+            sums_begin()
+        else:
+            arrived(sums, sum_ss.at[0])
+        sums_r[0] = sums[...]
+        remote(sums_r.at[0], sums_r.at[k + 1], sum_ss.at[0], sum_rs.at[k], exchanges[k]).start()
+
+    def exchange_end(k):
+        arrived(sums, sum_rs.at[k])
+        if k == 0:
+            sums[:, 0:d_model] += sums_r[1, :, 0:d_model]
+        else:
+            sums[...] += sums_r[k + 1]
+
+    def gradient_step(i, carry):
+        pl.when(i + AHEAD < steps)(lambda: fetch(i + AHEAD))
+        pl.when(i < steps)(lambda: products(i))
+        for k in range(4):
+            pl.when(i == EARLY + 4 * k + 2)(lambda k=k: exchange_start(k))
+            pl.when(i == EARLY + 4 * k + 5)(lambda k=k: exchange_end(k))
+
+        def late(lag, allowed, body):
+            m = i - lag
+            pl.when((m >= 0) & (m < steps) & allowed(m))(lambda: body(m))
+
+        late(LAGS[0], lambda m: m >= 0, chip_sum)
+        late(LAGS[1], lambda m: middle & jnp.logical_not(is_root(m)), pass_in)
+        late(LAGS[2], is_root, finish)
+        late(LAGS[3], lambda m: middle & jnp.logical_not(is_root(m)), hand_on)
+        late(LAGS[4], lambda m: at_end, hand_on)
+        return carry
+
+    def gradient_begin():
+        arrived(norm_st.at[0], store_sem.at[0])
+        arrived(norm_st.at[1], store_sem.at[1])
+        arrived(hid_st, store_sem.at[2])
+        arrived(mixed_st, store_sem.at[3])
+        arrived(dpre_st, store_sem.at[6])
+        for s in range(micro):
+            arrived(gfull.at[s], g_store.at[s])
+        for m in range(AHEAD):
+            fetch(jnp.int32(m))
+
     def at(seq, allowed, body):
         pl.when(allowed & (seq >= 0) & (seq < micro))(lambda: body(seq))
 
@@ -645,6 +962,7 @@
         lax.fori_loop(0, micro, lambda s, carry: (backward(s), carry)[1], 0)
 
     first = jnp.int32(0)
+    pl.when(sect == 1)(lambda: forward_meet(first))
     forward(first)
     forward_ff(first)
     always = sect >= 0
@@ -652,16 +970,28 @@
     def step(i, carry):
         f = i
         b = jnp.where(sect == 1, i, i - micro)
+        at(b, (sect == 0) & (b == 0), backward_meet)
         at(b, sect == 0, backward)
+        at(f + 1, sect == 1, forward_meet)
         at(f, always, forward_attention)
         at(f + 1, always, forward)
         at(b, always, backward_attention)
+        at(b - 1, always, backward_norm)
         at(f, always, forward_out)
-        at(b - 1, always, backward_norm)
         at(b, always, backward_ff)
+        at(b + 1, (sect == 0) & (b >= 0), backward_meet)
+        at(b - 1, always, backward_end)
         at(f, always, forward_end)
-        at(b - 1, always, backward_end)
         at(f + 1, always, forward_ff)
+
+        starts = jnp.where(sect == 1, i == micro, i == 2 * micro - 1)
+        goes_on = (sect == 0) & (i == 2 * micro)
+        pl.when(starts)(gradient_begin)
+        low = jnp.where(goes_on, EARLY, 0)
+        high = jnp.where(
+            goes_on | (starts & (sect == 1)), steps + LAGS[4], jnp.where(starts, EARLY, 0)
+        )
+        lax.fori_loop(low, high, gradient_step, 0)
         return carry
 
     lax.fori_loop(0, jnp.where(sect == 1, micro + 1, 2 * micro + 1), step, 0)
@@ -669,43 +999,39 @@
     for s in range(micro):
         arrived(xfull.at[s, my_rows], yx_s.at[s])
         arrived(gfull.at[s, my_rows], yg_s.at[s])
-        arrived(gfull.at[s], g_store.at[s])
-    arrived(norm_st.at[0], store_sem.at[0])
-    arrived(norm_st.at[1], store_sem.at[1])
-    arrived(hid_st, store_sem.at[2])
-    arrived(mixed_st, store_sem.at[3])
     arrived(out_st, store_sem.at[4])
-    arrived(dpre_st, store_sem.at[6])
-    arrived(dpk_st, store_sem.at[7])
     arrived(ig_st, store_sem.at[8])
     pl.when(sect == 0)(lambda: arrived(out_st, xs_ss.at[0]))
     pl.when(sect == 1)(lambda: arrived(gx_st, gs_ss.at[0]))
 
-
-def rotary_tables(doc_lengths, tokens):
-    ends = jnp.cumsum(doc_lengths, axis=1)
-    starts = ends - doc_lengths
-    inside = (tokens[None, :, None] >= starts[:, None, :]) & (
-        tokens[None, :, None] < ends[:, None, :]
-    )
-    begins = jnp.sum(jnp.where(inside, starts[:, None, :], 0), axis=2)
-    offsets = (tokens[None, :] - begins).astype(F32)
-    part_of = ROT // 2
-    freqs = ROPE_BASE ** (-2.0 * jnp.arange(part_of, dtype=F32) / ROT)
-    angle = offsets[:, :, None] * freqs
-    cos, sin = jnp.cos(angle), jnp.sin(angle)
-    ones = jnp.ones(offsets.shape + (HEAD_DIM - ROT,), F32)
-    zeros = jnp.zeros_like(sin)
-
-    def lanes(parts):
-        return jnp.concatenate(parts + parts, axis=2)
-
-    return (
-        ends.astype(jnp.int32),
-        lanes([cos, cos, ones]),
-        lanes([-sin, zeros, 0.0 * ones]),
-        lanes([zeros, sin, 0.0 * ones]),
-    )
+    arrived(sums, sum_ss.at[0])
+    for ring in range(RING):
+        arrived(tile_ref, core_ss.at[ring])
+
+    def drain(m, carry):
+        ring = lax.rem(m, RING)
+        root = is_root(m)
+        last = m + RING >= steps
+        pl.when(at_end & last)(lambda: arrived(tile_ref, red_ss.at[ring]))
+        pl.when(middle & jnp.logical_not(root) & last)(
+            lambda: arrived(tile_ref, red_ss.at[ring])
+        )
+
+        @pl.when(root & (m + 2 * TOTALS >= steps))
+        def _():
+            for k in range(4):
+                arrived(tile_ref, tot_ss.at[k, lax.rem(m // 2, TOTALS)])
+
+        @pl.when(middle & jnp.logical_not(root))
+        def _():
+            arrived(tile_ref, fwd_ss.at[m])
+
+        pl.when(jnp.logical_not(root))(lambda: arrived(tile_ref, share_ss.at[m]))
+        return carry
+
+    lax.fori_loop(0, steps, drain, 0)
+    for kind, (height, width) in enumerate(kinds):
+        arrived(targets[kind].at[pl.ds(0, height // 2)], fin_rs.at[kind])
 
 
 def relay(dims, doc_lengths, block_input, cotangent, weights, collective_id):
@@ -722,8 +1048,6 @@
         down_weight,
         down_bias,
     ) = weights
-    tokens = lax.axis_index("wide") * group + jnp.arange(group, dtype=jnp.int32)
-    ends, cos, front, back = rotary_tables(doc_lengths, tokens)
     inner = heads * HEAD_DIM
     per_source = group + group // 2
     anywhere = pl.BlockSpec(memory_space=pl.ANY)
@@ -740,10 +1064,18 @@
         jax.ShapeDtypeStruct((micro * group, ff), BF16),
         jax.ShapeDtypeStruct((micro * group, ff), BF16),
         jax.ShapeDtypeStruct((micro * group, 3 * inner), BF16),
-        jax.ShapeDtypeStruct((5, 8, d_model), F32),
-        jax.ShapeDtypeStruct((8, 3 * inner + ff), F32),
     ]
+    kinds = gradient_kinds(d_model, inner, ff)
+    steps = sum((height // TILE) * (width // (2 * ACROSS)) for height, width in kinds)
+    outs += [jax.ShapeDtypeStruct(kind, BF16) for kind in kinds]
+    outs += [jax.ShapeDtypeStruct((8, d_model + COLS), F32)]
+    regular = pltpu.SemaphoreType.REGULAR
     scratch = [
+        vmem((5, 8, d_model), F32),
+        vmem((8, 3 * inner + ff), F32),
+        vmem((micro, group, LANES), F32),
+        vmem((micro, group, LANES), F32),
+        vmem((micro, group, LANES), F32),
         vmem(qkv_weight.shape, BF16),
         vmem(dense_weight.shape, BF16),
         vmem(up_weight.shape, BF16),
@@ -808,420 +1140,52 @@
         dma((1,)),
         dma((9,)),
         dma((micro,)),
+        vmem((RING, TILE, ACROSS), BF16),
+        vmem((RING, TILE, ACROSS), BF16),
+        vmem((RING, TILE, ACROSS), BF16),
+        vmem((5, 8, d_model + COLS), F32),
+        dma((2, AHEAD + 1)),
+        dma((RING,)),
+        dma((RING,)),
+        dma((RING,)),
+        dma((RING,)),
+        dma((RING,)),
+        dma((steps,)),
+        dma((4, TOTALS)),
+        dma((steps,)),
+        dma((steps,)),
+        dma((4,)),
+        dma((1,)),
+        dma((4,)),
+        regular,
+        regular((2,)),
+        regular,
     ]
     return pl.pallas_call(
         functools.partial(relay_kernel, dims),
         out_shape=outs,
-        in_specs=[scalars, anywhere, anywhere]
-        + [local] * 5
-        + [anywhere] * 4
-        + [local] * 3,
-        out_specs=[anywhere] * 8 + [local] * 2,
+        in_specs=[scalars, anywhere, anywhere] + [local] * 6 + [anywhere] * 4,
+        out_specs=[anywhere] * 12 + [local],
         scratch_shapes=scratch,
         compiler_params=pltpu.CompilerParams(
             collective_id=collective_id, has_side_effects=True, vmem_limit_bytes=63 << 20
         ),
         name="relay",
     )(
-        ends,
+        doc_lengths,
         block_input,
         cotangent,
         norm_gain,
         norm_bias,
         qkv_bias[None],
         up_bias[None],
-        (dense_bias + down_bias)[None],
+        dense_bias[None],
+        down_bias[None],
         qkv_weight,
         dense_weight,
         up_weight,
         down_weight,
-        cos,
-        front,
-        back,
-    )
-
-
-TILE = 256
-RING = 8
-TOTALS = 4
-
-
-def gradient_kinds(d_model, inner, ff):
-    return ((d_model, ff), (ff, d_model), (inner, d_model), (d_model, 3 * inner))
-
-
-def gradient_kernel(
-    dims,
-    norm_hbm,
-    g_hbm,
-    mixed_hbm,
-    hid_hbm,
-    dpre_hbm,
-    dpk_hbm,
-    small,
-    biases,
-    up_out,
-    down_out,
-    dense_out,
-    qkv_out,
-    sums,
-    left_op,
-    right_op,
-    own,
-    core_r,
-    outer_r,
-    inner_r,
-    core_st,
-    red_st,
-    tot,
-    sums_r,
-    op_sem,
-    core_ss,
-    core_rs,
-    outer_rs,
-    inner_rs,
-    red_ss,
-    bc_rs,
-    tot_ss,
-    fwd_ss,
-    share_ss,
-    fin_rs,
-    sum_ss,
-    sum_rs,
-    core_free,
-    outer_free,
-    inner_free,
-):
-    micro, rows, group, wide, heads, d_model, ff = dims
-    tens = lax.axis_index("tensor")
-    me = lax.axis_index("wide")
-    chip, core = me // 2, lax.rem(me, 2)
-    partner = {"wide": me + 1 - 2 * core}
-    up_dev = {"wide": lax.rem(me + 2, wide)}
-    down_dev = {"wide": lax.rem(me + wide - 2, wide)}
-    at_bottom, at_top = chip == 0, chip == wide // 2 - 1
-    at_end = at_bottom | at_top
-    middle = jnp.logical_not(at_end)
-    lower = chip == 1
-    outer_of = {"wide": jnp.where(lower, me - 2, lax.rem(me + 2, wide))}
-    inner_of = {"wide": jnp.where(lower, me + 2, lax.rem(me + wide - 2, wide))}
-    end_of = {"wide": jnp.where(at_bottom, me + 2, lax.rem(me + wide - 2, wide))}
-    inner = heads * HEAD_DIM
-    kinds = gradient_kinds(d_model, inner, ff)
-    targets = (up_out, down_out, dense_out, qkv_out)
-    operands = (
-        (norm_hbm.at[1], dpre_hbm),
-        (hid_hbm, g_hbm),
-        (mixed_hbm, g_hbm),
-        (norm_hbm.at[0], dpk_hbm),
-    )
-    ranges, first = [], 0
-    for height, width in kinds:
-        count = (height // TILE) * (width // (2 * TILE))
-        ranges.append((first, first + count, width // (2 * TILE)))
-        first += count
-    steps = first
-
-    def remote(src, dst, ss, rs, dev):
-        return pltpu.make_async_remote_copy(
-            src_ref=src, dst_ref=dst, send_sem=ss, recv_sem=rs, device_id=dev, device_id_type=MESH
-        )
-
-    def arrived(ref, sem):
-        pltpu.make_async_copy(ref, ref, sem).wait()
-
-    tile_ref = tot.at[0]
-
-    def by_kind(m, body):
-        for kind, (low, high, across) in enumerate(ranges):
-
-            @pl.when((m >= low) & (m < high))
-            def _(kind=kind, low=low, across=across):
-                at = m - low
-                body(kind, at // across, lax.rem(at, across))
-
-    def tile_of(kind, row, col, which):
-        return targets[kind].at[
-            pl.ds(pl.multiple_of(row * TILE, TILE), TILE),
-            pl.ds(pl.multiple_of((2 * col + which) * TILE, TILE), TILE),
-        ]
-
-    def fetch(m):
-        def body(kind, row, col):
-            left, right = operands[kind]
-            slot = lax.rem(m, 2)
-            pltpu.make_async_copy(
-                left.at[:, pl.ds(pl.multiple_of(row * TILE, TILE), TILE)],
-                left_op.at[slot],
-                op_sem.at[0, slot],
-            ).start()
-            pltpu.make_async_copy(
-                right.at[:, pl.ds(pl.multiple_of(col * 2 * TILE, 2 * TILE), 2 * TILE)],
-                right_op.at[slot],
-                op_sem.at[1, slot],
-            ).start()
-
-        by_kind(m, body)
-
-    def is_root(m):
-        return middle & (chip == 1 + lax.rem(m, 2))
-
-    def products(m):
-        slot, ring = lax.rem(m, 2), lax.rem(m, RING)
-        arrived(left_op.at[slot], op_sem.at[0, slot])
-        arrived(right_op.at[slot], op_sem.at[1, slot])
-        left = left_op[slot]
-        mine = pl.ds(pl.multiple_of(core * TILE, TILE), TILE)
-        other = pl.ds(pl.multiple_of((1 - core) * TILE, TILE), TILE)
-
-        @pl.when(m >= RING)
-        def _():
-            arrived(tile_ref, core_ss.at[ring])
-            pl.semaphore_wait(core_free, 1)
-
-        core_st[ring] = t_dot(left, right_op[slot, :, other]).astype(BF16)
-        remote(
-            core_st.at[ring], core_r.at[ring], core_ss.at[ring], core_rs.at[ring], partner
-        ).start()
-        own[ring] = t_dot(left, right_op[slot, :, mine])
-
-    def send_red(m, value, target, sem, dev, free):
-        ring = lax.rem(m, RING)
-
-        @pl.when(m >= RING)
-        def _():
-            pl.semaphore_wait(free, 1)
-
-        red_st[ring] = value.astype(BF16)
-        remote(red_st.at[ring], target.at[ring], red_ss.at[ring], sem.at[ring], dev).start()
-
-    def chip_sum(m):
-        ring = lax.rem(m, RING)
-        arrived(tile_ref, core_rs.at[ring])
-        total = own[ring] + core_r[ring].astype(F32)
-
-        @pl.when(m + RING < steps)
-        def _():
-            pl.semaphore_signal(core_free, inc=1, device_id=partner, device_id_type=MESH)
-
-        @pl.when(at_end)
-        def _():
-            @pl.when(m >= RING)
-            def _():
-                arrived(tile_ref, red_ss.at[ring])
-
-            send_red(m, total, outer_r, outer_rs, end_of, outer_free.at[lax.rem(m, 2)])
-
-        @pl.when(middle)
-        def _():
-            own[ring] = total
-
-    def take_outer(m):
-        ring = lax.rem(m, RING)
-        arrived(tile_ref, outer_rs.at[ring])
-        total = own[ring] + outer_r[ring].astype(F32)
-
-        @pl.when(m + RING < steps)
-        def _():
-            pl.semaphore_signal(
-                outer_free.at[lax.rem(m, 2)], inc=1, device_id=outer_of, device_id_type=MESH
-            )
-
-        return total
-
-    def pass_in(m):
-        ring = lax.rem(m, RING)
-        total = take_outer(m)
-
-        @pl.when(m >= RING)
-        def _():
-            arrived(tile_ref, red_ss.at[ring])
-
-        send_red(m, total, inner_r, inner_rs, inner_of, inner_free)
-
-    def finish(m):
-        ring = lax.rem(m, RING)
-        slot = lax.rem(m // 2, TOTALS)
-        total = take_outer(m)
-        arrived(tile_ref, inner_rs.at[ring])
-        total = total + inner_r[ring].astype(F32)
-
-        @pl.when(m + RING < steps)
-        def _():
-            pl.semaphore_signal(inner_free, inc=1, device_id=inner_of, device_id_type=MESH)
-
-        @pl.when(m >= 2 * TOTALS)
-        def _():
-            for k in range(4):
-                arrived(tile_ref, tot_ss.at[k, slot])
-
-        tot[slot] = total.astype(BF16)
-
-        def body(kind, row, col):
-            here = tile_of(kind, row, col, core)
-            remote(tot.at[slot], here, tot_ss.at[0, slot], bc_rs.at[m], outer_of).start()
-            remote(tot.at[slot], here, tot_ss.at[1, slot], bc_rs.at[m], inner_of).start()
-            remote(tot.at[slot], here, tot_ss.at[2, slot], fin_rs.at[kind], partner).start()
-            pltpu.make_async_copy(tot.at[slot], here, tot_ss.at[3, slot]).start()
-
-        by_kind(m, body)
-
-    def hand_on(m):
-        arrived(tile_ref, bc_rs.at[m])
-
-        def body(kind, row, col):
-            here = tile_of(kind, row, col, core)
-
-            @pl.when(middle)
-            def _():
-                remote(here, here, fwd_ss.at[m], bc_rs.at[m], outer_of).start()
-
-            remote(here, here, share_ss.at[m], fin_rs.at[kind], partner).start()
-
-        by_kind(m, body)
-
-    exchanges = (
-        {"tensor": 1 - tens},
-        partner,
-        {"wide": me + 2 - 4 * lax.rem(chip, 2)},
-        {"wide": me + 4 - 8 * (chip // 2)},
-    )
-
-    barrier = pltpu.get_barrier_semaphore()
-    for dev in exchanges:
-        pl.semaphore_signal(barrier, inc=1, device_id=dev, device_id_type=MESH)
-
-    @pl.when(middle)
-    def _():
-        pl.semaphore_signal(barrier, inc=1, device_id=inner_of, device_id_type=MESH)
-
-    fetch(jnp.int32(0))
-    sums[:, 0:d_model] = jnp.concatenate(
-        [jnp.sum(small[k], axis=0, keepdims=True) for k in range(5)]
-        + [jnp.zeros((3, d_model), F32)],
-        axis=0,
-    )
-    total = jnp.sum(biases[...], axis=0, keepdims=True)
-    lines = [total[:, k * COLS : (k + 1) * COLS] for k in range(total.shape[1] // COLS)]
-    lines.append(jnp.zeros((8 - len(lines), COLS), F32))
-    sums[:, d_model:] = jnp.concatenate(lines, axis=0)
-    pl.when(middle)(lambda: pl.semaphore_wait(barrier, len(exchanges) + 1))
-    pl.when(at_end)(lambda: pl.semaphore_wait(barrier, len(exchanges)))
-
-    def exchange_start(k):
-        if k > 0:
-            arrived(sums, sum_ss.at[0])
-        sums_r[0] = sums[...]
-        remote(sums_r.at[0], sums_r.at[k + 1], sum_ss.at[0], sum_rs.at[k], exchanges[k]).start()
-
-    def exchange_end(k):
-        arrived(sums, sum_rs.at[k])
-        if k == 0:
-            sums[:, 0:d_model] += sums_r[1, :, 0:d_model]
-        else:
-            sums[...] += sums_r[k + 1]
-
-    def step(i, carry):
-        pl.when(i + 1 < steps)(lambda: fetch(i + 1))
-        pl.when(i < steps)(lambda: products(i))
-        for k in range(4):
-            pl.when(i == 4 * k + 2)(lambda k=k: exchange_start(k))
-            pl.when(i == 4 * k + 5)(lambda k=k: exchange_end(k))
-
-        def at(lag, allowed, body):
-            m = i - lag
-            pl.when((m >= 0) & (m < steps) & allowed(m))(lambda: body(m))
-
-        at(1, lambda m: m >= 0, chip_sum)
-        at(3, lambda m: middle & jnp.logical_not(is_root(m)), pass_in)
-        at(5, is_root, finish)
-        at(8, lambda m: middle & jnp.logical_not(is_root(m)), hand_on)
-        at(10, lambda m: at_end, hand_on)
-        return carry
-
-    lax.fori_loop(0, steps + 10, step, 0)
-
-    arrived(sums, sum_ss.at[0])
-    for ring in range(RING):
-        arrived(tile_ref, core_ss.at[ring])
-
-    def drain(m, carry):
-        ring = lax.rem(m, RING)
-        root = is_root(m)
-        last = m + RING >= steps
-        pl.when(at_end & last)(lambda: arrived(tile_ref, red_ss.at[ring]))
-        pl.when(middle & jnp.logical_not(root) & last)(
-            lambda: arrived(tile_ref, red_ss.at[ring])
-        )
-
-        @pl.when(root & (m + 2 * TOTALS >= steps))
-        def _():
-            for k in range(4):
-                arrived(tile_ref, tot_ss.at[k, lax.rem(m // 2, TOTALS)])
-
-        @pl.when(middle & jnp.logical_not(root))
-        def _():
-            arrived(tile_ref, fwd_ss.at[m])
-
-        pl.when(jnp.logical_not(root))(lambda: arrived(tile_ref, share_ss.at[m]))
-        return carry
-
-    lax.fori_loop(0, steps, drain, 0)
-    for kind, (height, width) in enumerate(kinds):
-        arrived(targets[kind].at[pl.ds(0, height // 2)], fin_rs.at[kind])
-
-
-def gradient_sums(dims, operands, small, biases, collective_id):
-    micro, rows, group, wide, heads, d_model, ff = dims
-    inner = heads * HEAD_DIM
-    kinds = gradient_kinds(d_model, inner, ff)
-    steps = sum((height // TILE) * (width // (2 * TILE)) for height, width in kinds)
-    count = micro * group
-    anywhere = pl.BlockSpec(memory_space=pl.ANY)
-    local = pl.BlockSpec(memory_space=pltpu.VMEM)
-    dma = pltpu.SemaphoreType.DMA
-    regular = pltpu.SemaphoreType.REGULAR
-    vmem = pltpu.VMEM
-    width = d_model + COLS
-    return pl.pallas_call(
-        functools.partial(gradient_kernel, dims),
-        out_shape=[jax.ShapeDtypeStruct(kind, BF16) for kind in kinds]
-        + [jax.ShapeDtypeStruct((8, width), F32)],
-        in_specs=[anywhere] * 6 + [local] * 2,
-        out_specs=[anywhere] * 4 + [local],
-        scratch_shapes=[
-            vmem((2, count, TILE), BF16),
-            vmem((2, count, 2 * TILE), BF16),
-            vmem((RING, TILE, TILE), F32),
-            vmem((RING, TILE, TILE), BF16),
-            vmem((RING, TILE, TILE), BF16),
-            vmem((RING, TILE, TILE), BF16),
-            vmem((RING, TILE, TILE), BF16),
-            vmem((RING, TILE, TILE), BF16),
-            vmem((TOTALS, TILE, TILE), BF16),
-            vmem((5, 8, width), F32),
-            dma((2, 2)),
-            dma((RING,)),
-            dma((RING,)),
-            dma((RING,)),
-            dma((RING,)),
-            dma((RING,)),
-            dma((steps,)),
-            dma((4, TOTALS)),
-            dma((steps,)),
-            dma((steps,)),
-            dma((4,)),
-            dma((1,)),
-            dma((4,)),
-            regular,
-            regular((2,)),
-            regular,
-        ],
-        compiler_params=pltpu.CompilerParams(
-            collective_id=collective_id, has_side_effects=True, vmem_limit_bytes=40 << 20
-        ),
-        name="gradient_sums",
-    )(*operands, small, biases)
+    )
 
 
 def relay_shards(
@@ -1260,11 +1224,8 @@
     heads = qkv_weight.shape[2] // (3 * HEAD_DIM)
     ff = up_weight.shape[2]
     dims = (micro, rows, group, wide, heads, d_model, ff)
-    out, input_grad, *operands, small, bias_sums = relay(
+    out, input_grad, *_, up_grad, down_grad, dense_grad, qkv_grad, sums = relay(
         dims, doc_lengths, block_input, cotangent, weights, 1
-    )
-    up_grad, down_grad, dense_grad, qkv_grad, sums = gradient_sums(
-        dims, operands, small, bias_sums, 2
     )
     up_grad, down_grad, dense_grad, qkv_grad = (
         grad.astype(F32)[None] for grad in (up_grad, down_grad, dense_grad, qkv_grad)
@@ -1749,9 +1710,12 @@
 
     def program(*args):
         heads = args[4].shape[2] // (3 * HEAD_DIM * mesh.shape["tensor"])
-        one_head_each = heads == mesh.shape["wide"] and heads % 2 == 0
-        two_by_two = mesh.shape["section"] == 2 and mesh.shape["tensor"] == 2
-        body = relay_shards if one_head_each and two_by_two else general_shards
+        micro, seq_len, d_model = args[0].shape
+        group = seq_len // mesh.shape["wide"]
+        fits = heads == mesh.shape["wide"] == 8
+        fits = fits and mesh.shape["section"] == 2 and mesh.shape["tensor"] == 2
+        fits = fits and micro * group == d_model and args[8].shape[2] == 4 * d_model
+        body = relay_shards if fits and group == TILE else general_shards
         return jax.shard_map(
             body, mesh=mesh, in_specs=placed, out_specs=results, check_vma=False
         )(*args)

time: 538 us -> 504 us (0.937)
  Pallas kernels: 494 us -> 474 us
  local copies, waits for them, and re-layouts: 16.6 us -> 7.23 us
    pallas_call x1 -> x0, Pallas kernels: 167 us -> none  [gradient_sums(): pl.pallas_call(functools.partial(gradient_kernel, dims), out_shape=[jax.S...]
    pallas_call x1, Pallas kernels: 327 us -> 474 us  [relay(): pl.pallas_call(functools.partial(relay_kernel, dims), out_shape=outs, in_...]
    unnamed x27 -> x17, local copies, waits for them, and re-layouts: 9.44 us -> 3.68 us
where the time goes in v5:
time: 504 us; the launch traced here: 497 us
  Pallas kernels  474 us (94%)
  other arithmetic  15.3 us (3%)
  local copies, waits for them, and re-layouts  7.23 us (1%)
    pallas_call x1, Pallas kernels, relay(): pl.pallas_call(functools.partial(relay_kernel, dims), out_shape=outs, in_...  474 us
    broadcast_in_dim x4, other arithmetic, relay_shards(): grad.astype(F32)[None]  15.3 us

profile of v5, /device:TPU:0, one launch (start us, length us, event | category | flops | bytes accessed | tf_op | source)
XLA Modules:
  0.0 497.3 jit_solution(3772359844393273592)
XLA Ops:
  0.6 473.9 %relay.1 = (bf16[4,128,1024]{2,1,0:T(8,128)(2,1)}, f32[4,128,1024]{2,1,0:T(8,128)}, bf16[2,1024,1024]{2,1,0:T(8,128)(2,1)}, bf16[1024,1024]{1,0:T(8,128)(2,1)}, ...) custom-call(s32[4,8]{1,0:T(4,128)} %lengths.1, ...), custom_call_target="tpu_custom_call" | custom-call | tf_op jit(solution)/shard_map/relay/pallas_call | solution.py:1164
  474.6 0.0 copy-start.2
  474.6 0.9 slice.22
  475.5 0.0 copy-start.5
  475.5 0.8 slice_bitcast_fusion
  476.3 1.4 slice_bitcast_fusion.1
  477.7 0.6 slice.24
  478.3 0.6 slice.25
  478.9 2.8 bitcast_convert_fusion.3
  481.7 0.0 copy-done.2
  481.7 0.0 copy-start.1
  481.7 3.6 bitcast_convert_fusion.2
  485.3 0.0 copy-done.1
  485.3 0.0 copy-start
  485.3 4.4 bitcast_convert_fusion.1
  489.8 0.0 copy-done
  489.8 0.0 copy-start.4
  489.8 0.0 copy-start.3
  489.8 4.4 bitcast_convert_fusion
  494.2 0.0 copy-done.5
  494.2 0.6 copy.29
  494.8 0.0 copy-done.4
  494.8 1.0 copy.30
  495.8 0.0 copy-done.3
  495.8 1.3 copy.31
  (1 shorter events, 0.0 us)
Async XLA Ops:
  474.6 7.1 %copy-start.2 = (bf16[1024,1536]{1,0:T(8,128)(2,1)S(1)}, bf16[1024,1536]{1,0:T(8,128)(2,1)}, u32[]{:S(2)}) copy-start(bf16[1024,1536]{1,0:T(8,128)(2,1)} %get-tuple-element.22) | copy-start | bytes 9437188
  475.5 18.7 %copy-start.5 = (f32[1,1024]{1,0:T(1,128)}, f32[1,1024]{1,0:T(1,128)S(1)}, u32[]{:S(2)}) copy-start(f32[1,1024]{1,0:T(1,128)S(1)} %slice.22) | copy-start | bytes 12292
  481.7 3.6 copy-start.1
  485.3 4.5 copy-start
  489.8 5.0 %copy-start.4 = (bf16[4,128,1024]{2,1,0:T(8,128)(2,1)S(1)}, bf16[4,128,1024]{2,1,0:T(8,128)(2,1)}, u32[]{:S(2)}) copy-start(bf16[4,128,1024]{2,1,0:T(8,128)(2,1)} %get-tuple-element.19) | copy-start | bytes 3145732
  489.8 6.0 %copy-start.3 = (f32[4,128,1024]{2,1,0:T(8,128)S(1)}, f32[4,128,1024]{2,1,0:T(8,128)}, u32[]{:S(2)}) copy-start(f32[4,128,1024]{2,1,0:T(8,128)} %get-tuple-element.20) | copy-start | bytes 6291460

commit v6 on v5

--- a/solution.py
+++ b/solution.py
@@ -31,8 +31,10 @@
 AHEAD = 3
 RING = 8
 TOTALS = 8
-LAGS = (1, 3, 5, 8, 10)
-EARLY = 16
+LAGS = (2, 5, 8, 12, 15)
+OWN = 16
+GUESTS = 10
+EARLY = 24
 
 
 def gradient_kinds(d_model, inner, ff):
@@ -97,6 +99,7 @@
     down_out,
     dense_out,
     qkv_out,
+    guest_hbm,
     sums,
     small,
     bias_sums,
@@ -170,6 +173,7 @@
     core_r,
     outer_r,
     inner_r,
+    turned,
     sums_r,
     op_sem,
     core_ss,
@@ -184,6 +188,8 @@
     fin_rs,
     sum_ss,
     sum_rs,
+    guest_ss,
+    guest_rs,
     core_free,
     outer_free,
     inner_free,
@@ -686,6 +692,11 @@
 
         lax.fori_loop(0, rows // 32, in_step, 0, unroll=True)
 
+        @pl.when(s == micro - 1)
+        def _():
+            for k in range(micro):
+                arrived(xfull.at[k, my_rows], yx_s.at[k])
+
         @pl.when(sect == 1)
         def _():
             remote(gx_st, gfull.at[s, my_rows], gs_ss.at[0], owng_sem.at[s], x_dev).start()
@@ -719,7 +730,17 @@
     steps = first
 
     def own_at(ring):
-        return scores.at[0:TILE, pl.ds(pl.multiple_of(ring * ACROSS, ACROSS), ACROSS)]
+        rows_at = pl.ds(pl.multiple_of((ring // RING) * TILE, TILE), TILE)
+        return scores.at[
+            rows_at, pl.ds(pl.multiple_of(lax.rem(ring, RING) * ACROSS, ACROSS), ACROSS)
+        ]
+
+    def guest_at(number):
+        cols = pl.ds(pl.multiple_of(lax.rem(number, 4) * ACROSS, ACROSS), ACROSS)
+        return xfull.at[number // 4, :, cols]
+
+    def guest_st_at(slot):
+        return mixed_st.at[:, pl.ds(pl.multiple_of(slot * ACROSS, ACROSS), ACROSS)]
 
     def core_st_at(ring):
         return hid_st.at[:, pl.ds(pl.multiple_of(ring * ACROSS, ACROSS), ACROSS)]
@@ -762,11 +783,15 @@
         def body(kind, row, col):
             left, right = operands[kind]
             slot = lax.rem(m, AHEAD + 1)
-            pltpu.make_async_copy(
-                left.at[:, pl.ds(pl.multiple_of(row * TILE, TILE), TILE)],
-                left_at(slot),
-                op_sem.at[0, slot],
-            ).start()
+
+            @pl.when(col == 0)
+            def _():
+                pltpu.make_async_copy(
+                    left.at[:, pl.ds(pl.multiple_of(row * TILE, TILE), TILE)],
+                    left_at(slot),
+                    op_sem.at[0, slot],
+                ).start()
+
             pltpu.make_async_copy(
                 right.at[:, pl.ds(pl.multiple_of(col * 2 * ACROSS, 2 * ACROSS), 2 * ACROSS)],
                 right_at(slot),
@@ -775,27 +800,44 @@
 
         by_kind(m, body)
 
-    def is_root(m):
-        return middle & (chip == 1 + lax.rem(m, 2))
+    chain = jnp.where(sect == 1, steps + GUESTS, steps - GUESTS)
+
+    def place(m):
+        shared = (sect == 0) & (m < 2 * GUESTS)
+        away = shared & (lax.rem(m, 2) == 1)
+        visitor = (sect == 1) & (m >= steps)
+        n = jnp.where(shared, m // 2, jnp.where(sect == 0, m - GUESTS, m))
+        number = jnp.where(visitor, m - steps, m // 2)
+        tile = jnp.where(visitor, 2 * (m - steps) + 1, m)
+        return away, visitor, n, number, tile
+
+    def is_root(n):
+        return middle & (chip == 1 + lax.rem(n, 2))
 
     def products(m):
         slot, ring = lax.rem(m, AHEAD + 1), lax.rem(m, RING)
-        arrived(left_at(slot), op_sem.at[0, slot])
+
+        def body(kind, row, col):
+            @pl.when(col == 0)
+            def _():
+                arrived(left_at(slot), op_sem.at[0, slot])
+                turned[...] = left_at(slot)[...].T
+
+        by_kind(m, body)
         arrived(right_at(slot), op_sem.at[1, slot])
-        left, right = left_at(slot), right_at(slot)
-        mine = pl.ds(pl.multiple_of(core * ACROSS, ACROSS), ACROSS)
-        other = pl.ds(pl.multiple_of((1 - core) * ACROSS, ACROSS), ACROSS)
+        both = dot(turned[...], right_at(slot)[...])
+        first, second = both[:, :ACROSS], both[:, ACROSS:]
+        own_at(lax.rem(m, OWN))[...] = jnp.where(core == 0, first, second)
 
         @pl.when(m >= RING)
         def _():
             arrived(tile_ref, core_ss.at[ring])
             pl.semaphore_wait(core_free, 1)
 
-        core_st_at(ring)[...] = t_dot(left[...], right[:, other]).astype(BF16)
+        core_st_at(ring)[...] = jnp.where(core == 0, second, first).astype(BF16)
         remote(
             core_st_at(ring), core_r.at[ring], core_ss.at[ring], core_rs.at[ring], partner
         ).start()
-        own_at(ring)[...] = t_dot(left[...], right[:, mine])
 
     def send_red(m, value, target, sem, dev, free):
         ring = lax.rem(m, RING)
@@ -808,89 +850,139 @@
         remote(red_st_at(ring), target.at[ring], red_ss.at[ring], sem.at[ring], dev).start()
 
     def chip_sum(m):
+        away, visitor, n, number, _ = place(m)
         ring = lax.rem(m, RING)
-        arrived(tile_ref, core_rs.at[ring])
-        total = own_at(ring)[...] + core_r[ring].astype(F32)
-
-        @pl.when(m + RING < steps)
-        def _():
-            pl.semaphore_signal(core_free, inc=1, device_id=partner, device_id_type=MESH)
-
-        @pl.when(at_end)
-        def _():
-            @pl.when(m >= RING)
+        own = own_at(lax.rem(m, OWN))
+
+        @pl.when(visitor)
+        def _():
+            arrived(tile_ref, guest_rs.at[number])
+            own[...] = guest_at(number)[...].astype(F32)
+
+        @pl.when(jnp.logical_not(visitor))
+        def _():
+            arrived(tile_ref, core_rs.at[ring])
+            own[...] = own[...] + core_r[ring].astype(F32)
+
+            @pl.when(m + RING < steps)
             def _():
-                arrived(tile_ref, red_ss.at[ring])
-
-            send_red(m, total, outer_r, outer_rs, end_of, outer_free.at[lax.rem(m, 2)])
-
-        @pl.when(middle)
-        def _():
-            own_at(ring)[...] = total
-
-    def take_outer(m):
-        ring = lax.rem(m, RING)
+                pl.semaphore_signal(core_free, inc=1, device_id=partner, device_id_type=MESH)
+
+        @pl.when(away)
+        def _():
+            slot = lax.rem(number, 2)
+            pl.when(number >= 2)(lambda: arrived(tile_ref, guest_ss.at[slot]))
+            guest_st_at(slot)[...] = own[...].astype(BF16)
+            remote(
+                guest_st_at(slot),
+                guest_at(number),
+                guest_ss.at[slot],
+                guest_rs.at[number],
+                x_dev,
+            ).start()
+
+        @pl.when(at_end & jnp.logical_not(away))
+        def _():
+            pl.when(n >= RING)(lambda: arrived(tile_ref, red_ss.at[lax.rem(n, RING)]))
+            send_red(n, own[...], outer_r, outer_rs, end_of, outer_free.at[lax.rem(n, 2)])
+
+    def take_outer(m, n):
+        ring = lax.rem(n, RING)
         arrived(tile_ref, outer_rs.at[ring])
-        total = own_at(ring)[...] + outer_r[ring].astype(F32)
-
-        @pl.when(m + RING < steps)
+        total = own_at(lax.rem(m, OWN))[...] + outer_r[ring].astype(F32)
+
+        @pl.when(n + RING < chain)
         def _():
             pl.semaphore_signal(
-                outer_free.at[lax.rem(m, 2)], inc=1, device_id=outer_of, device_id_type=MESH
+                outer_free.at[lax.rem(n, 2)], inc=1, device_id=outer_of, device_id_type=MESH
             )
 
         return total
 
     def pass_in(m):
-        ring = lax.rem(m, RING)
-        total = take_outer(m)
-
-        @pl.when(m >= RING)
-        def _():
-            arrived(tile_ref, red_ss.at[ring])
-
-        send_red(m, total, inner_r, inner_rs, inner_of, inner_free)
+        _, _, n, _, _ = place(m)
+        total = take_outer(m, n)
+        pl.when(n >= RING)(lambda: arrived(tile_ref, red_ss.at[lax.rem(n, RING)]))
+        send_red(n, total, inner_r, inner_rs, inner_of, inner_free)
 
     def finish(m):
-        ring = lax.rem(m, RING)
-        slot = lax.rem(m // 2, TOTALS)
-        total = take_outer(m)
+        _, visitor, n, number, tile = place(m)
+        ring = lax.rem(n, RING)
+        slot = lax.rem(n // 2, TOTALS)
+        total = take_outer(m, n)
         arrived(tile_ref, inner_rs.at[ring])
         total = total + inner_r[ring].astype(F32)
 
-        @pl.when(m + RING < steps)
+        @pl.when(n + RING < chain)
         def _():
             pl.semaphore_signal(inner_free, inc=1, device_id=inner_of, device_id_type=MESH)
 
-        @pl.when(m >= 2 * TOTALS)
+        @pl.when(n >= 2 * TOTALS)
         def _():
             for k in range(4):
                 arrived(tile_ref, tot_ss.at[k, slot])
 
         tot_at(slot)[...] = total.astype(BF16)
 
+        def send(here):
+            remote(tot_at(slot), here, tot_ss.at[0, slot], bc_rs.at[m], outer_of).start()
+            remote(tot_at(slot), here, tot_ss.at[1, slot], bc_rs.at[m], inner_of).start()
+            pltpu.make_async_copy(tot_at(slot), here, tot_ss.at[3, slot]).start()
+
         def body(kind, row, col):
             here = tile_of(kind, row, col, core)
-            remote(tot_at(slot), here, tot_ss.at[0, slot], bc_rs.at[m], outer_of).start()
-            remote(tot_at(slot), here, tot_ss.at[1, slot], bc_rs.at[m], inner_of).start()
-            remote(tot_at(slot), here, tot_ss.at[2, slot], fin_rs.at[kind], partner).start()
-            pltpu.make_async_copy(tot_at(slot), here, tot_ss.at[3, slot]).start()
-
-        by_kind(m, body)
+
+            @pl.when(visitor)
+            def _():
+                send(guest_hbm.at[number])
+                remote(tot_at(slot), here, tot_ss.at[2, slot], bc_rs.at[tile], x_dev).start()
+
+            @pl.when(jnp.logical_not(visitor))
+            def _():
+                send(here)
+                remote(
+                    tot_at(slot), here, tot_ss.at[2, slot], fin_rs.at[kind], partner
+                ).start()
+
+        by_kind(tile, body)
 
     def hand_on(m):
+        _, visitor, _, number, tile = place(m)
         arrived(tile_ref, bc_rs.at[m])
 
         def body(kind, row, col):
             here = tile_of(kind, row, col, core)
 
-            @pl.when(middle)
+            @pl.when(visitor)
             def _():
-                remote(here, here, fwd_ss.at[m], bc_rs.at[m], outer_of).start()
-
+                held = guest_hbm.at[number]
+
+                @pl.when(middle)
+                def _():
+                    remote(held, held, fwd_ss.at[m], bc_rs.at[m], outer_of).start()
+
+                remote(held, here, share_ss.at[m], bc_rs.at[tile], x_dev).start()
+
+            @pl.when(jnp.logical_not(visitor))
+            def _():
+                @pl.when(middle)
+                def _():
+                    remote(here, here, fwd_ss.at[m], bc_rs.at[m], outer_of).start()
+
+                remote(here, here, share_ss.at[m], fin_rs.at[kind], partner).start()
+
+        by_kind(tile, body)
+
+    def guest_home(number, carry):
+        m = 2 * number + 1
+        arrived(tile_ref, bc_rs.at[m])
+
+        def body(kind, row, col):
+            here = tile_of(kind, row, col, core)
             remote(here, here, share_ss.at[m], fin_rs.at[kind], partner).start()
 
         by_kind(m, body)
+        return carry
 
     exchanges = (
         {"tensor": 1 - tens},
@@ -934,13 +1026,18 @@
 
         def late(lag, allowed, body):
             m = i - lag
-            pl.when((m >= 0) & (m < steps) & allowed(m))(lambda: body(m))
-
-        late(LAGS[0], lambda m: m >= 0, chip_sum)
-        late(LAGS[1], lambda m: middle & jnp.logical_not(is_root(m)), pass_in)
-        late(LAGS[2], is_root, finish)
-        late(LAGS[3], lambda m: middle & jnp.logical_not(is_root(m)), hand_on)
-        late(LAGS[4], lambda m: at_end, hand_on)
+            away, _, n, _, _ = place(m)
+            inside = (m >= 0) & (m < jnp.where(sect == 1, steps + GUESTS, steps))
+            pl.when(inside & allowed(away, n))(lambda: body(m))
+
+        def outside(away, n):
+            return middle & jnp.logical_not(away | is_root(n))
+
+        late(LAGS[0], lambda away, n: n >= 0, chip_sum)
+        late(LAGS[1], outside, pass_in)
+        late(LAGS[2], lambda away, n: is_root(n) & jnp.logical_not(away), finish)
+        late(LAGS[3], outside, hand_on)
+        late(LAGS[4], lambda away, n: at_end & jnp.logical_not(away), hand_on)
         return carry
 
     def gradient_begin():
@@ -989,7 +1086,9 @@
         pl.when(starts)(gradient_begin)
         low = jnp.where(goes_on, EARLY, 0)
         high = jnp.where(
-            goes_on | (starts & (sect == 1)), steps + LAGS[4], jnp.where(starts, EARLY, 0)
+            goes_on | (starts & (sect == 1)),
+            steps + LAGS[4] + jnp.where(sect == 1, GUESTS, 0),
+            jnp.where(starts, EARLY, 0),
         )
         lax.fori_loop(low, high, gradient_step, 0)
         return carry
@@ -997,7 +1096,6 @@
     lax.fori_loop(0, jnp.where(sect == 1, micro + 1, 2 * micro + 1), step, 0)
 
     for s in range(micro):
-        arrived(xfull.at[s, my_rows], yx_s.at[s])
         arrived(gfull.at[s, my_rows], yg_s.at[s])
     arrived(out_st, store_sem.at[4])
     arrived(ig_st, store_sem.at[8])
@@ -1008,28 +1106,33 @@
     for ring in range(RING):
         arrived(tile_ref, core_ss.at[ring])
 
+    @pl.when(sect == 0)
+    def _():
+        lax.fori_loop(0, GUESTS, guest_home, 0)
+        for slot in range(2):
+            arrived(tile_ref, guest_ss.at[slot])
+
     def drain(m, carry):
-        ring = lax.rem(m, RING)
-        root = is_root(m)
-        last = m + RING >= steps
-        pl.when(at_end & last)(lambda: arrived(tile_ref, red_ss.at[ring]))
-        pl.when(middle & jnp.logical_not(root) & last)(
-            lambda: arrived(tile_ref, red_ss.at[ring])
-        )
-
-        @pl.when(root & (m + 2 * TOTALS >= steps))
+        away, _, n, _, _ = place(m)
+        root = is_root(n)
+        stays = jnp.logical_not(away)
+        ring = lax.rem(n, RING)
+        sends = at_end | (middle & jnp.logical_not(root))
+        pl.when(stays & sends & (n + RING >= chain))(lambda: arrived(tile_ref, red_ss.at[ring]))
+
+        @pl.when(stays & root & (n + 2 * TOTALS >= chain))
         def _():
             for k in range(4):
-                arrived(tile_ref, tot_ss.at[k, lax.rem(m // 2, TOTALS)])
-
-        @pl.when(middle & jnp.logical_not(root))
+                arrived(tile_ref, tot_ss.at[k, lax.rem(n // 2, TOTALS)])
+
+        @pl.when(stays & middle & jnp.logical_not(root))
         def _():
             arrived(tile_ref, fwd_ss.at[m])
 
-        pl.when(jnp.logical_not(root))(lambda: arrived(tile_ref, share_ss.at[m]))
+        pl.when(away | jnp.logical_not(root))(lambda: arrived(tile_ref, share_ss.at[m]))
         return carry
 
-    lax.fori_loop(0, steps, drain, 0)
+    lax.fori_loop(0, jnp.where(sect == 1, steps + GUESTS, steps), drain, 0)
     for kind, (height, width) in enumerate(kinds):
         arrived(targets[kind].at[pl.ds(0, height // 2)], fin_rs.at[kind])
 
@@ -1068,6 +1171,7 @@
     kinds = gradient_kinds(d_model, inner, ff)
     steps = sum((height // TILE) * (width // (2 * ACROSS)) for height, width in kinds)
     outs += [jax.ShapeDtypeStruct(kind, BF16) for kind in kinds]
+    outs += [jax.ShapeDtypeStruct((GUESTS, TILE, ACROSS), BF16)]
     outs += [jax.ShapeDtypeStruct((8, d_model + COLS), F32)]
     regular = pltpu.SemaphoreType.REGULAR
     scratch = [
@@ -1143,6 +1247,7 @@
         vmem((RING, TILE, ACROSS), BF16),
         vmem((RING, TILE, ACROSS), BF16),
         vmem((RING, TILE, ACROSS), BF16),
+        vmem((TILE, micro * group), BF16),
         vmem((5, 8, d_model + COLS), F32),
         dma((2, AHEAD + 1)),
         dma((RING,)),
@@ -1150,13 +1255,15 @@
         dma((RING,)),
         dma((RING,)),
         dma((RING,)),
-        dma((steps,)),
+        dma((steps + GUESTS,)),
         dma((4, TOTALS)),
-        dma((steps,)),
-        dma((steps,)),
+        dma((steps + GUESTS,)),
+        dma((steps + GUESTS,)),
         dma((4,)),
         dma((1,)),
         dma((4,)),
+        dma((2,)),
+        dma((GUESTS,)),
         regular,
         regular((2,)),
         regular,
@@ -1165,7 +1272,7 @@
         functools.partial(relay_kernel, dims),
         out_shape=outs,
         in_specs=[scalars, anywhere, anywhere] + [local] * 6 + [anywhere] * 4,
-        out_specs=[anywhere] * 12 + [local],
+        out_specs=[anywhere] * 13 + [local],
         scratch_shapes=scratch,
         compiler_params=pltpu.CompilerParams(
             collective_id=collective_id, has_side_effects=True, vmem_limit_bytes=63 << 20
@@ -1224,7 +1331,7 @@
     heads = qkv_weight.shape[2] // (3 * HEAD_DIM)
     ff = up_weight.shape[2]
     dims = (micro, rows, group, wide, heads, d_model, ff)
-    out, input_grad, *_, up_grad, down_grad, dense_grad, qkv_grad, sums = relay(
+    out, input_grad, *_, up_grad, down_grad, dense_grad, qkv_grad, _, sums = relay(
         dims, doc_lengths, block_input, cotangent, weights, 1
     )
     up_grad, down_grad, dense_grad, qkv_grad = (

time: 504 us -> 482 us (0.956)
  Pallas kernels: 474 us -> 450 us
    pallas_call x1, Pallas kernels: 474 us -> 450 us  [relay(): pl.pallas_call(functools.partial(relay_kernel, dims), out_shape=outs, in_...]
where the time goes in v6:
time: 482 us; the launch traced here: 474 us
  Pallas kernels  450 us (93%)
  other arithmetic  15.3 us (3%)
  local copies, waits for them, and re-layouts  7.23 us (2%)
    pallas_call x1, Pallas kernels, relay(): pl.pallas_call(functools.partial(relay_kernel, dims), out_shape=outs, in_...  450 us
    broadcast_in_dim x4, other arithmetic, relay_shards(): grad.astype(F32)[None]  15.3 us

profile of v6, /device:TPU:0, one launch (start us, length us, event | category | flops | bytes accessed | tf_op | source)
XLA Modules:
  0.0 473.5 jit_solution(15844949610182131516)
XLA Ops:
  0.6 450.2 %relay.1 = (bf16[4,128,1024]{2,1,0:T(8,128)(2,1)}, f32[4,128,1024]{2,1,0:T(8,128)}, bf16[2,1024,1024]{2,1,0:T(8,128)(2,1)}, bf16[1024,1024]{1,0:T(8,128)(2,1)}, ...) custom-call(s32[4,8]{1,0:T(4,128)} %lengths.1, ...), custom_call_target="tpu_custom_call" | custom-call | tf_op jit(solution)/shard_map/relay/pallas_call | solution.py:1271
  450.8 0.0 copy-start.2
  450.9 0.9 slice.22
  451.8 0.0 copy-start.5
  451.8 0.8 slice_bitcast_fusion
  452.5 1.4 slice_bitcast_fusion.1
  454.0 0.6 slice.24
  454.6 0.6 slice.25
  455.2 2.8 bitcast_convert_fusion.3
  458.0 0.0 copy-done.2
  458.0 0.0 copy-start.1
  458.0 3.6 bitcast_convert_fusion.2
  461.6 0.0 copy-done.1
  461.6 0.0 copy-start
  461.6 4.4 bitcast_convert_fusion.1
  466.0 0.0 copy-done
  466.0 0.0 copy-start.4
  466.0 0.0 copy-start.3
  466.0 4.4 bitcast_convert_fusion
  470.5 0.0 copy-done.5
  470.5 0.6 copy.29
  471.1 0.0 copy-done.4
  471.1 1.0 copy.30
  472.0 0.0 copy-done.3
  472.0 1.3 copy.31
  (1 shorter events, 0.0 us)
Async XLA Ops:
  450.8 7.1 %copy-start.2 = (bf16[1024,1536]{1,0:T(8,128)(2,1)S(1)}, bf16[1024,1536]{1,0:T(8,128)(2,1)}, u32[]{:S(2)}) copy-start(bf16[1024,1536]{1,0:T(8,128)(2,1)} %get-tuple-element.22) | copy-start | bytes 9437188
  451.8 18.7 %copy-start.5 = (f32[1,1024]{1,0:T(1,128)}, f32[1,1024]{1,0:T(1,128)S(1)}, u32[]{:S(2)}) copy-start(f32[1,1024]{1,0:T(1,128)S(1)} %slice.22) | copy-start | bytes 12292
  458.0 3.6 copy-start.1
  461.6 4.5 copy-start
  466.0 5.0 %copy-start.4 = (bf16[4,128,1024]{2,1,0:T(8,128)(2,1)S(1)}, bf16[4,128,1024]{2,1,0:T(8,128)(2,1)}, u32[]{:S(2)}) copy-start(bf16[4,128,1024]{2,1,0:T(8,128)(2,1)} %get-tuple-element.19) | copy-start | bytes 3145732
  466.0 6.0 %copy-start.3 = (f32[4,128,1024]{2,1,0:T(8,128)S(1)}, f32[4,128,1024]{2,1,0:T(8,128)}, u32[]{:S(2)}) copy-start(f32[4,128,1024]{2,1,0:T(8,128)} %get-tuple-element.20) | copy-start | bytes 6291460

commit v7 on v6

--- a/solution.py
+++ b/solution.py
@@ -800,21 +800,24 @@
 
         by_kind(m, body)
 
+    total_steps = jnp.where(sect == 1, steps + GUESTS, steps)
     chain = jnp.where(sect == 1, steps + GUESTS, steps - GUESTS)
+    visit = ranges[2][0]
 
     def place(m):
         shared = (sect == 0) & (m < 2 * GUESTS)
         away = shared & (lax.rem(m, 2) == 1)
-        visitor = (sect == 1) & (m >= steps)
+        later = (sect == 1) & (m >= visit)
+        visitor = later & (m < visit + GUESTS)
         n = jnp.where(shared, m // 2, jnp.where(sect == 0, m - GUESTS, m))
-        number = jnp.where(visitor, m - steps, m // 2)
-        tile = jnp.where(visitor, 2 * (m - steps) + 1, m)
+        number = jnp.where(visitor, m - visit, m // 2)
+        tile = jnp.where(visitor, 2 * (m - visit) + 1, jnp.where(later, m - GUESTS, m))
         return away, visitor, n, number, tile
 
     def is_root(n):
         return middle & (chip == 1 + lax.rem(n, 2))
 
-    def products(m):
+    def products(step_at, m):
         slot, ring = lax.rem(m, AHEAD + 1), lax.rem(m, RING)
 
         def body(kind, row, col):
@@ -827,7 +830,7 @@
         arrived(right_at(slot), op_sem.at[1, slot])
         both = dot(turned[...], right_at(slot)[...])
         first, second = both[:, :ACROSS], both[:, ACROSS:]
-        own_at(lax.rem(m, OWN))[...] = jnp.where(core == 0, first, second)
+        own_at(lax.rem(step_at, OWN))[...] = jnp.where(core == 0, first, second)
 
         @pl.when(m >= RING)
         def _():
@@ -850,8 +853,8 @@
         remote(red_st_at(ring), target.at[ring], red_ss.at[ring], sem.at[ring], dev).start()
 
     def chip_sum(m):
-        away, visitor, n, number, _ = place(m)
-        ring = lax.rem(m, RING)
+        away, visitor, n, number, tile = place(m)
+        ring = lax.rem(tile, RING)
         own = own_at(lax.rem(m, OWN))
 
         @pl.when(visitor)
@@ -864,7 +867,7 @@
             arrived(tile_ref, core_rs.at[ring])
             own[...] = own[...] + core_r[ring].astype(F32)
 
-            @pl.when(m + RING < steps)
+            @pl.when(tile + RING < steps)
             def _():
                 pl.semaphore_signal(core_free, inc=1, device_id=partner, device_id_type=MESH)
 
@@ -1018,8 +1021,10 @@
             sums[...] += sums_r[k + 1]
 
     def gradient_step(i, carry):
-        pl.when(i + AHEAD < steps)(lambda: fetch(i + AHEAD))
-        pl.when(i < steps)(lambda: products(i))
+        _, visits, _, _, here_tile = place(i)
+        works = (i < total_steps) & jnp.logical_not(visits)
+        pl.when(works & (here_tile + AHEAD < steps))(lambda: fetch(here_tile + AHEAD))
+        pl.when(works)(lambda: products(i, here_tile))
         for k in range(4):
             pl.when(i == EARLY + 4 * k + 2)(lambda k=k: exchange_start(k))
             pl.when(i == EARLY + 4 * k + 5)(lambda k=k: exchange_end(k))
@@ -1027,7 +1032,7 @@
         def late(lag, allowed, body):
             m = i - lag
             away, _, n, _, _ = place(m)
-            inside = (m >= 0) & (m < jnp.where(sect == 1, steps + GUESTS, steps))
+            inside = (m >= 0) & (m < total_steps)
             pl.when(inside & allowed(away, n))(lambda: body(m))
 
         def outside(away, n):
@@ -1087,7 +1092,7 @@
         low = jnp.where(goes_on, EARLY, 0)
         high = jnp.where(
             goes_on | (starts & (sect == 1)),
-            steps + LAGS[4] + jnp.where(sect == 1, GUESTS, 0),
+            total_steps + LAGS[4],
             jnp.where(starts, EARLY, 0),
         )
         lax.fori_loop(low, high, gradient_step, 0)
@@ -1132,7 +1137,7 @@
         pl.when(away | jnp.logical_not(root))(lambda: arrived(tile_ref, share_ss.at[m]))
         return carry
 
-    lax.fori_loop(0, jnp.where(sect == 1, steps + GUESTS, steps), drain, 0)
+    lax.fori_loop(0, total_steps, drain, 0)
     for kind, (height, width) in enumerate(kinds):
         arrived(targets[kind].at[pl.ds(0, height // 2)], fin_rs.at[kind])
 
@@ -1295,6 +1300,44 @@
     )
 
 
+WIDEN_STEPS = 8
+
+
+def widen_kernel(sums, *refs):
+    count = (len(refs) - 5) // 2
+    sources, targets = refs[:count], refs[count : 2 * count]
+    gain, shift, out_bias, qkv_bias, up_bias = refs[2 * count :]
+    for source, target in zip(sources, targets):
+        target[0] = source[...].astype(F32)
+    d_model = gain.shape[2]
+    gain[0] = sums[0:2, :d_model]
+    shift[0] = sums[2:4, :d_model]
+    out_bias[...] = sums[4:5, :d_model]
+    lines = qkv_bias.shape[1] // COLS
+    for k in range(lines):
+        qkv_bias[:, k * COLS : (k + 1) * COLS] = sums[k : k + 1, d_model:]
+    for k in range(up_bias.shape[1] // COLS):
+        up_bias[:, k * COLS : (k + 1) * COLS] = sums[lines + k : lines + k + 1, d_model:]
+
+
+def widened(grads, sums, d_model, qkv_width, ff):
+    def rows_of(grad):
+        return grad.shape[0] // WIDEN_STEPS, grad.shape[1]
+
+    small = [(1, 2, d_model), (1, 2, d_model), (1, d_model), (1, qkv_width), (1, ff)]
+    return pl.pallas_call(
+        widen_kernel,
+        grid=(WIDEN_STEPS,),
+        out_shape=[jax.ShapeDtypeStruct((1,) + grad.shape, F32) for grad in grads]
+        + [jax.ShapeDtypeStruct(shape, F32) for shape in small],
+        in_specs=[pl.BlockSpec(sums.shape, lambda i: (0, 0))]
+        + [pl.BlockSpec(rows_of(grad), lambda i: (i, 0)) for grad in grads],
+        out_specs=[pl.BlockSpec((1,) + rows_of(grad), lambda i: (0, i, 0)) for grad in grads]
+        + [pl.BlockSpec(shape, lambda i, zeros=(0,) * len(shape): zeros) for shape in small],
+        name="widened",
+    )(sums, *grads)
+
+
 def relay_shards(
     block_input,
     doc_lengths,
@@ -1334,25 +1377,22 @@
     out, input_grad, *_, up_grad, down_grad, dense_grad, qkv_grad, _, sums = relay(
         dims, doc_lengths, block_input, cotangent, weights, 1
     )
-    up_grad, down_grad, dense_grad, qkv_grad = (
-        grad.astype(F32)[None] for grad in (up_grad, down_grad, dense_grad, qkv_grad)
-    )
-    biases = sums[:, d_model:].reshape(1, -1)
-    qkv_width = qkv_weight.shape[2]
-    out_bias_grad = sums[4:5, :d_model]
+    up_grad, down_grad, dense_grad, qkv_grad, gain, shift, out_bias, qkv_b, up_b = widened(
+        (up_grad, down_grad, dense_grad, qkv_grad), sums, d_model, qkv_weight.shape[2], ff
+    )
     return (
         out[None],
         input_grad[None],
-        sums[None, 0:2, :d_model],
-        sums[None, 2:4, :d_model],
+        gain,
+        shift,
         qkv_grad,
-        biases[:, :qkv_width],
+        qkv_b,
         dense_grad,
-        out_bias_grad,
+        out_bias,
         up_grad,
-        biases[:, qkv_width : qkv_width + ff],
+        up_b,
         down_grad,
-        out_bias_grad,
+        out_bias,
     )
 
 

time: 482 us -> 479 us (level)
  Pallas kernels: 450 us -> 469 us
  other arithmetic: 15.3 us -> 0 us
    broadcast_in_dim x4 -> x0, other arithmetic: 15.3 us -> none  [relay_shards(): grad.astype(F32)[None]]
    pallas_call x0 -> x1, Pallas kernels: none -> 14.5 us  [widened(): pl.pallas_call(widen_kernel, grid=(WIDEN_STEPS,), out_shape=[jax.ShapeDty...]
where the time goes in v7:
time: 479 us; the launch traced here: 473 us
  Pallas kernels  469 us (98%)
    pallas_call x1, Pallas kernels, relay(): pl.pallas_call(functools.partial(relay_kernel, dims), out_shape=outs, in_...  454 us
    pallas_call x1, Pallas kernels, widened(): pl.pallas_call(widen_kernel, grid=(WIDEN_STEPS,), out_shape=[jax.ShapeDty...  14.5 us

profile of v7, /device:TPU:0, one launch (start us, length us, event | category | flops | bytes accessed | tf_op | source)
XLA Modules:
  0.0 473.4 jit_solution(13707203743860532373)
XLA Ops:
  0.6 454.2 %relay.1 = (bf16[4,128,1024]{2,1,0:T(8,128)(2,1)}, f32[4,128,1024]{2,1,0:T(8,128)}, bf16[2,1024,1024]{2,1,0:T(8,128)(2,1)}, bf16[1024,1024]{1,0:T(8,128)(2,1)}, ...) custom-call(s32[4,8]{1,0:T(4,128)} %lengths.1, ...), custom_call_target="tpu_custom_call" | custom-call | tf_op jit(solution)/shard_map/relay/pallas_call | solution.py:1276
  454.9 0.0 copy-start.1
  454.9 0.0 copy-start
  454.9 14.5 %widened.1 = (f32[1,1024,2048]{2,1,0:T(8,128)}, f32[1,2048,1024]{2,1,0:T(8,128)}, f32[1,512,1024]{2,1,0:T(8,128)}, f32[1,1024,1536]{2,1,0:T(8,128)}, f32[1,2,102...) custom-call(f32[8,1536]{1,0:T(8,128)} %get-tuple-element.30.sums, ...), custom_call_target="tpu_custom_call" | custom-call | tf_op jit(solution)/shard_map/widened/pallas_call | solution.py:1328
  469.4 1.3 copy.28
  470.7 0.0 copy-done.1
  470.7 1.0 copy.29
  471.7 0.0 copy-done
  471.7 1.3 copy.30
Async XLA Ops:
  454.9 15.9 %copy-start.1 = (bf16[4,128,1024]{2,1,0:T(8,128)(2,1)S(1)}, bf16[4,128,1024]{2,1,0:T(8,128)(2,1)}, u32[]{:S(2)}) copy-start(bf16[4,128,1024]{2,1,0:T(8,128)(2,1)} %get-tuple-element.28) | copy-start | bytes 3145732
  454.9 16.8 %copy-start = (f32[4,128,1024]{2,1,0:T(8,128)S(1)}, f32[4,128,1024]{2,1,0:T(8,128)}, u32[]{:S(2)}) copy-start(f32[4,128,1024]{2,1,0:T(8,128)} %get-tuple-element.29) | copy-start | bytes 6291460

commit v8 on v7

--- a/solution.py
+++ b/solution.py
@@ -294,8 +294,9 @@
     @pl.when(sect == 0)
     def _():
         for s in range(micro):
+            remote(x_hbm.at[s], xfull.at[s, my_rows], yx_s.at[s], yx_r.at[s], y_dev).start()
+        for s in range(micro):
             arrived(xfull.at[s, my_rows], ownx_sem.at[s])
-            y_send_x(s).start()
 
     @pl.when(sect == 1)
     def _():
@@ -1304,15 +1305,16 @@
 
 
 def widen_kernel(sums, *refs):
-    count = (len(refs) - 5) // 2
+    count = (len(refs) - 6) // 2
     sources, targets = refs[:count], refs[count : 2 * count]
-    gain, shift, out_bias, qkv_bias, up_bias = refs[2 * count :]
+    gain, shift, dense_bias, down_bias, qkv_bias, up_bias = refs[2 * count :]
     for source, target in zip(sources, targets):
-        target[0] = source[...].astype(F32)
+        target[...] = source[...].astype(target.dtype).reshape(target.shape)
     d_model = gain.shape[2]
     gain[0] = sums[0:2, :d_model]
     shift[0] = sums[2:4, :d_model]
-    out_bias[...] = sums[4:5, :d_model]
+    dense_bias[...] = sums[4:5, :d_model]
+    down_bias[...] = sums[4:5, :d_model]
     lines = qkv_bias.shape[1] // COLS
     for k in range(lines):
         qkv_bias[:, k * COLS : (k + 1) * COLS] = sums[k : k + 1, d_model:]
@@ -1320,22 +1322,35 @@
         up_bias[:, k * COLS : (k + 1) * COLS] = sums[lines + k : lines + k + 1, d_model:]
 
 
-def widened(grads, sums, d_model, qkv_width, ff):
+def widened(rows_out, grads, sums, d_model, qkv_width, ff):
+    micro, rows, _ = rows_out[0].shape
+    parts = WIDEN_STEPS // micro
+
     def rows_of(grad):
         return grad.shape[0] // WIDEN_STEPS, grad.shape[1]
 
-    small = [(1, 2, d_model), (1, 2, d_model), (1, d_model), (1, qkv_width), (1, ff)]
+    def place(i):
+        return i // parts, lax.rem(i, parts), 0
+
+    small = [(1, 2, d_model)] * 2 + [(1, d_model)] * 2 + [(1, qkv_width), (1, ff)]
     return pl.pallas_call(
         widen_kernel,
         grid=(WIDEN_STEPS,),
-        out_shape=[jax.ShapeDtypeStruct((1,) + grad.shape, F32) for grad in grads]
+        out_shape=[jax.ShapeDtypeStruct((1,) + part.shape, part.dtype) for part in rows_out]
+        + [jax.ShapeDtypeStruct((1,) + grad.shape, F32) for grad in grads]
         + [jax.ShapeDtypeStruct(shape, F32) for shape in small],
         in_specs=[pl.BlockSpec(sums.shape, lambda i: (0, 0))]
+        + [pl.BlockSpec((1, rows // parts, d_model), place) for _ in rows_out]
         + [pl.BlockSpec(rows_of(grad), lambda i: (i, 0)) for grad in grads],
-        out_specs=[pl.BlockSpec((1,) + rows_of(grad), lambda i: (0, i, 0)) for grad in grads]
+        out_specs=[
+            pl.BlockSpec((1, 1, rows // parts, d_model), lambda i: (0,) + place(i))
+            for _ in rows_out
+        ]
+        + [pl.BlockSpec((1,) + rows_of(grad), lambda i: (0, i, 0)) for grad in grads]
         + [pl.BlockSpec(shape, lambda i, zeros=(0,) * len(shape): zeros) for shape in small],
+        compiler_params=pltpu.CompilerParams(vmem_limit_bytes=60 << 20),
         name="widened",
-    )(sums, *grads)
+    )(sums, *rows_out, *grads)
 
 
 def relay_shards(
@@ -1377,22 +1392,28 @@
     out, input_grad, *_, up_grad, down_grad, dense_grad, qkv_grad, _, sums = relay(
         dims, doc_lengths, block_input, cotangent, weights, 1
     )
-    up_grad, down_grad, dense_grad, qkv_grad, gain, shift, out_bias, qkv_b, up_b = widened(
-        (up_grad, down_grad, dense_grad, qkv_grad), sums, d_model, qkv_weight.shape[2], ff
-    )
+    out, input_grad, up_grad, down_grad, dense_grad, qkv_grad, *small = widened(
+        (out, input_grad),
+        (up_grad, down_grad, dense_grad, qkv_grad),
+        sums,
+        d_model,
+        qkv_weight.shape[2],
+        ff,
+    )
+    gain, shift, dense_b, down_b, qkv_b, up_b = small
     return (
-        out[None],
-        input_grad[None],
+        out,
+        input_grad,
         gain,
         shift,
         qkv_grad,
         qkv_b,
         dense_grad,
-        out_bias,
+        dense_b,
         up_grad,
         up_b,
         down_grad,
-        out_bias,
+        down_b,
     )
 
 

time: 479 us -> 478 us (level)
  no operation moved by 1% of the time
where the time goes in v8:
time: 478 us; the launch traced here: 472 us
  Pallas kernels  471 us (99%)
    pallas_call x1, Pallas kernels, relay(): pl.pallas_call(functools.partial(relay_kernel, dims), out_shape=outs, in_...  454 us
    pallas_call x1, Pallas kernels, widened(): pl.pallas_call(widen_kernel, grid=(WIDEN_STEPS,), out_shape=[jax.ShapeDty...  16.3 us

profile of v8, /device:TPU:0, one launch (start us, length us, event | category | flops | bytes accessed | tf_op | source)
XLA Modules:
  0.0 471.8 jit_solution(5763409631135963993)
XLA Ops:
  0.6 454.4 %relay.1 = (bf16[4,128,1024]{2,1,0:T(8,128)(2,1)}, f32[4,128,1024]{2,1,0:T(8,128)}, bf16[2,1024,1024]{2,1,0:T(8,128)(2,1)}, bf16[1024,1024]{1,0:T(8,128)(2,1)}, ...) custom-call(s32[4,8]{1,0:T(4,128)} %lengths.1, ...), custom_call_target="tpu_custom_call" | custom-call | tf_op jit(solution)/shard_map/relay/pallas_call | solution.py:1277
  455.1 16.3 %widened.1 = (bf16[1,4,128,1024]{3,2,1,0:T(8,128)(2,1)}, f32[1,4,128,1024]{3,2,1,0:T(8,128)}, f32[1,1024,2048]{2,1,0:T(8,128)}, f32[1,2048,1024]{2,1,0:T(8,128)}...) custom-call(f32[8,1536]{1,0:T(8,128)} %get-tuple-element.31.sums, ...), custom_call_target="tpu_custom_call" | custom-call | tf_op jit(solution)/shard_map/widened/pallas_call | solution.py:1336

commit v9 on v8

--- a/solution.py
+++ b/solution.py
@@ -33,7 +33,7 @@
 TOTALS = 8
 LAGS = (2, 5, 8, 12, 15)
 OWN = 16
-GUESTS = 10
+GUESTS = 12
 EARLY = 24
 
 

time: 478 us -> 476 us (level)
  no operation moved by 1% of the time
where the time goes in v9:
time: 476 us; the launch traced here: 470 us
  Pallas kernels  469 us (99%)
    pallas_call x1, Pallas kernels, relay(): pl.pallas_call(functools.partial(relay_kernel, dims), out_shape=outs, in_...  452 us
    pallas_call x1, Pallas kernels, widened(): pl.pallas_call(widen_kernel, grid=(WIDEN_STEPS,), out_shape=[jax.ShapeDty...  16.3 us

profile of v9, /device:TPU:0, one launch (start us, length us, event | category | flops | bytes accessed | tf_op | source)
XLA Modules:
  0.0 469.7 jit_solution(16320851498688893837)
XLA Ops:
  0.6 452.4 %relay.1 = (bf16[4,128,1024]{2,1,0:T(8,128)(2,1)}, f32[4,128,1024]{2,1,0:T(8,128)}, bf16[2,1024,1024]{2,1,0:T(8,128)(2,1)}, bf16[1024,1024]{1,0:T(8,128)(2,1)}, ...) custom-call(s32[4,8]{1,0:T(4,128)} %lengths.1, ...), custom_call_target="tpu_custom_call" | custom-call | tf_op jit(solution)/shard_map/relay/pallas_call | solution.py:1277
  453.1 16.3 %widened.1 = (bf16[1,4,128,1024]{3,2,1,0:T(8,128)(2,1)}, f32[1,4,128,1024]{3,2,1,0:T(8,128)}, f32[1,1024,2048]{2,1,0:T(8,128)}, f32[1,2048,1024]{2,1,0:T(8,128)}...) custom-call(f32[8,1536]{1,0:T(8,128)} %get-tuple-element.31.sums, ...), custom_call_target="tpu_custom_call" | custom-call | tf_op jit(solution)/shard_map/widened/pallas_call | solution.py:1336
